TPU v7x, 32 devices: a whole 2x2x4 slice. The times are simulated.
32 devices in a mesh: img: 8 (over z, y), row: 4 (over x, core).
Axes of the slice: x: 2, y: 2, z: 4, core: 2. Of those that a mesh axis runs over, the one named last changes fastest.
Arguments:
- activations: bfloat16 [24, 16, 192, 512], P('img', 'row'), may hold values from -4 to 4
- cotangent: bfloat16 [24, 16, 192, 512], P('img', 'row'), may hold values from -6 to 6
- weights: bfloat16 [3147776], P(('img', 'row')), may hold values from -2 to 2
Outputs:
- block_out: bfloat16 [24, 16, 192, 512], P('img', 'row')
- input_grad: float32 [24, 16, 192, 512], P('img', 'row')
- weight_grad: float32 [3147776], P(('img', 'row'))
- summary_mean: float32 [512], replicated
- summary_var: float32 [512], replicated
All inputs are finite; a program needn't handle non-finite values.
Results may differ from a plain program's by a relative error of at most 0.0102.
Values may be sent and summed in bfloat16 or wider, within the bound.
No kernel may reach another device: no remote copies, remote signals or barrier semaphores. Data moves between devices by JAX's collectives and lax.ppermute only.
A program may use at most 256 MiB of HBM per device.

v0:
```python
import functools
import math

import jax
import jax.numpy as jnp
from jax import lax
from jax.experimental import pallas as pl
from jax.experimental.pallas import tpu as pltpu
from jax.sharding import PartitionSpec as P

FF = 2048
HEADS = 8
LANES = 128


EPS = 1e-05
NEGATIVE = -1e30
HALF = jnp.bfloat16
SINGLE = jnp.float32
VMEM_BYTES = 56 * 1024 * 1024

TAIL = 16


def swap(value, axis, distance):
    size = lax.axis_size(axis)
    return lax.ppermute(value, axis, [(i, i ^ distance) for i in range(size)])


def hops():
    rows, images = lax.axis_size("row"), lax.axis_size("img")
    inner = ("row", 1, 1)
    across = ("row", 2, 2)
    along = ("img", 1, rows)
    outer = []
    distance = images // 2
    while distance > 1:
        outer.append(("img", distance, distance * rows))
        distance //= 2
    distance = rows // 2
    while distance > 2:
        outer.append(("row", distance, distance))
        distance //= 2
    return inner, across, along, outer


def piece_order():
    inner, across, along, outer = hops()
    masks = [0]
    for _, _, mask in outer:
        masks = masks + [m ^ mask for m in masks]
    near = (
        masks
        + [m ^ across[2] for m in masks]
        + [m ^ along[2] for m in masks]
        + [m ^ across[2] ^ along[2] for m in masks]
    )
    return near + [m ^ inner[2] for m in near]


def device_index():
    return lax.axis_index("img") * lax.axis_size("row") + lax.axis_index("row")


def gather_pieces(own):
    inner, across, along, outer = hops()
    held = own[None]
    for axis, distance, _ in outer:
        held = jnp.concatenate([held, swap(held, axis, distance)])
    half = held.shape[0] // 2
    held_x = swap(held, across[0], across[1])
    held_y = swap(held, along[0], along[1])
    corner_first = swap(held_x[:half], along[0], along[1])
    corner_second = swap(held_y[half:], across[0], across[1])
    near = [held, held_x, held_y, corner_first, corner_second]
    far = [swap(part, inner[0], inner[1]) for part in near]
    return jnp.concatenate(near + far)


def scatter_pieces(pieces):
    inner, across, along, outer = hops()

    def add(kept, sent, axis, distance):
        return kept + swap(sent.astype(HALF), axis, distance).astype(SINGLE)

    count = pieces.shape[0] // 2
    near = add(pieces[:count], pieces[count:], inner[0], inner[1])
    quarter = count // 4
    half = quarter // 2
    held, held_x, held_y, corner = (near[i * quarter : (i + 1) * quarter] for i in range(4))
    first = add(
        jnp.concatenate([held[:half], held_x[:half]]),
        jnp.concatenate([held_y[:half], corner[:half]]),
        along[0],
        along[1],
    )
    second = add(
        jnp.concatenate([held[half:], held_y[half:]]),
        jnp.concatenate([held_x[half:], corner[half:]]),
        across[0],
        across[1],
    )
    first = add(first[:half], first[half:], across[0], across[1])
    second = add(second[:half], second[half:], along[0], along[1])
    held = jnp.concatenate([first, second])
    for axis, distance, _ in reversed(outer):
        half = held.shape[0] // 2
        held = add(held[:half], held[half:], axis, distance)
    return held[0]


def row_hops():
    inner, across, _, outer = hops()
    return [inner, across] + [hop for hop in outer if hop[0] == "row"]


def image_hops():
    _, _, along, outer = hops()
    return [along] + [hop for hop in outer if hop[0] == "img"]


def gather_rows(own, shown):
    width = own.shape[-1]
    count = shown.shape[0]
    held, masks = own[None], [0]
    for axis, distance, mask in row_hops():
        got = swap(jnp.concatenate([held.reshape(-1, width), shown]), axis, distance)
        held = jnp.concatenate([held, got[:-count].reshape(held.shape)])
        shown = shown + got[-count:]
        masks = masks + [m ^ mask for m in masks]
    place = [0] * len(masks)
    for at, mask in enumerate(masks):
        place[mask] = at
    order = jnp.asarray(place, jnp.int32)[jnp.arange(len(masks)) ^ lax.axis_index("row")]
    held = jnp.moveaxis(jnp.take(held, order, axis=0, mode="clip"), 0, 1)
    return held.reshape(own.shape[0], -1, width), shown


def gather_weights(weights, model_width):
    length = weights.shape[0]
    me = device_index()
    devices = lax.axis_size("img") * lax.axis_size("row")
    block = length // model_width
    rest = length % model_width
    start = TAIL * model_width + rest * me - 4 * model_width
    own = lax.dynamic_update_slice(jnp.zeros(((block + TAIL) * model_width,), HALF), weights, (start,))
    own = own.reshape(block + TAIL, model_width)
    pieces = gather_pieces(own)
    place = [0] * devices
    for at, mask in enumerate(piece_order()):
        place[mask] = at
    order = jnp.asarray(place, jnp.int32)[jnp.arange(devices) ^ me]
    pieces = jnp.take(pieces, order, axis=0, mode="clip")
    tails = jnp.concatenate([pieces[1:, :TAIL], jnp.zeros((1, TAIL, model_width), HALF)])
    body = jnp.concatenate([pieces[:, TAIL:block], pieces[:, block:] + tails], axis=1)
    return pieces[0, TAIL - 4 : TAIL], body.reshape(devices * block, model_width)


def scatter_grads(vectors, rows, length):
    model_width = rows.shape[1]
    me = device_index()
    devices = lax.axis_size("img") * lax.axis_size("row")
    block = length // model_width
    rest = length % model_width
    whole = jnp.concatenate([jnp.zeros((TAIL - 4, model_width), SINGLE), vectors, rows])
    place = jnp.asarray(piece_order(), jnp.int32)
    pieces = jnp.stack([whole[block * s : block * s + block + TAIL] for s in range(devices)])
    pieces = jnp.take(pieces, place ^ me, axis=0, mode="clip")
    mine = scatter_pieces(pieces)
    start = TAIL * model_width + rest * me - 4 * model_width
    return lax.dynamic_slice(mine.reshape(-1), (start,), (length,))


def dot(left, right):
    return jnp.dot(left, right, preferred_element_type=SINGLE)


def dot_rows(left, right):
    return lax.dot_general(left, right, (((1,), (1,)), ((), ())), preferred_element_type=SINGLE)


def dot_outer(left, right):
    return lax.dot_general(left, right, (((0,), (0,)), ((), ())), preferred_element_type=SINGLE)


def normalize(values):
    centred = values - jnp.mean(values, axis=-1, keepdims=True)
    inverse = lax.rsqrt(jnp.mean(centred * centred, axis=-1, keepdims=True) + EPS)
    return (centred * inverse, inverse)


def norm_back(grad_norm, normed, inverse):
    return inverse * (
        grad_norm
        - jnp.mean(grad_norm, axis=-1, keepdims=True)
        - normed * jnp.mean(grad_norm * normed, axis=-1, keepdims=True)
    )


def whole_block(shape):
    return pl.BlockSpec(shape, lambda *_: (0,) * len(shape), pipeline_mode=pl.Buffered(1))


def head_keys(rows_per_step, model_width):
    return [
        (row, pair, half)
        for row in range(rows_per_step)
        for pair in range(model_width // LANES)
        for half in range(2)
    ]


def attention_forward_kernel(
    scaling,
    rows_per_step,
    local_rows,
    first_row_ref,
    block_ref,
    gain_ref,
    w_ref,
    key_far_ref,
    value_far_ref,
    causal_ref,
    query_ref,
    key_ref,
    value_ref,
    mixed_ref,
    probs_ref,
):
    columns = causal_ref.shape[0]
    far = key_far_ref.shape[0]
    width = block_ref.shape[1]
    head_width = width // HEADS
    step = pl.program_id(0)
    normed, _ = normalize(block_ref[...].astype(SINGLE))
    attn_in = (normed * gain_ref[...]).astype(HALF)
    for i, ref in enumerate((query_ref, key_ref, value_ref)):
        ref[...] = dot(attn_in, w_ref[:, i * width : (i + 1) * width]).astype(HALF)
    first_half = lax.broadcasted_iota(jnp.int32, (columns + far, LANES), 1) < head_width
    far_index = lax.broadcasted_iota(jnp.int32, (far, columns), 0)
    keys = head_keys(rows_per_step, width)
    for start in range(0, len(keys), HEADS):
        group = keys[start : start + HEADS]
        scores, low, mixed = {}, {}, {}
        for row, pair, half in group:
            global_row = first_row_ref[0] + lax.rem(step * rows_per_step + row, local_rows)
            far_bias = jnp.where(far_index < global_row, 0.0, NEGATIVE)
            tokens = slice(row * columns, (row + 1) * columns)
            lanes = slice(pair * LANES, (pair + 1) * LANES)
            all_keys = jnp.concatenate([key_ref[tokens, lanes], key_far_ref[:, lanes]], axis=0)
            one_head = jnp.where(
                first_half if half == 0 else ~first_half, all_keys, jnp.zeros_like(all_keys)
            )
            found = dot_rows(one_head, query_ref[tokens, lanes])
            scores[row, pair, half] = jnp.concatenate(
                [found[:columns] + causal_ref[...], found[columns:] + far_bias], axis=0
            )
        for row, pair, half in group:
            found = scores.pop((row, pair, half))
            top = jnp.max(found, axis=0, keepdims=True)
            powers = jnp.exp((found - top) * scaling)
            inverse = 1.0 / jnp.sum(powers, axis=0, keepdims=True)
            low[row, pair, half] = (powers * inverse).astype(HALF)
            probs_ref[row, 2 * pair + half] = low[row, pair, half]
        for row, pair, half in group:
            tokens = slice(row * columns, (row + 1) * columns)
            lanes = slice(pair * LANES, (pair + 1) * LANES)
            all_values = jnp.concatenate([value_ref[tokens, lanes], value_far_ref[:, lanes]], axis=0)
            turned = all_values.T[half * head_width : (half + 1) * head_width]
            mixed[row, pair, half] = dot(turned, low[row, pair, half])
        for row, pair, half in group:
            if half == 0:
                tokens = slice(row * columns, (row + 1) * columns)
                lanes = slice(pair * LANES, (pair + 1) * LANES)
                both = jnp.concatenate([mixed[row, pair, 0], mixed[row, pair, 1]], axis=0)
                mixed_ref[tokens, lanes] = both.T.astype(HALF)


def image_groups(images):
    return [(0, 1), (1, images - 1)] if images > 1 else [(0, images)]


def step_groups(steps):
    if steps < 4:
        return [(0, steps)]
    first, last = steps // 3, max(1, steps // 6)
    return [(0, first), (first, steps - first - last), (steps - last, last)]


def kept_arrays(previous, start):
    if previous is None:
        return ([], [], {})
    specs = [pl.BlockSpec(memory_space=pl.ANY)] * len(previous)
    return (list(previous), specs, {start + i: i for i in range(len(previous))})


def attention_forward(
    group, previous, block_in, gain, w_qkv, key_far, value_far, first_row, local_rows, columns
):
    tokens, width = block_in.shape
    images, far, _ = key_far.shape
    first_image, count = group
    rows_per_step = math.gcd(local_rows, 2)
    steps = local_rows // rows_per_step
    first_step = first_image * steps
    size = rows_per_step * columns
    position = jnp.arange(columns)
    causal = jnp.where(position[:, None] <= position[None, :], 0.0, NEGATIVE).astype(SINGLE)
    block = pl.BlockSpec((size, width), lambda i, _: (first_step + i, 0))
    far_block = pl.BlockSpec((None, far, width), lambda i, _: (first_image + i // steps, 0, 0))
    probs_block = pl.BlockSpec(
        (rows_per_step, HEADS, columns + far, columns), lambda i, _: (first_step + i, 0, 0, 0)
    )
    inputs = [block_in, gain, w_qkv, key_far, value_far, causal]
    kept, kept_specs, aliases = kept_arrays(previous, 1 + len(inputs))
    low = jax.ShapeDtypeStruct((tokens, width), HALF)
    part = count * tokens // images
    kernel = functools.partial(
        attention_forward_kernel, 1.0 / math.sqrt(width // HEADS), rows_per_step, local_rows
    )

    def body(*refs):
        kernel(*refs[: 1 + len(inputs)], *refs[1 + len(inputs) + len(kept) :])

    return pl.pallas_call(
        body,
        grid_spec=pltpu.PrefetchScalarGridSpec(
            num_scalar_prefetch=1,
            grid=(count * steps,),
            in_specs=[
                block,
                whole_block((1, width)),
                whole_block((width, 3 * width)),
                far_block,
                far_block,
                whole_block((columns, columns)),
            ]
            + kept_specs,
            out_specs=[block] * 4 + [probs_block],
        ),
        out_shape=[low] * 4
        + [jax.ShapeDtypeStruct((images * local_rows, HEADS, columns + far, columns), HALF)],
        input_output_aliases=aliases,
        compiler_params=pltpu.CompilerParams(vmem_limit_bytes=VMEM_BYTES),
        cost_estimate=pl.CostEstimate(
            flops=part * width * (6 * width + 8 * (columns + far)),
            bytes_accessed=part * width * 12 + part * HEADS * (columns + far) * 2,
            transcendentals=part * HEADS * (columns + far),
        ),
        name="attention_forward",
    )(first_row, *inputs, *kept)


GELU_OUTER = math.sqrt(2.0 / math.pi)
GELU_CUBE = 0.044715


def gelu_and_slope(value):
    square = value * value
    gate = 0.5 * jnp.tanh(value * (GELU_OUTER * GELU_CUBE * square + GELU_OUTER)) + 0.5
    activated = value * gate
    slope = gate + activated * (1.0 - gate) * (6.0 * GELU_OUTER * GELU_CUBE * square + 2.0 * GELU_OUTER)
    return (activated, slope)


def start_pieces(plan, flat_ref, outs, sems, index):
    copies = []
    for i, (out, place, offset, rows) in enumerate(plan):
        source = flat_ref.at[pl.ds(pl.multiple_of(offset(index), TAIL), rows)]
        target = outs[out].at[place] if place else outs[out]
        copies.append(pltpu.make_async_copy(source, target, sems.at[i]))
    for copy in copies:
        copy.start()
    return copies


def feed_forward_kernel(
    chunk,
    plan,
    masks,
    block,
    index_ref,
    block_ref,
    mixed_ref,
    cotangent_ref,
    gain_ref,
    *rest,
):
    given, rest = rest[: len(masks)], rest[len(masks) :]
    out_ref, middle_grad_ref, mixed_grad_ref, grad_gain_ref, *rest = rest
    *pieces, grad_out_ref, grad_inner_ref, grad_outer_ref, w_inner_ref, flat_ref, sems = rest
    width, hidden = w_inner_ref.shape
    groups = hidden // width
    per = 256 // groups
    inner_start = TAIL + width
    outer_start = inner_start + hidden
    w_out_ref = flat_ref.at[TAIL:inner_start]
    w_outer_ref = flat_ref.at[outer_start:]

    @pl.when(pl.program_id(0) == 0)
    def _():
        for ref in (grad_out_ref, grad_inner_ref, grad_outer_ref, grad_gain_ref):
            ref[...] = jnp.zeros_like(ref)
        if block is None:
            flat_ref[...] = given[0][...]
        else:
            placed = [(ref, mask, first) for ref, (mask, first) in zip(given, masks)]
            assemble(flat_ref, placed, lax.rem(index_ref[0], 8), block, 3)
        mix = weave(groups, per)
        for c in range(width // per):
            start = inner_start + c * groups * per
            parted = dot_outer(mix, flat_ref[start : start + groups * per]).astype(HALF)
            for g in range(groups):
                w_inner_ref[c * per : (c + 1) * per, g * width : (g + 1) * width] = parted[
                    g * per : (g + 1) * per
                ]

    mixed = mixed_ref[...]
    cotangent = cotangent_ref[...]
    middle = block_ref[...].astype(SINGLE) + dot(mixed, w_out_ref[...])
    normed, inverse = normalize(middle)
    ff_in = (normed * gain_ref[...]).astype(HALF)
    out = middle
    ff_grad = jnp.zeros_like(middle)
    cotangent_turned = cotangent.T
    ff_turned = ff_in.T
    count = hidden // chunk
    spans = [slice(j * chunk, (j + 1) * chunk) for j in range(count)]

    def products(j):
        return (dot(ff_in, w_inner_ref[:, spans[j]]), dot_rows(cotangent, w_outer_ref[spans[j], :]))

    ready = products(0)
    for j in range(count):
        inner, act_grad = ready
        if j + 1 < count:
            ready = products(j + 1)
        activated, slope = gelu_and_slope(inner)
        activated = activated.astype(HALF)
        inner_grad = (slope * act_grad).astype(HALF)
        out = out + dot(activated, w_outer_ref[spans[j], :])
        ff_grad = ff_grad + dot_rows(inner_grad, w_inner_ref[:, spans[j]])
        grad_inner_ref[:, spans[j]] += dot(ff_turned, inner_grad)
        grad_outer_ref[:, spans[j]] += dot(cotangent_turned, activated)
    out_ref[...] = out.astype(HALF)
    grad_gain_ref[...] += jnp.sum(ff_grad * normed, axis=0, keepdims=True)
    middle_grad = cotangent.astype(SINGLE) + norm_back(ff_grad * gain_ref[...], normed, inverse)
    middle_grad_ref[...] = middle_grad
    branch_grad = middle_grad.astype(HALF)
    mixed_grad_ref[...] = dot_rows(branch_grad, w_out_ref[...]).astype(HALF)
    grad_out_ref[...] += dot_outer(mixed, branch_grad)

    @pl.when(pl.program_id(0) == pl.num_programs(0) - 1)
    def _():
        flat_ref[:TAIL] = jnp.zeros((TAIL, width), HALF)
        flat_ref[TAIL : TAIL + width] = grad_out_ref[...].astype(HALF)
        mix = weave(groups, per)
        for c in range(width // per):
            parts = [
                grad_inner_ref[c * per : (c + 1) * per, g * width : (g + 1) * width].astype(HALF)
                for g in range(groups)
            ]
            start = TAIL + width + c * groups * per
            woven = dot(mix, jnp.concatenate(parts, axis=0))
            flat_ref[start : start + groups * per] = woven.astype(HALF)
        start = TAIL + width + hidden
        for j in range(hidden // width):
            turned = grad_outer_ref[:, j * width : (j + 1) * width].astype(HALF).T
            flat_ref[start + j * width : start + (j + 1) * width] = turned
        for copy in start_pieces(plan, flat_ref, pieces, sems, index_ref[0]):
            copy.wait()


def weave(groups, per):
    size = groups * per
    row = lax.broadcasted_iota(jnp.int32, (size, size), 0)
    column = lax.broadcasted_iota(jnp.int32, (size, size), 1)
    wanted = lax.rem(row, groups) * per + lax.div(row, groups)
    return (wanted == column).astype(SINGLE).astype(HALF)


def piece_outputs(shapes):
    return (
        [pl.BlockSpec(memory_space=pl.ANY)] * len(shapes),
        [jax.ShapeDtypeStruct(shape, HALF) for shape in shapes],
    )


def feed_forward(index, block_in, mixed, cotangent, gain, given, block, hidden, size, plan, shapes):
    tokens, width = block_in.shape
    tile = pl.BlockSpec((size, width), lambda i, _: (i, 0))
    piece_specs, piece_shapes = piece_outputs(shapes)
    masks = [entry[1:] for entry in given]
    return pl.pallas_call(
        functools.partial(feed_forward_kernel, 512, plan, masks, block),
        grid_spec=pltpu.PrefetchScalarGridSpec(
            num_scalar_prefetch=1,
            grid=(tokens // size,),
            in_specs=[tile, tile, tile, whole_block((1, width))] + vmem_specs(len(given)),
            out_specs=[tile, tile, tile, whole_block((1, width))] + piece_specs,
            scratch_shapes=[
                pltpu.VMEM((width, width), SINGLE),
                pltpu.VMEM((width, hidden), SINGLE),
                pltpu.VMEM((width, hidden), SINGLE),
                pltpu.VMEM((width, hidden), HALF),
                pltpu.VMEM((TAIL + width + 2 * hidden, width), HALF),
                pltpu.SemaphoreType.DMA((len(plan),)),
            ],
        ),
        out_shape=[
            jax.ShapeDtypeStruct((tokens, width), HALF),
            jax.ShapeDtypeStruct((tokens, width), SINGLE),
            jax.ShapeDtypeStruct((tokens, width), HALF),
            jax.ShapeDtypeStruct((1, width), SINGLE),
        ]
        + piece_shapes,
        compiler_params=pltpu.CompilerParams(vmem_limit_bytes=VMEM_BYTES),
        cost_estimate=pl.CostEstimate(
            flops=tokens * width * (6 * width + 12 * hidden),
            bytes_accessed=tokens * width * 14 + width * hidden * 8,
            transcendentals=tokens * hidden,
        ),
        name="feed_forward",
    )(index, block_in, mixed, cotangent, gain, *[entry[0] for entry in given])


def attention_backward_kernel(
    scaling,
    rows_per_step,
    per_image,
    first_step,
    plan,
    ends,
    index_ref,
    block_ref,
    query_ref,
    key_ref,
    value_ref,
    key_far_ref,
    value_far_ref,
    probs_ref,
    mixed_grad_ref,
    *rest,
):
    rest = list(rest)
    earlier = None
    if first_step > 0:
        earlier, rest = rest[:3], rest[6:]
    if ends:
        fixed, rest = rest[:6], rest[6:]
    query_grad_ref, key_grad_ref, value_grad_ref, *rest = rest
    if ends:
        shared_ref, *rest = rest
        small_ref = shared_ref.at[shared_ref.shape[0] - 8 - TAIL :]
        *pieces, total_ref, key_far_grad_ref, value_far_grad_ref, flat_ref, sems = rest
    else:
        total_ref, key_far_grad_ref, value_far_grad_ref = rest
    width = query_ref.shape[1]
    head_width = width // HEADS
    far = key_far_ref.shape[0]
    columns = query_ref.shape[0] // rows_per_step
    image = lax.div(first_step + pl.program_id(0), per_image)

    @pl.when(pl.program_id(0) == 0)
    def _():
        for i, ref in enumerate((total_ref, key_far_grad_ref, value_far_grad_ref)):
            ref[...] = jnp.zeros_like(ref) if earlier is None else earlier[i][...]

    first_half = lax.broadcasted_iota(jnp.int32, (columns + far, LANES), 1) < head_width
    keys = head_keys(rows_per_step, width)
    for start in range(0, len(keys), HEADS):
        group = keys[start : start + HEADS]
        prob_grad, score_grad, value_grad, key_grad, query_grad = {}, {}, {}, {}, {}
        for row, pair, half in group:
            tokens = slice(row * columns, (row + 1) * columns)
            lanes = slice(pair * LANES, (pair + 1) * LANES)
            all_values = jnp.concatenate([value_ref[tokens, lanes], value_far_ref[:, lanes]], axis=0)
            one_head = jnp.where(
                first_half if half == 0 else ~first_half, all_values, jnp.zeros_like(all_values)
            )
            prob_grad[row, pair, half] = dot_rows(one_head, mixed_grad_ref[tokens, lanes])
        for row, pair, half in group:
            tokens = slice(row * columns, (row + 1) * columns)
            lanes = slice(pair * LANES, (pair + 1) * LANES)
            value_grad[row, pair, half] = dot(
                probs_ref[row, 2 * pair + half], mixed_grad_ref[tokens, lanes]
            )
        for row, pair, half in group:
            probs = probs_ref[row, 2 * pair + half].astype(SINGLE)
            grad = prob_grad.pop((row, pair, half))
            total = jnp.sum(probs * grad, axis=0, keepdims=True)
            score_grad[row, pair, half] = (probs * (grad - total)).astype(HALF)
        for row, pair, half in group:
            tokens = slice(row * columns, (row + 1) * columns)
            lanes = slice(pair * LANES, (pair + 1) * LANES)
            key_grad[row, pair, half] = dot(score_grad[row, pair, half], query_ref[tokens, lanes])
            all_keys = jnp.concatenate([key_ref[tokens, lanes], key_far_ref[:, lanes]], axis=0)
            turned = all_keys.T[half * head_width : (half + 1) * head_width]
            query_grad[row, pair, half] = dot(turned, score_grad[row, pair, half])
        for row, pair, half in group:
            if half == 0:
                tokens = slice(row * columns, (row + 1) * columns)
                lanes = slice(pair * LANES, (pair + 1) * LANES)
                first, second = (row, pair, 0), (row, pair, 1)
                value_both = jnp.where(first_half, value_grad[first], value_grad[second])
                key_both = jnp.where(first_half, key_grad[first], key_grad[second]) * scaling
                value_grad_ref[tokens, lanes] = value_both[:columns].astype(HALF)
                key_grad_ref[tokens, lanes] = key_both[:columns].astype(HALF)
                value_far_grad_ref[image, :, lanes] += value_both[columns:]
                key_far_grad_ref[image, :, lanes] += key_both[columns:]
                query_both = jnp.concatenate([query_grad[first], query_grad[second]], axis=0) * scaling
                query_grad_ref[tokens, lanes] = query_both.T.astype(HALF)
    normed, _ = normalize(block_ref[...].astype(SINGLE))
    turned = normed.astype(HALF).T
    for i, ref in enumerate((query_grad_ref, key_grad_ref, value_grad_ref)):
        total_ref[:, i * width : (i + 1) * width] += dot(turned, ref[...])
    if not ends:
        return

    @pl.when(pl.program_id(0) == pl.num_programs(0) - 1)
    def _():
        gain_ref, gain_two_grad_ref, w_ref, summary_ref, standard_ref, gain_sum_ref = fixed

        key_low = key_far_grad_ref[...].reshape(-1, width).astype(HALF)
        value_low = value_far_grad_ref[...].reshape(-1, width).astype(HALF)
        gain = jnp.broadcast_to(gain_ref[...], (8, width)).T[:, :1]
        matched = jnp.zeros((width, width), SINGLE)
        flat_ref[:TAIL] = jnp.zeros((TAIL, width), HALF)
        for i in range(3):
            total = total_ref[:, i * width : (i + 1) * width]
            matched = matched + total * w_ref[:, i * width : (i + 1) * width].astype(SINGLE)
            grad = total * gain
            if i > 0:
                grad = grad + dot_outer(summary_ref[...], key_low if i == 1 else value_low)
            flat_ref[TAIL + i * width : TAIL + (i + 1) * width] = grad.astype(HALF)
            if i == 2:
                small_ref[8:] = grad[width - TAIL :]
        copies = start_pieces(plan, flat_ref, pieces, sems, index_ref[0])
        summary_grad = dot_rows(key_low, w_ref[:, width : 2 * width]) + dot_rows(
            value_low, w_ref[:, 2 * width :]
        )
        standard = standard_ref[...]
        standard_grad = summary_grad * gain_sum_ref[...]
        shared_ref[: standard.shape[0]] = standard_grad

        def fold(value):
            return jnp.sum(value, axis=0, keepdims=True)

        small_ref[0:1] = fold(standard_grad)
        small_ref[1:2] = fold(standard_grad * standard)
        small_ref[2:3] = fold(matched.T)
        small_ref[3:4] = fold(summary_grad * standard)
        small_ref[4:5] = fold(summary_grad)
        small_ref[5:6] = gain_two_grad_ref[...]
        small_ref[6:8] = jnp.zeros((2, width), SINGLE)
        for copy in copies:
            copy.wait()


def attention_backward(
    group,
    previous,
    index,
    block_in,
    query,
    key,
    value,
    key_far,
    value_far,
    probs,
    mixed_grad,
    last,
    local_rows,
    columns,
    plan,
    shapes,
):
    tokens, width = query.shape
    images, far, _ = key_far.shape
    first_step, count = group
    rows_per_step = math.gcd(local_rows, 4)
    per_image = local_rows // rows_per_step
    ends = first_step + count == images * per_image
    size = rows_per_step * columns
    part = count * size
    block = pl.BlockSpec((size, width), lambda i, _: (first_step + i, 0))
    far_block = pl.BlockSpec((None, far, width), lambda i, _: ((first_step + i) // per_image, 0, 0))
    probs_block = pl.BlockSpec(
        (rows_per_step, HEADS, columns + far, columns), lambda i, _: (first_step + i, 0, 0, 0)
    )
    inputs = [block_in, query, key, value, key_far, value_far, probs, mixed_grad]
    in_specs = [block] * 4 + [far_block] * 2 + [probs_block, block]
    aliases = {}
    total_shape = (width, 3 * width)
    far_shape = (images, far, width)
    if previous is not None:
        sums = list(previous[3:])
        inputs = inputs + sums
        in_specs = in_specs + [whole_block(array.shape) for array in sums]
        kept, kept_specs, aliases = kept_arrays(previous[:3], 1 + len(inputs))
        inputs, in_specs = inputs + kept, in_specs + kept_specs
    out_specs = [block] * 3
    out_shape = [jax.ShapeDtypeStruct((tokens, width), HALF)] * 3
    scratch = []
    if ends:
        inputs = inputs + list(last)
        in_specs = in_specs + [whole_block(array.shape) for array in last]
        piece_specs, piece_shapes = piece_outputs(shapes)
        summaries = images * far
        shared_shape = (summaries + 8 + TAIL, width)
        out_specs += [whole_block(shared_shape)] + piece_specs
        out_shape += [jax.ShapeDtypeStruct(shared_shape, SINGLE)] + piece_shapes
        scratch = [
            pltpu.VMEM(total_shape, SINGLE),
            pltpu.VMEM(far_shape, SINGLE),
            pltpu.VMEM(far_shape, SINGLE),
            pltpu.VMEM((TAIL + 3 * width, width), HALF),
            pltpu.SemaphoreType.DMA((len(plan),)),
        ]
    else:
        out_specs += [whole_block(total_shape), whole_block(far_shape), whole_block(far_shape)]
        out_shape += [
            jax.ShapeDtypeStruct(total_shape, SINGLE),
            jax.ShapeDtypeStruct(far_shape, SINGLE),
            jax.ShapeDtypeStruct(far_shape, SINGLE),
        ]
    return pl.pallas_call(
        functools.partial(
            attention_backward_kernel,
            1.0 / math.sqrt(width // HEADS),
            rows_per_step,
            per_image,
            first_step,
            plan,
            ends,
        ),
        grid_spec=pltpu.PrefetchScalarGridSpec(
            num_scalar_prefetch=1,
            grid=(count,),
            in_specs=in_specs,
            out_specs=out_specs,
            scratch_shapes=scratch,
        ),
        out_shape=out_shape,
        input_output_aliases=aliases,
        compiler_params=pltpu.CompilerParams(vmem_limit_bytes=VMEM_BYTES),
        cost_estimate=pl.CostEstimate(
            flops=part * width * (6 * width + 16 * (columns + far)),
            bytes_accessed=part * width * 16 + part * HEADS * (columns + far) * 2,
            transcendentals=0,
        ),
        name="attention_backward",
    )(index, *inputs)


def input_grad_kernel(
    rows_per_step,
    block_ref,
    gain_ref,
    query_grad_ref,
    key_grad_ref,
    value_grad_ref,
    w_ref,
    middle_grad_ref,
    mean_grad_ref,
    out_ref,
):
    width = block_ref.shape[1]
    columns = block_ref.shape[0] // rows_per_step

    attn_grad = (
        dot_rows(query_grad_ref[...], w_ref[:, :width])
        + dot_rows(key_grad_ref[...], w_ref[:, width : 2 * width])
        + dot_rows(value_grad_ref[...], w_ref[:, 2 * width :])
    )
    normed, inverse = normalize(block_ref[...].astype(SINGLE))
    total = middle_grad_ref[...] + norm_back(attn_grad * gain_ref[...], normed, inverse)
    for row in range(rows_per_step):
        tokens = slice(row * columns, (row + 1) * columns)
        out_ref[tokens] = total[tokens] + mean_grad_ref[row : row + 1]


def input_grads(
    group,
    previous,
    block_in,
    gain,
    query_grad,
    key_grad,
    value_grad,
    w_qkv,
    middle_grad,
    mean_grad,
    local_rows,
    columns,
):
    tokens, width = block_in.shape
    images = mean_grad.shape[0]
    first_image, count = group
    rows_per_step = math.gcd(local_rows, 2)
    per_image = local_rows // rows_per_step
    first_step = first_image * per_image
    size = rows_per_step * columns
    part = count * tokens // images
    block = pl.BlockSpec((size, width), lambda i: (first_step + i, 0))
    inputs = [block_in, gain, query_grad, key_grad, value_grad, w_qkv, middle_grad]
    inputs = inputs + [mean_grad.reshape(tokens // size, rows_per_step, width)]
    kept, kept_specs, aliases = kept_arrays(None if previous is None else [previous], len(inputs))
    kernel = functools.partial(input_grad_kernel, rows_per_step)

    def body(*refs):
        kernel(*refs[: len(inputs)], *refs[len(inputs) + len(kept) :])

    return pl.pallas_call(
        body,
        grid=(count * per_image,),
        in_specs=[block, whole_block((1, width))]
        + [block] * 3
        + [whole_block((width, 3 * width)), block]
        + [pl.BlockSpec((None, rows_per_step, width), lambda i: (first_step + i, 0, 0))]
        + kept_specs,
        out_specs=block,
        out_shape=jax.ShapeDtypeStruct((tokens, width), SINGLE),
        input_output_aliases=aliases,
        compiler_params=pltpu.CompilerParams(vmem_limit_bytes=VMEM_BYTES),
        cost_estimate=pl.CostEstimate(
            flops=part * width * 6 * width, bytes_accessed=part * width * 16, transcendentals=0
        ),
        name="input_grads",
    )(*inputs, *kept)


def assemble(flat_ref, pieces, index, block, count):
    plane = 8 * block
    width = flat_ref.shape[1]
    for at in range(0, count * plane + 1, block):
        flat_ref[at : at + TAIL] = jnp.zeros((TAIL, width), HALF)
    for ref, mask, first in pieces:
        spot = pl.multiple_of((index ^ mask) * block, TAIL)
        for slot in range(count):
            part = ref.at[slot] if len(ref.shape) == 3 else ref
            last = first + part.shape[0]
            for low, high in ((0, TAIL), (TAIL, block), (block, block + TAIL)):
                low, high = max(low, first), min(high, last)
                if low >= high:
                    continue
                rows = pl.ds(spot + (slot * plane + low), high - low)
                value = part[low - first : high - first]
                if low < TAIL or low >= block:
                    value = flat_ref[rows] + value
                flat_ref[rows] = value


def projection_weights_kernel(masks, block, index_ref, tail_ref, summary_ref, *refs):
    *piece_refs, w_ref, key_far_ref, value_far_ref, flat_ref = refs
    width = flat_ref.shape[1]
    pieces = [(ref, mask, first) for ref, (mask, first) in zip(piece_refs, masks)]
    assemble(flat_ref, pieces, lax.rem(index_ref[0], 8), block, 1)
    flat_ref[3 * width :] += tail_ref[...]
    for i in range(3):
        w_ref[:, i * width : (i + 1) * width] = flat_ref[TAIL + i * width : TAIL + (i + 1) * width]
    key_far_ref[...] = dot(summary_ref[...], w_ref[:, width : 2 * width]).astype(HALF)
    value_far_ref[...] = dot(summary_ref[...], w_ref[:, 2 * width :]).astype(HALF)


def vmem_specs(count):
    return [pl.BlockSpec(memory_space=pltpu.VMEM)] * count


def projection_weights(index, tail, summary_low, pieces, block):
    width = tail.shape[1]
    arrays, masks = [p[0] for p in pieces], [p[1:] for p in pieces]
    far = summary_low.shape[0]
    return pl.pallas_call(
        functools.partial(projection_weights_kernel, masks, block),
        in_specs=[pl.BlockSpec(memory_space=pltpu.SMEM)] + vmem_specs(2 + len(arrays)),
        out_specs=vmem_specs(3),
        out_shape=[
            jax.ShapeDtypeStruct((width, 3 * width), HALF),
            jax.ShapeDtypeStruct((far, width), HALF),
            jax.ShapeDtypeStruct((far, width), HALF),
        ],
        scratch_shapes=[pltpu.VMEM((TAIL + 3 * width, width), HALF)],
        compiler_params=pltpu.CompilerParams(vmem_limit_bytes=VMEM_BYTES),
        name="projection_weights",
    )(index, tail, summary_low, *arrays)


def swap_core(value):
    return swap(value, "row", 1)


def swap_x(value):
    return swap(value, "row", 2)


def swap_y(value):
    return swap(value, "img", 1)


def swap_both(value):
    size = lax.axis_size("img") * lax.axis_size("row")
    return lax.ppermute(value, ("img", "row"), [(i, i ^ 6) for i in range(size)])


def swap_near(value):
    return swap(value, "img", 2)


def swap_far(value):
    return swap(value, "img", 4)


def send_far(value):
    return lax.ppermute(value, "img", [(i, i ^ 4) for i in range(lax.axis_size("img")) if i // 2 != 2])


def send_down(value, distance):
    size = lax.axis_size("img")
    senders = [i for i in range(size) if i & distance and not i & (distance - 1) & ~1]
    return lax.ppermute(value, "img", [(i, i ^ distance) for i in senders])


def corners(over_x, over_y, split):
    rows = over_x.ndim - 2
    first = lax.slice_in_dim(over_x, 0, split, axis=rows)
    second = lax.slice_in_dim(over_y, split, over_y.shape[rows], axis=rows)
    return (swap_y(first), swap_x(second))


def with_cores(value, over_x, over_y, corner_first, corner_second, split):
    near = [(value, 0, 0), (over_x, 2, 0), (over_y, 4, 0), (corner_first, 6, 0), (corner_second, 6, split)]
    return near + [(swap_core(array), mask | 1, first) for array, mask, first in near]


def sum_planes(value):
    far = lax.ppermute(value, "img", [(i, i ^ 6) for i in range(lax.axis_size("img"))])
    return value + swap_near(value) + swap_far(value) + far


def piece_plan(block, slots):
    plan, shapes = [], []
    rows = block + TAIL
    for out, (side, masks) in enumerate(((0, (0,)), (0, (2, 4, 6)), (1, (0, 2, 4, 6)))):
        shapes.append((len(masks), slots, rows))
        for place, mask in enumerate(masks):
            for slot in range(slots):

                def offset(index, mask=mask | side, slot=slot):
                    return (slot * 8 + (lax.rem(index, 8) ^ mask)) * block

                plan.append((out, (place, slot), offset, rows))
    return plan, shapes


def sum_core(kept, sent, other):
    other = swap_core(other).astype(SINGLE)
    return (kept[0].astype(SINGLE) + other[0], (sent.astype(SINGLE) + other[1:]).astype(HALF))


def across_plane(sent):
    return (swap_x(sent[0]), swap_y(sent[1]), swap_both(sent[2]))


def sum_plane(kept, over_x, over_y, over_both):
    return (kept + over_x.astype(SINGLE)) + (over_y.astype(SINGLE) + over_both.astype(SINGLE))


def together(*values):
    return lax.optimization_barrier(values)


def fits_planes(width, block):
    return lax.axis_size("row") == 4 and lax.axis_size("img") == 8 and 8 * block == 3 * width


def own_rows(weights, width):
    length = weights.shape[0]
    block, rest = length // width, length % width
    start = TAIL * width + rest * device_index() - 4 * width
    own = lax.dynamic_update_slice(jnp.zeros(((block + TAIL) * width,), HALF), weights, (start,))
    return own.reshape(block + TAIL, width), start


def per_device(activations, cotangent, weights):
    images, local_rows, columns, width = activations.shape
    tokens = images * local_rows * columns
    size = tokens // images
    rows_all = local_rows * lax.axis_size("row")
    far = images * rows_all
    first_row = lax.axis_index("row") * local_rows
    summary_count = float(images * lax.axis_size("img") * rows_all)
    block = weights.shape[0] // width
    planes = fits_planes(width, block)
    split = block // 2 // TAIL * TAIL
    me = device_index()
    index = me[None]
    z = lax.axis_index("img") // 2
    block_in = activations.reshape(tokens, width)

    row_means = jnp.mean(activations.astype(SINGLE), axis=2)
    if planes:
        own, start = own_rows(weights, width)
        shown = jnp.concatenate(
            [
                jnp.where(me == 0, own[TAIL - 4 : TAIL].astype(SINGLE), 0.0),
                jnp.where(me == 8, own[:TAIL].astype(SINGLE), 0.0),
            ]
        )
    else:
        gathered, matrix_rows = gather_weights(weights, width)
        shown = jnp.zeros((4 + TAIL, width), SINGLE)
    all_means, shown = gather_rows(row_means, shown)
    sums = jnp.stack([jnp.sum(all_means, axis=(0, 1)), jnp.sum(all_means * all_means, axis=(0, 1))])
    sums = jnp.concatenate([sums, shown])
    if planes:
        over_far, sums = together(swap_far(own), sums)
        over_near = swap_near(jnp.stack([own, over_far]))
        over_near, sums = together(over_near, sum_planes(sums + swap_y(sums)))
        held = jnp.stack([own, over_near[0], over_far, over_near[1]])
        first_slot = lax.dynamic_index_in_dim(held, z, 0, keepdims=False)
        first_near = [swap_x(first_slot), swap_y(first_slot), swap_both(first_slot)]
        other_slots = jnp.stack(
            [lax.dynamic_index_in_dim(held, z ^ i, 0, keepdims=False) for i in (1, 2, 3)]
        )
        first_near, other_slots, sums = together(first_near, other_slots, sums)
        first_pieces = [(array, 2 * i, 0) for i, array in enumerate([first_slot] + list(first_near))]
        first_pieces += [(swap_core(array), mask | 1, 0) for array, mask, _ in first_pieces]
        other_x, other_y = swap_x(other_slots), swap_y(other_slots)
    else:
        for axis, distance, _ in image_hops():
            sums = sums + swap(sums, axis, distance)
    summary_mean = sums[0] / summary_count
    summary_var = sums[1] / summary_count - summary_mean * summary_mean
    summary_inv = lax.rsqrt(summary_var + EPS)
    standard = (all_means - summary_mean) * summary_inv
    vectors = sums[2:6] if planes else gathered.astype(SINGLE)
    gain_one, gain_sum, bias_sum, gain_two = (vectors[i : i + 1] for i in range(4))
    summary_low = (standard * gain_sum + bias_sum).astype(HALF).reshape(far, width)

    if planes:
        w_qkv, key_far, value_far = projection_weights(
            index, sums[6:].astype(HALF), summary_low, first_pieces, block
        )
    else:
        w_qkv = jnp.concatenate([matrix_rows[i * width : (i + 1) * width] for i in range(3)], axis=1)
        key_far = dot(summary_low, w_qkv[:, width : 2 * width]).astype(HALF)
        value_far = dot(summary_low, w_qkv[:, 2 * width :]).astype(HALF)
    key_far = key_far.reshape(images, rows_all, width)
    value_far = value_far.reshape(images, rows_all, width)

    forward = None
    for group in image_groups(images):
        forward = attention_forward(
            group,
            forward,
            block_in,
            gain_one,
            w_qkv,
            key_far,
            value_far,
            first_row[None],
            local_rows,
            columns,
        )
        if planes and group[0] == 0:
            other_x, other_y, forward = together(other_x, other_y, forward)
            other_corners = corners(other_x, other_y, split)
    if planes:
        other_corners, forward = together(other_corners, forward)
        given = with_cores(other_slots, other_x, other_y, *other_corners, split)
    query, key, value, mixed, probs = forward

    if planes:
        late_plan, late_shapes = piece_plan(block, 1)
        early_plan, early_shapes = piece_plan(block, 3)
        early_shapes = [shape + (width,) for shape in early_shapes]
        late_shapes = [shape + (width,) for shape in late_shapes]
    else:
        early_shapes = [(TAIL + width + 2 * FF, width)]
        late_shapes = [(TAIL + 3 * width, width)]
        early_plan = [(0, (), lambda i: i * 0, early_shapes[0][0])]
        late_plan = [(0, (), lambda i: i * 0, late_shapes[0][0])]
        given = [(jnp.pad(matrix_rows[3 * width :], ((TAIL, 0), (0, 0))), 0, 0)]

    out, middle_grad, mixed_grad, gain_two_grad, *early = feed_forward(
        index,
        block_in,
        mixed,
        cotangent.reshape(tokens, width),
        gain_two,
        given,
        block if planes else None,
        FF,
        size,
        early_plan,
        early_shapes,
    )
    standard_flat = standard.reshape(far, width)
    last = [gain_one, gain_two_grad, w_qkv, summary_low, standard_flat, gain_sum]
    if planes:
        (early_kept, early_sent), mixed_grad = together(sum_core(*early), mixed_grad)
        early_in = across_plane(early_sent)
    steps = images * local_rows // math.gcd(local_rows, 4)
    backward = attention_backward(
        (0, steps),
        None,
        index,
        block_in,
        query,
        key,
        value,
        key_far,
        value_far,
        probs,
        mixed_grad,
        last,
        local_rows,
        columns,
        late_plan,
        late_shapes,
    )
    query_grad, key_grad, value_grad, shared, *late = backward
    if planes:
        (late_kept, late_sent), shared, early = together(
            sum_core(*late), shared + swap_core(shared), sum_plane(early_kept, *early_in)
        )
        late_in = across_plane(late_sent)
        by_mask = [
            jnp.where(z == i, 0.0, lax.dynamic_index_in_dim(early, (z ^ i) - 1, 0, keepdims=False))
            for i in range(4)
        ]
        early_in = swap_near(jnp.stack([by_mask[1], by_mask[3]]).astype(HALF))
        small = shared[far:]
        over_x = swap_x(shared)
        small = small + over_x[far:] + swap_y(small) + swap_both(small)
        late_in, small, shared, early_in = together(
            late_in, small, shared[:far] + over_x[:far], early_in
        )
        late = sum_plane(late_kept, *late_in)[0]
        late = late + send_down(late.astype(HALF), 2).astype(SINGLE)
        late, small = together(late, sum_planes(small))
    else:
        for axis, distance, _ in row_hops():
            shared = shared + swap(shared, axis, distance)
        small = shared[far:]
        for axis, distance, _ in image_hops():
            small = small + swap(small, axis, distance)
    own_grad = lax.dynamic_slice_in_dim(
        shared[:far].reshape(images, rows_all, width), first_row, local_rows, axis=1
    )
    own_standard = lax.dynamic_slice_in_dim(standard, first_row, local_rows, axis=1)
    mean_grad = summary_inv * (
        own_grad - small[0] / summary_count - own_standard * (small[1] / summary_count)
    )
    input_grad = None
    for group in [(0, images)]:
        input_grad = input_grads(
            group,
            input_grad,
            block_in,
            gain_one,
            query_grad,
            key_grad,
            value_grad,
            w_qkv,
            middle_grad,
            mean_grad / columns,
            local_rows,
            columns,
        )
    if planes:
        late_own = late + send_down(late.astype(HALF), 4).astype(SINGLE)
        early_far = send_far((by_mask[2] + early_in[1].astype(SINGLE)).astype(HALF))
        early_own = by_mask[0] + early_in[0].astype(SINGLE) + early_far.astype(SINGLE)
        head = jnp.where(
            me == 0,
            jnp.concatenate([jnp.zeros((TAIL - 4, width), SINGLE), small[2:6]]),
            jnp.where(me == 8, small[8:], 0.0),
        )
        mine = jnp.where(z == 0, late_own, early_own)
        mine = jnp.concatenate([mine[:TAIL] + head, mine[TAIL:]])
        weight_grad = lax.dynamic_slice(mine.reshape(-1), (start,), weights.shape)
    else:
        grad_rows = jnp.concatenate([late[0][TAIL:], early[0][TAIL:]]).astype(SINGLE)
        weight_grad = scatter_grads(small[2:6], grad_rows, weights.shape[0])
    return (
        out.reshape(activations.shape),
        input_grad.reshape(activations.shape),
        weight_grad,
        summary_mean,
        summary_var,
    )


def solution(mesh):
    placed = (P("img", "row", None, None), P("img", "row", None, None), P(("img", "row")))
    return jax.shard_map(
        per_device,
        mesh=mesh,
        in_specs=placed,
        out_specs=(
            P("img", "row", None, None),
            P("img", "row", None, None),
            P(("img", "row")),
            P(),
            P(),
        ),
        check_vma=False,
    )
```

profile of v0, /device:TPU:0, one launch (start us, length us, event | category | flops | bytes accessed | tf_op | source)
XLA Modules:
  0.0 227.9 jit_solution(5609724890038138332)
XLA Ops:
  0.7 3.8 %dynamic_update_slice.3 = bf16[106496]{0:T(1024)(128)(2,1)S(1)} dynamic-update-slice(bf16[106496]{0:T(1024)(128)(2,1)S(1)} %broadcast_in_dim.57, bf16[98368]{0:T(1024)(128)(2,1)} %param.6, s32[]{:T(128)S(6)} %select_n.130) | dynamic-update-slice | bytes 393476 | tf_op jit(solution)/shard_map/dynamic_update_slice | solution.py:981
  4.6 2.0 convert_reduce_fusion
  7.3 3.6 %collective-permute-start = (bf16[208,512]{1,0:T(8,128)(2,1)S(1)}, bf16[208,512]{1,0:T(8,128)(2,1)S(1)}, u32[]{:S(2)}, u32[]{:S(2)}) collective-permute-start(bf16[208,512]{1,0:T(8,128)(2,1)S(1)} %reshape.189), channel_id=1, source_target_pairs={{0,16},{4,20},{8,24},{12,28},{16,0},{20,4},{24,8},{28,12},{1,17},{... | collective-permute-start | bytes 638984 | tf_op jit(solution)/shard_map/ppermute | solution.py:27
  11.9 1.6 collective-permute-start.2
  13.4 3.4 %collective-permute-done.2 = f32[44,512]{1,0:T(8,128)S(1)} collective-permute-done((f32[44,512]{1,0:T(8,128)S(1)}, f32[44,512]{1,0:T(8,128)S(1)}, u32[]{:S(2)}, u32[]{:S(2)}) %collective-permute-start.2) | collective-permute-done | bytes 90144 | tf_op jit(solution)/shard_map/ppermute | solution.py:27
  17.6 3.8 %collective-permute-done = bf16[208,512]{1,0:T(8,128)(2,1)S(1)} collective-permute-done((bf16[208,512]{1,0:T(8,128)(2,1)S(1)}, bf16[208,512]{1,0:T(8,128)(2,1)S(1)}, u32[]{:S(2)}, u32[]{:S(2)}) %collective-permute-start) | collective-permute-done | bytes 213024 | tf_op jit(solution)/shard_map/ppermute | solution.py:27
  23.8 2.6 %collective-permute-done.4 = f32[22,512]{1,0:T(8,128)S(1)} collective-permute-done((f32[22,512]{1,0:T(8,128)S(1)}, f32[22,512]{1,0:T(8,128)S(1)}, u32[]{:S(2)}, u32[]{:S(2)}) %collective-permute-start.4) | collective-permute-done | bytes 45088 | tf_op jit(solution)/shard_map/ppermute | solution.py:27
  27.7 2.2 collective-permute-start.6
  31.2 4.0 %collective-permute-done.5 = f32[22,512]{1,0:T(8,128)S(1)} collective-permute-done((f32[22,512]{1,0:T(8,128)S(1)}, f32[22,512]{1,0:T(8,128)S(1)}, u32[]{:S(2)}, u32[]{:S(2)}) %collective-permute-start.5) | collective-permute-done | bytes 45088 | tf_op jit(solution)/shard_map/ppermute | solution.py:27
  35.3 3.0 %collective-permute-done.7 = f32[22,512]{1,0:T(8,128)S(1)} collective-permute-done((f32[22,512]{1,0:T(8,128)S(1)}, f32[22,512]{1,0:T(8,128)S(1)}, u32[]{:S(2)}, u32[]{:S(2)}) %collective-permute-start.7) | collective-permute-done | bytes 45088 | tf_op jit(solution)/shard_map/ppermute | solution.py:937
  38.5 2.5 %collective-permute-start.10 = (bf16[208,512]{1,0:T(8,128)(2,1)S(1)}, bf16[208,512]{1,0:T(8,128)(2,1)S(1)}, u32[]{:S(2)}, u32[]{:S(2)}) collective-permute-start(bf16[208,512]{1,0:T(8,128)(2,1)S(1)} %get-tuple-element.147.refs_0_), channel_id=1, source_target_pairs={{0,6},{1,7},{2,4},{3,5},{4,2},{5,3},{6,0},{7,1},{8,14},{9,15},{10,... | collective-permute-start | bytes 638984 | tf_op jit(solution)/shard_map/ppermute | solution.py:903
  43.0 4.7 %collective-permute-done.10.refs_3_ = bf16[208,512]{1,0:T(8,128)(2,1)S(1)} collective-permute-done((bf16[208,512]{1,0:T(8,128)(2,1)S(1)}, bf16[208,512]{1,0:T(8,128)(2,1)S(1)}, u32[]{:S(2)}, u32[]{:S(2)}) %collective-permute-start.10) | collective-permute-done | bytes 213024 | tf_op jit(solution)/shard_map/ppermute | solution.py:903
  47.7 2.9 %collective-permute-done.8.refs_1_ = bf16[208,512]{1,0:T(8,128)(2,1)S(1)} collective-permute-done((bf16[208,512]{1,0:T(8,128)(2,1)S(1)}, bf16[208,512]{1,0:T(8,128)(2,1)S(1)}, u32[]{:S(2)}, u32[]{:S(2)}) %collective-permute-start.8) | collective-permute-done | bytes 213024 | tf_op jit(solution)/shard_map/ppermute | solution.py:27
  58.0 3.2 %projection_weights.1 = (bf16[512,1536]{1,0:T(8,128)(2,1)}, bf16[48,512]{1,0:T(8,128)(2,1)}, bf16[48,512]{1,0:T(8,128)(2,1)}) custom-call(s32[1]{0:T(128)} %bitcast.index_ref, bf16[16,512]{1,0:T(8,128)(2,1)} %slice.238.tail_ref, bf16[48,512]{1,0:T(8,128)(2,1)} %get-tuple-element.135.summary_ref.rest_3_, bf16[208,512]{1,0:T(8,128)(2,1)} %copy-done.1, ...), custom_call_target="tpu_custom_call" | custom-call | tf_op jit(solution)/shard_map/projection_weights/pallas_call | solution.py:874
  61.1 8.6 %attention_forward.2 = (bf16[2304,512]{1,0:T(8,128)(2,1)}, bf16[2304,512]{1,0:T(8,128)(2,1)}, bf16[2304,512]{1,0:T(8,128)(2,1)}, bf16[2304,512]{1,0:T(8,128)(2,1)}, bf16[12,8,208,192]{3,2,1,0:T(8,128)(2,1)}) custom-call(s32[1]{0:T(128)} %bitcast.9.refs_0_, bf16[2304,512]{1,0:T(8,128)(2,1)} %bitcast.54, f32[1,512]{1,0:T(1,128)} %get-tuple-element.160.refs_2_.rest_0_.refs_1_, ...), custom_call_target="tpu_custom_call" | custom-call | flops 1862270976 | bytes 7274496 | tf_op jit(solution)/shard_map/attention_forward/pallas_call | solution.py:325
  71.6 14.3 %attention_forward.3 = (bf16[2304,512]{1,0:T(8,128)(2,1)}, bf16[2304,512]{1,0:T(8,128)(2,1)}, bf16[2304,512]{1,0:T(8,128)(2,1)}, bf16[2304,512]{1,0:T(8,128)(2,1)}, bf16[12,8,208,192]{3,2,1,0:T(8,128)(2,1)}) custom-call(s32[1]{0:T(128)} %bitcast.9.refs_0_, ...), custom_call_target="tpu_custom_call", output_to_operand_aliasing={{0}: (7, {}), {1}: (8, {}), {2}: (9, {}), {3}: (10, {}), {4... | custom-call | flops 3724541952 | bytes 14548992 | tf_op jit(solution)/shard_map/attention_forward/pallas_call | solution.py:325
  86.5 1.6 collective-permute-done.22.rest_8_
  89.4 48.6 %feed_forward.1 = (bf16[2304,512]{1,0:T(8,128)(2,1)}, f32[2304,512]{1,0:T(8,128)}, bf16[2304,512]{1,0:T(8,128)(2,1)}, f32[1,512]{1,0:T(1,128)}, bf16[1,3,208,512...) custom-call(s32[1]{0:T(128)} %bitcast.index_ref, bf16[2304,512]{1,0:T(8,128)(2,1)} %bitcast.56, ...), custom_call_target="tpu_custom_call" | custom-call | flops 32614907904 | bytes 24903680 | tf_op jit(solution)/shard_map/feed_forward/pallas_call | solution.py:494
  138.2 4.9 %collective-permute-done.24 = bf16[4,3,208,512]{3,2,1,0:T(8,128)(2,1)S(1)} collective-permute-done((bf16[4,3,208,512]{3,2,1,0:T(8,128)(2,1)}, bf16[4,3,208,512]{3,2,1,0:T(8,128)(2,1)S(1)}, u32[]{:S(2)}, u32[]{:S(2)}) %collective-permute-start.24) | collective-permute-done | bytes 2555936 | tf_op jit(solution)/shard_map/ppermute | solution.py:27
  149.9 23.7 %attention_backward.1 = (bf16[2304,512]{1,0:T(8,128)(2,1)}, bf16[2304,512]{1,0:T(8,128)(2,1)}, bf16[2304,512]{1,0:T(8,128)(2,1)}, f32[72,512]{1,0:T(8,128)}, bf1...) custom-call(s32[1]{0:T(128)} %bitcast.index_ref, ...), custom_call_target="tpu_custom_call" | custom-call | flops 7549747200 | bytes 26542080 | tf_op jit(solution)/shard_map/attention_backward/pallas_call | solution.py:727
  174.2 2.3 collective-permute-done.26
  178.3 1.8 add_add_fusion
  181.4 1.6 collective-permute-start.33
  185.3 1.6 collective-permute-start.30
  189.4 1.8 collective-permute-start.32
  191.2 2.4 %collective-permute-done.30 = bf16[1,208,512]{2,1,0:T(8,128)(2,1)S(1)} collective-permute-done((bf16[1,208,512]{2,1,0:T(8,128)(2,1)S(1)}, bf16[1,208,512]{2,1,0:T(8,128)(2,1)S(1)}, u32[]{:S(2)}, u32[]{:S(2)}) %collective-permute-start.30) | collective-permute-done | bytes 213024 | tf_op jit(solution)/shard_map/ppermute | solution.py:27
  193.7 5.0 %collective-permute-done.31 = bf16[1,208,512]{2,1,0:T(8,128)(2,1)S(1)} collective-permute-done((bf16[1,208,512]{2,1,0:T(8,128)(2,1)S(1)}, bf16[1,208,512]{2,1,0:T(8,128)(2,1)S(1)}, u32[]{:S(2)}, u32[]{:S(2)}) %collective-permute-start.31) | collective-permute-done | bytes 213024 | tf_op jit(solution)/shard_map/ppermute | solution.py:27
  199.3 1.7 collective-permute-start.39
  201.0 2.1 collective-permute-start.40
  203.2 1.9 collective-permute-start.42
  207.4 5.5 %collective-permute-done.37 = bf16[208,512]{1,0:T(8,128)(2,1)S(1)} collective-permute-done((bf16[208,512]{1,0:T(8,128)(2,1)S(1)}, bf16[208,512]{1,0:T(8,128)(2,1)S(1)}, u32[]{:S(2)}, u32[]{:S(2)}) %collective-permute-start.37) | collective-permute-done | bytes 213024 | tf_op jit(solution)/shard_map/ppermute | solution.py:921
  215.1 11.5 %input_grads.1 = f32[2304,512]{1,0:T(8,128)} custom-call(bf16[2304,512]{1,0:T(8,128)(2,1)} %bitcast.58, f32[1,512]{1,0:T(1,128)} %get-tuple-element.160.refs_2_.rest_0_.refs_1_, bf16[2304,512]{1,0:T(8,128)(2,1)} %get-tuple-element.113.refs_2_, bf16[2304,512]{1,0:T(8,128)(2,1)} %get-tuple-element.114.refs_3_, bf16[2304,512]{1,0:T(8,128)(2,1)} %get-tuple-element.115.refs_4_, ...), custom_call_target="tpu_custom_call" | custom-call | flops 3623878656 | bytes 18874368 | tf_op jit(solution)/shard_map/input_grads/pallas_call | solution.py:814
  (188 shorter events, 42.6 us)
Async XLA Ops:
  7.3 14.1 %collective-permute-start = (bf16[208,512]{1,0:T(8,128)(2,1)S(1)}, bf16[208,512]{1,0:T(8,128)(2,1)S(1)}, u32[]{:S(2)}, u32[]{:S(2)}) collective-permute-start(bf16[208,512]{1,0:T(8,128)(2,1)S(1)} %reshape.189), channel_id=1, source_target_pairs={{0,16},{4,20},{8,24},{12,28},{16,0},{20,4},{24,8},{28,12},{1,17},{... | collective-permute-start | bytes 638984 | tf_op jit(solution)/shard_map/ppermute | solution.py:27
  21.4 16.8 %collective-permute-start.3 = (bf16[2,208,512]{2,1,0:T(8,128)(2,1)S(1)}, bf16[2,208,512]{2,1,0:T(8,128)(2,1)S(1)}, u32[]{:S(2)}, u32[]{:S(2)}) collective-permute-start(bf16[2,208,512]{2,1,0:T(8,128)(2,1)S(1)} %pad_maximum_fusion.2), channel_id=1, source_target_pairs={{0,8},{4,12},{8,0},{12,4},{16,24},{20,28},{24,16},{28,20},{1,9},{5... | collective-permute-start | bytes 1277960 | tf_op jit(solution)/shard_map/ppermute | solution.py:27
  26.4 8.9 %collective-permute-start.5 = (f32[22,512]{1,0:T(8,128)S(1)}, f32[22,512]{1,0:T(8,128)S(1)}, u32[]{:S(2)}, u32[]{:S(2)}) collective-permute-start(f32[22,512]{1,0:T(8,128)S(1)} %add.202), channel_id=1, source_target_pairs={{0,8},{4,12},{8,0},{12,4},{16,24},{20,28},{24,16},{28,20},{1,9},{5... | collective-permute-start | bytes 135176 | tf_op jit(solution)/shard_map/ppermute | solution.py:27
  27.7 7.6 %collective-permute-start.6 = (f32[22,512]{1,0:T(8,128)S(1)}, f32[22,512]{1,0:T(8,128)S(1)}, u32[]{:S(2)}, u32[]{:S(2)}) collective-permute-start(f32[22,512]{1,0:T(8,128)S(1)} %add.202), channel_id=1, source_target_pairs={{0,16},{4,20},{8,24},{12,28},{16,0},{20,4},{24,8},{28,12},{1,17},{... | collective-permute-start | bytes 135176 | tf_op jit(solution)/shard_map/ppermute | solution.py:27
  29.9 8.4 %collective-permute-start.7 = (f32[22,512]{1,0:T(8,128)S(1)}, f32[22,512]{1,0:T(8,128)S(1)}, u32[]{:S(2)}, u32[]{:S(2)}) collective-permute-start(f32[22,512]{1,0:T(8,128)S(1)} %add.202), channel_id=1, source_target_pairs={{0,24},{4,28},{8,16},{12,20},{16,8},{20,12},{24,0},{28,4},{1,25},{... | collective-permute-start | bytes 135176 | tf_op jit(solution)/shard_map/ppermute | solution.py:937
  38.5 9.2 %collective-permute-start.10 = (bf16[208,512]{1,0:T(8,128)(2,1)S(1)}, bf16[208,512]{1,0:T(8,128)(2,1)S(1)}, u32[]{:S(2)}, u32[]{:S(2)}) collective-permute-start(bf16[208,512]{1,0:T(8,128)(2,1)S(1)} %get-tuple-element.147.refs_0_), channel_id=1, source_target_pairs={{0,6},{1,7},{2,4},{3,5},{4,2},{5,3},{6,0},{7,1},{8,14},{9,15},{10,... | collective-permute-start | bytes 638984 | tf_op jit(solution)/shard_map/ppermute | solution.py:903
  41.1 9.5 %collective-permute-start.8 = (bf16[208,512]{1,0:T(8,128)(2,1)S(1)}, bf16[208,512]{1,0:T(8,128)(2,1)S(1)}, u32[]{:S(2)}, u32[]{:S(2)}) collective-permute-start(bf16[208,512]{1,0:T(8,128)(2,1)S(1)} %get-tuple-element.147.refs_0_), channel_id=1, source_target_pairs={{0,2},{1,3},{2,0},{3,1},{4,6},{5,7},{6,4},{7,5},{8,10},{9,11},{10,... | collective-permute-start | bytes 638984 | tf_op jit(solution)/shard_map/ppermute | solution.py:27
  41.6 9.0 %collective-permute-start.9 = (bf16[208,512]{1,0:T(8,128)(2,1)S(1)}, bf16[208,512]{1,0:T(8,128)(2,1)S(1)}, u32[]{:S(2)}, u32[]{:S(2)}) collective-permute-start(bf16[208,512]{1,0:T(8,128)(2,1)S(1)} %get-tuple-element.147.refs_0_), channel_id=1, source_target_pairs={{0,4},{4,0},{8,12},{12,8},{16,20},{20,16},{24,28},{28,24},{1,5},{5... | collective-permute-start | bytes 638984 | tf_op jit(solution)/shard_map/ppermute | solution.py:27
  42.9 13.0 %collective-permute-start.13 = (bf16[208,512]{1,0:T(8,128)(2,1)S(1)}, bf16[208,512]{1,0:T(8,128)(2,1)S(1)}, u32[]{:S(2)}, u32[]{:S(2)}) collective-permute-start(bf16[208,512]{1,0:T(8,128)(2,1)S(1)} %get-tuple-element.147.refs_0_), channel_id=1, source_target_pairs={{0,1},{1,0},{2,3},{3,2},{4,5},{5,4},{6,7},{7,6},{8,9},{9,8},{10,11... | collective-permute-start | bytes 638984 | tf_op jit(solution)/shard_map/ppermute | solution.py:27
  50.6 19.1 %collective-permute-start.11 = (bf16[3,208,512]{2,1,0:T(8,128)(2,1)S(1)}, bf16[3,208,512]{2,1,0:T(8,128)(2,1)S(1)}, u32[]{:S(2)}, u32[]{:S(2)}) collective-permute-start(bf16[3,208,512]{2,1,0:T(8,128)(2,1)S(1)} %pad_maximum_fusion.1.rest_0_), channel_id=1, source_target_pairs={{0,2},{1,3},{2,0},{3,1},{4,6},{5,7},{6,4},{7,5},{8,10},{9,11},{10,... | collective-permute-start | bytes 1916936 | tf_op jit(solution)/shard_map/ppermute | solution.py:27
  52.1 17.6 %collective-permute-start.12 = (bf16[3,208,512]{2,1,0:T(8,128)(2,1)S(1)}, bf16[3,208,512]{2,1,0:T(8,128)(2,1)S(1)}, u32[]{:S(2)}, u32[]{:S(2)}) collective-permute-start(bf16[3,208,512]{2,1,0:T(8,128)(2,1)S(1)} %pad_maximum_fusion.1.rest_0_), channel_id=1, source_target_pairs={{0,4},{4,0},{8,12},{12,8},{16,20},{20,16},{24,28},{28,24},{1,5},{5... | collective-permute-start | bytes 1916936 | tf_op jit(solution)/shard_map/ppermute | solution.py:27
  56.6 30.0 %collective-permute-start.19 = (bf16[3,208,512]{2,1,0:T(8,128)(2,1)S(1)}, bf16[3,208,512]{2,1,0:T(8,128)(2,1)S(1)}, u32[]{:S(2)}, u32[]{:S(2)}) collective-permute-start(bf16[3,208,512]{2,1,0:T(8,128)(2,1)S(1)} %pad_maximum_fusion.1.rest_0_), channel_id=1, source_target_pairs={{0,1},{1,0},{2,3},{3,2},{4,5},{5,4},{6,7},{7,6},{8,9},{9,8},{10,11... | collective-permute-start | bytes 1916936 | tf_op jit(solution)/shard_map/ppermute | solution.py:27
  69.8 18.3 %collective-permute-start.20 = (bf16[3,208,512]{2,1,0:T(8,128)(2,1)S(1)}, bf16[3,208,512]{2,1,0:T(8,128)(2,1)S(1)}, u32[]{:S(2)}, u32[]{:S(2)}) collective-permute-start(bf16[3,208,512]{2,1,0:T(8,128)(2,1)S(1)} %collective-permute-done.11.rest_1_), channel_id=1, source_target_pairs={{0,1},{1,0},{2,3},{3,2},{4,5},{5,4},{6,7},{7,6},{8,9},{9,8},{10,11... | collective-permute-start | bytes 1916936 | tf_op jit(solution)/shard_map/ppermute | solution.py:27
  70.0 18.1 %collective-permute-start.21 = (bf16[3,208,512]{2,1,0:T(8,128)(2,1)S(1)}, bf16[3,208,512]{2,1,0:T(8,128)(2,1)S(1)}, u32[]{:S(2)}, u32[]{:S(2)}) collective-permute-start(bf16[3,208,512]{2,1,0:T(8,128)(2,1)S(1)} %collective-permute-done.12.rest_2_), channel_id=1, source_target_pairs={{0,1},{1,0},{2,3},{3,2},{4,5},{5,4},{6,7},{7,6},{8,9},{9,8},{10,11... | collective-permute-start | bytes 1916936 | tf_op jit(solution)/shard_map/ppermute | solution.py:27
  70.4 15.5 %collective-permute-start.18 = (bf16[3,112,512]{2,1,0:T(8,128)(2,1)S(1)}, bf16[3,112,512]{2,1,0:T(8,128)(2,1)S(1)}, u32[]{:S(2)}, u32[]{:S(2)}) collective-permute-start(bf16[3,112,512]{2,1,0:T(8,128)(2,1)S(1)} %slice.156), channel_id=1, source_target_pairs={{0,2},{1,3},{2,0},{3,1},{4,6},{5,7},{6,4},{7,5},{8,10},{9,11},{10,... | collective-permute-start | bytes 1032200 | tf_op jit(solution)/shard_map/ppermute | solution.py:27
  71.0 15.0 %collective-permute-start.17 = (bf16[3,96,512]{2,1,0:T(8,128)(2,1)S(1)}, bf16[3,96,512]{2,1,0:T(8,128)(2,1)S(1)}, u32[]{:S(2)}, u32[]{:S(2)}) collective-permute-start(bf16[3,96,512]{2,1,0:T(8,128)(2,1)S(1)} %slice.155), channel_id=1, source_target_pairs={{0,4},{4,0},{8,12},{12,8},{16,20},{20,16},{24,28},{28,24},{1,5},{5... | collective-permute-start | bytes 884744 | tf_op jit(solution)/shard_map/ppermute | solution.py:27
  146.4 31.0 %collective-permute-start.27 = (bf16[3,208,512]{2,1,0:T(8,128)(2,1)}, bf16[3,208,512]{2,1,0:T(8,128)(2,1)S(1)}, u32[]{:S(2)}, u32[]{:S(2)}) collective-permute-start(bf16[3,208,512]{2,1,0:T(8,128)(2,1)} %get-tuple-element.139), channel_id=1, source_target_pairs={{0,2},{1,3},{2,0},{3,1},{4,6},{5,7},{6,4},{7,5},{8,10},{9,11},{10,... | collective-permute-start | bytes 1916936 | tf_op jit(solution)/shard_map/ppermute | solution.py:27
  147.9 30.2 %collective-permute-start.28 = (bf16[3,208,512]{2,1,0:T(8,128)(2,1)}, bf16[3,208,512]{2,1,0:T(8,128)(2,1)}, u32[]{:S(2)}, u32[]{:S(2)}) collective-permute-start(bf16[3,208,512]{2,1,0:T(8,128)(2,1)} %get-tuple-element.141), channel_id=1, source_target_pairs={{0,4},{4,0},{8,12},{12,8},{16,20},{20,16},{24,28},{28,24},{1,5},{5... | collective-permute-start | bytes 1916936 | tf_op jit(solution)/shard_map/ppermute | solution.py:27
  149.3 29.0 %collective-permute-start.29 = (bf16[3,208,512]{2,1,0:T(8,128)(2,1)}, bf16[3,208,512]{2,1,0:T(8,128)(2,1)}, u32[]{:S(2)}, u32[]{:S(2)}) collective-permute-start(bf16[3,208,512]{2,1,0:T(8,128)(2,1)} %get-tuple-element.140), channel_id=1, source_target_pairs={{0,6},{1,7},{2,4},{3,5},{4,2},{5,3},{6,0},{7,1},{8,14},{9,15},{10,... | collective-permute-start | bytes 1916936 | tf_op jit(solution)/shard_map/ppermute | solution.py:903
  173.6 6.5 %collective-permute-start.25 = (bf16[4,1,208,512]{3,2,1,0:T(8,128)(2,1)}, bf16[4,1,208,512]{3,2,1,0:T(8,128)(2,1)S(1)}, u32[]{:S(2)}, u32[]{:S(2)}) collective-permute-start(bf16[4,1,208,512]{3,2,1,0:T(8,128)(2,1)} %get-tuple-element.118), channel_id=1, source_target_pairs={{0,1},{1,0},{2,3},{3,2},{4,5},{5,4},{6,7},{7,6},{8,9},{9,8},{10,11... | collective-permute-start | bytes 2555912 | tf_op jit(solution)/shard_map/ppermute | solution.py:27
  181.4 6.7 %collective-permute-start.33 = (f32[72,512]{1,0:T(8,128)S(1)}, f32[72,512]{1,0:T(8,128)S(1)}, u32[]{:S(2)}, u32[]{:S(2)}) collective-permute-start(f32[72,512]{1,0:T(8,128)S(1)} %add.221), channel_id=1, source_target_pairs={{0,2},{1,3},{2,0},{3,1},{4,6},{5,7},{6,4},{7,5},{8,10},{9,11},{10,... | collective-permute-start | bytes 442376 | tf_op jit(solution)/shard_map/ppermute | solution.py:27
  183.0 6.5 %collective-permute-start.34 = (f32[24,512]{1,0:T(8,128)S(1)}, f32[24,512]{1,0:T(8,128)S(1)}, u32[]{:S(2)}, u32[]{:S(2)}) collective-permute-start(f32[24,512]{1,0:T(8,128)S(1)} %slice.168), channel_id=1, source_target_pairs={{0,4},{4,0},{8,12},{12,8},{16,20},{20,16},{24,28},{28,24},{1,5},{5... | collective-permute-start | bytes 147464 | tf_op jit(solution)/shard_map/ppermute | solution.py:27
  184.3 6.9 %collective-permute-start.35 = (f32[24,512]{1,0:T(8,128)S(1)}, f32[24,512]{1,0:T(8,128)S(1)}, u32[]{:S(2)}, u32[]{:S(2)}) collective-permute-start(f32[24,512]{1,0:T(8,128)S(1)} %slice.168), channel_id=1, source_target_pairs={{0,6},{1,7},{2,4},{3,5},{4,2},{5,3},{6,0},{7,1},{8,14},{9,15},{10,... | collective-permute-start | bytes 147464 | tf_op jit(solution)/shard_map/ppermute | solution.py:903
  185.1 13.6 %collective-permute-start.36 = (bf16[2,208,512]{2,1,0:T(8,128)(2,1)S(1)}, bf16[2,208,512]{2,1,0:T(8,128)(2,1)S(1)}, u32[]{:S(2)}, u32[]{:S(2)}) collective-permute-start(bf16[2,208,512]{2,1,0:T(8,128)(2,1)S(1)} %pad_maximum_fusion.3), channel_id=1, source_target_pairs={{0,8},{4,12},{8,0},{12,4},{16,24},{20,28},{24,16},{28,20},{1,9},{5... | collective-permute-start | bytes 1277960 | tf_op jit(solution)/shard_map/ppermute | solution.py:27
  185.3 8.4 %collective-permute-start.30 = (bf16[1,208,512]{2,1,0:T(8,128)(2,1)S(1)}, bf16[1,208,512]{2,1,0:T(8,128)(2,1)S(1)}, u32[]{:S(2)}, u32[]{:S(2)}) collective-permute-start(bf16[1,208,512]{2,1,0:T(8,128)(2,1)S(1)} %get-tuple-element.150), channel_id=1, source_target_pairs={{0,2},{1,3},{2,0},{3,1},{4,6},{5,7},{6,4},{7,5},{8,10},{9,11},{10,... | collective-permute-start | bytes 638984 | tf_op jit(solution)/shard_map/ppermute | solution.py:27
  188.1 10.6 %collective-permute-start.31 = (bf16[1,208,512]{2,1,0:T(8,128)(2,1)S(1)}, bf16[1,208,512]{2,1,0:T(8,128)(2,1)S(1)}, u32[]{:S(2)}, u32[]{:S(2)}) collective-permute-start(bf16[1,208,512]{2,1,0:T(8,128)(2,1)S(1)} %get-tuple-element.149), channel_id=1, source_target_pairs={{0,4},{4,0},{8,12},{12,8},{16,20},{20,16},{24,28},{28,24},{1,5},{5... | collective-permute-start | bytes 638984 | tf_op jit(solution)/shard_map/ppermute | solution.py:27
  189.4 9.3 %collective-permute-start.32 = (bf16[1,208,512]{2,1,0:T(8,128)(2,1)S(1)}, bf16[1,208,512]{2,1,0:T(8,128)(2,1)S(1)}, u32[]{:S(2)}, u32[]{:S(2)}) collective-permute-start(bf16[1,208,512]{2,1,0:T(8,128)(2,1)S(1)} %get-tuple-element.148), channel_id=1, source_target_pairs={{0,6},{1,7},{2,4},{3,5},{4,2},{5,3},{6,0},{7,1},{8,14},{9,15},{10,... | collective-permute-start | bytes 638984 | tf_op jit(solution)/shard_map/ppermute | solution.py:903
  198.7 7.7 %collective-permute-start.38 = (f32[24,512]{1,0:T(8,128)S(1)}, f32[24,512]{1,0:T(8,128)S(1)}, u32[]{:S(2)}, u32[]{:S(2)}) collective-permute-start(f32[24,512]{1,0:T(8,128)S(1)} %fusion.8), channel_id=1, source_target_pairs={{0,8},{4,12},{8,0},{12,4},{16,24},{20,28},{24,16},{28,20},{1,9},{5... | collective-permute-start | bytes 147464 | tf_op jit(solution)/shard_map/ppermute | solution.py:27
  199.3 7.2 %collective-permute-start.39 = (f32[24,512]{1,0:T(8,128)S(1)}, f32[24,512]{1,0:T(8,128)S(1)}, u32[]{:S(2)}, u32[]{:S(2)}) collective-permute-start(f32[24,512]{1,0:T(8,128)S(1)} %fusion.8), channel_id=1, source_target_pairs={{0,16},{4,20},{8,24},{12,28},{16,0},{20,4},{24,8},{28,12},{1,17},{... | collective-permute-start | bytes 147464 | tf_op jit(solution)/shard_map/ppermute | solution.py:27
  203.2 23.4 %collective-permute-start.42 = (bf16[208,512]{1,0:T(8,128)(2,1)S(1)}, bf16[208,512]{1,0:T(8,128)(2,1)S(1)}, u32[]{:S(2)}, u32[]{:S(2)}) collective-permute-start(bf16[208,512]{1,0:T(8,128)(2,1)S(1)} %fusion.5), channel_id=1, source_target_pairs={{0,16},{4,20},{8,24},{12,28},{24,8},{28,12},{1,17},{5,21},{9,25},{... | collective-permute-start | bytes 638984 | tf_op jit(solution)/shard_map/ppermute | solution.py:915
  205.2 7.7 %collective-permute-start.37 = (bf16[208,512]{1,0:T(8,128)(2,1)S(1)}, bf16[208,512]{1,0:T(8,128)(2,1)S(1)}, u32[]{:S(2)}, u32[]{:S(2)}) collective-permute-start(bf16[208,512]{1,0:T(8,128)(2,1)S(1)} %bitcast_convert_fusion), channel_id=1, source_target_pairs={{8,0},{12,4},{24,16},{28,20},{9,1},{13,5},{25,17},{29,21},{10,2},{... | collective-permute-start | bytes 638984 | tf_op jit(solution)/shard_map/ppermute | solution.py:921
  213.1 13.5 %collective-permute-start.41 = (bf16[208,512]{1,0:T(8,128)(2,1)S(1)}, bf16[208,512]{1,0:T(8,128)(2,1)S(1)}, u32[]{:S(2)}, u32[]{:S(2)}) collective-permute-start(bf16[208,512]{1,0:T(8,128)(2,1)S(1)} %convert_element_type.118), channel_id=1, source_target_pairs={{16,0},{20,4},{17,1},{21,5},{18,2},{22,6},{19,3},{23,7}} | collective-permute-start | bytes 638984 | tf_op jit(solution)/shard_map/ppermute | solution.py:921
  (36 other events, 354.9 us)
where the time goes:
time: 229 us; the launch traced here: 228 us
  Pallas kernels  110 us (48%)
  waiting for transfers between devices  49.2 us (21%)
  starting transfers between devices  44.2 us (19%)
  local copies, waits for them, and re-layouts  12.7 us (6%)
  other arithmetic  10.7 us (5%)
    pallas_call x1, Pallas kernels, feed_forward(): pl.pallas_call(functools.partial(feed_forward_kernel, 512, plan, masks, b...  48.6 us
    ppermute x34, waiting for transfers between devices, swap(): return lax.ppermute(value, axis, [(i, i ^ distance) for i in range(size)])  35.1 us
    ppermute x34, starting transfers between devices, swap(): return lax.ppermute(value, axis, [(i, i ^ distance) for i in range(size)])  30.7 us
    pallas_call x1, Pallas kernels, attention_backward(): pl.pallas_call(functools.partial(attention_backward_kernel, 1.0 / math.sq...  23.7 us
    pallas_call x2, Pallas kernels, attention_forward(): pl.pallas_call(body, grid_spec=pltpu.PrefetchScalarGridSpec(num_scalar_pr...  22.8 us
    pallas_call x1, Pallas kernels, input_grads(): pl.pallas_call(body, grid=(count * per_image,), in_specs=[block, whole_bl...  11.5 us
    ppermute x4, starting transfers between devices, swap_both(): lax.ppermute(value, ('img', 'row'), [(i, i ^ 6) for i in range(size)])  5.57 us
    ppermute x2, waiting for transfers between devices, send_down(): return lax.ppermute(value, 'img', [(i, i ^ distance) for i in senders])  5.5 us
  transfers between devices with their start and end apart: 43, of which 17 were waited for; matrix products, arithmetic and copies ran while one was open for 4% of the time, Pallas kernels for 27%

commit v1 on v0

--- a/solution.py
+++ b/solution.py
@@ -119,21 +119,17 @@
     return [along] + [hop for hop in outer if hop[0] == "img"]
 
 
-def gather_rows(own, shown):
-    width = own.shape[-1]
-    count = shown.shape[0]
+def gather_rows(own):
     held, masks = own[None], [0]
     for axis, distance, mask in row_hops():
-        got = swap(jnp.concatenate([held.reshape(-1, width), shown]), axis, distance)
-        held = jnp.concatenate([held, got[:-count].reshape(held.shape)])
-        shown = shown + got[-count:]
+        held = jnp.concatenate([held, swap(held, axis, distance)])
         masks = masks + [m ^ mask for m in masks]
     place = [0] * len(masks)
     for at, mask in enumerate(masks):
         place[mask] = at
     order = jnp.asarray(place, jnp.int32)[jnp.arange(len(masks)) ^ lax.axis_index("row")]
     held = jnp.moveaxis(jnp.take(held, order, axis=0, mode="clip"), 0, 1)
-    return held.reshape(own.shape[0], -1, width), shown
+    return held.reshape(own.shape[0], -1, own.shape[-1])
 
 
 def gather_weights(weights, model_width):
@@ -754,7 +750,6 @@
 
 
 def input_grad_kernel(
-    rows_per_step,
     block_ref,
     gain_ref,
     query_grad_ref,
@@ -762,72 +757,38 @@
     value_grad_ref,
     w_ref,
     middle_grad_ref,
-    mean_grad_ref,
     out_ref,
 ):
     width = block_ref.shape[1]
-    columns = block_ref.shape[0] // rows_per_step
-
     attn_grad = (
         dot_rows(query_grad_ref[...], w_ref[:, :width])
         + dot_rows(key_grad_ref[...], w_ref[:, width : 2 * width])
         + dot_rows(value_grad_ref[...], w_ref[:, 2 * width :])
     )
     normed, inverse = normalize(block_ref[...].astype(SINGLE))
-    total = middle_grad_ref[...] + norm_back(attn_grad * gain_ref[...], normed, inverse)
-    for row in range(rows_per_step):
-        tokens = slice(row * columns, (row + 1) * columns)
-        out_ref[tokens] = total[tokens] + mean_grad_ref[row : row + 1]
+    out_ref[...] = middle_grad_ref[...] + norm_back(attn_grad * gain_ref[...], normed, inverse)
 
 
 def input_grads(
-    group,
-    previous,
-    block_in,
-    gain,
-    query_grad,
-    key_grad,
-    value_grad,
-    w_qkv,
-    middle_grad,
-    mean_grad,
-    local_rows,
-    columns,
+    block_in, gain, query_grad, key_grad, value_grad, w_qkv, middle_grad, local_rows, columns
 ):
     tokens, width = block_in.shape
-    images = mean_grad.shape[0]
-    first_image, count = group
-    rows_per_step = math.gcd(local_rows, 2)
-    per_image = local_rows // rows_per_step
-    first_step = first_image * per_image
-    size = rows_per_step * columns
-    part = count * tokens // images
-    block = pl.BlockSpec((size, width), lambda i: (first_step + i, 0))
-    inputs = [block_in, gain, query_grad, key_grad, value_grad, w_qkv, middle_grad]
-    inputs = inputs + [mean_grad.reshape(tokens // size, rows_per_step, width)]
-    kept, kept_specs, aliases = kept_arrays(None if previous is None else [previous], len(inputs))
-    kernel = functools.partial(input_grad_kernel, rows_per_step)
-
-    def body(*refs):
-        kernel(*refs[: len(inputs)], *refs[len(inputs) + len(kept) :])
-
+    size = math.gcd(local_rows, 2) * columns
+    block = pl.BlockSpec((size, width), lambda i: (i, 0))
     return pl.pallas_call(
-        body,
-        grid=(count * per_image,),
+        input_grad_kernel,
+        grid=(tokens // size,),
         in_specs=[block, whole_block((1, width))]
         + [block] * 3
-        + [whole_block((width, 3 * width)), block]
-        + [pl.BlockSpec((None, rows_per_step, width), lambda i: (first_step + i, 0, 0))]
-        + kept_specs,
+        + [whole_block((width, 3 * width)), block],
         out_specs=block,
         out_shape=jax.ShapeDtypeStruct((tokens, width), SINGLE),
-        input_output_aliases=aliases,
         compiler_params=pltpu.CompilerParams(vmem_limit_bytes=VMEM_BYTES),
         cost_estimate=pl.CostEstimate(
-            flops=part * width * 6 * width, bytes_accessed=part * width * 16, transcendentals=0
+            flops=tokens * width * 6 * width, bytes_accessed=tokens * width * 16, transcendentals=0
         ),
         name="input_grads",
-    )(*inputs, *kept)
+    )(block_in, gain, query_grad, key_grad, value_grad, w_qkv, middle_grad)
 
 
 def assemble(flat_ref, pieces, index, block, count):
@@ -851,39 +812,108 @@
                 flat_ref[rows] = value
 
 
-def projection_weights_kernel(masks, block, index_ref, tail_ref, summary_ref, *refs):
-    *piece_refs, w_ref, key_far_ref, value_far_ref, flat_ref = refs
+def parts_of(value):
+    high = lax.reduce_precision(value, 8, 7)
+    middle = lax.reduce_precision(value - high, 8, 7)
+    low = value - high - middle
+    return [part.astype(HALF) for part in (high, middle, low)]
+
+
+def whole_of(parts):
+    rows = parts.shape[0] // 3
+    parts = parts.astype(SINGLE)
+    return (parts[:rows] + parts[rows : 2 * rows]) + parts[2 * rows :]
+
+
+def projection_weights_kernel(
+    masks,
+    block,
+    images,
+    local_rows,
+    summary_count,
+    index_ref,
+    *refs,
+):
+    piece_refs, refs = refs[: len(masks)], refs[len(masks) :]
+    w_ref, key_far_ref, value_far_ref, standard_ref, summary_ref, *refs = refs
+    *stat_refs, flat_ref, shown_ref, means_ref = refs
     width = flat_ref.shape[1]
-    pieces = [(ref, mask, first) for ref, (mask, first) in zip(piece_refs, masks)]
-    assemble(flat_ref, pieces, lax.rem(index_ref[0], 8), block, 1)
-    flat_ref[3 * width :] += tail_ref[...]
+    rows = block + TAIL
+    here = lax.rem(index_ref[0], 8)
+    assemble(
+        flat_ref, [(ref.at[:rows], mask, 0) for ref, mask in zip(piece_refs, masks)], here, block, 1
+    )
+    for ref, mask in zip(piece_refs, masks):
+        shown_ref[here ^ mask] = ref[rows:]
+    flat_ref[3 * width :] += shown_ref[0, :TAIL]
     for i in range(3):
         w_ref[:, i * width : (i + 1) * width] = flat_ref[TAIL + i * width : TAIL + (i + 1) * width]
-    key_far_ref[...] = dot(summary_ref[...], w_ref[:, width : 2 * width]).astype(HALF)
-    value_far_ref[...] = dot(summary_ref[...], w_ref[:, 2 * width :]).astype(HALF)
+    own_rows = images * local_rows
+    total = jnp.zeros((2, width), SINGLE)
+    for j in range(8):
+        total = total + whole_of(shown_ref[j, TAIL:])[own_rows : own_rows + 2]
+    for j in range(4):
+        means = whole_of(shown_ref[lax.div(here, 4) * 4 + j, TAIL:])
+        for image in range(images):
+            start = (image * 4 + j) * local_rows
+            means_ref[start : start + local_rows] = means[image * local_rows : (image + 1) * local_rows]
+    vectors = flat_ref[:TAIL].astype(SINGLE)[TAIL - 4 :]
+    mean = total[:1] / summary_count
+    variance = total[1:] / summary_count - mean * mean
+    inverse = lax.rsqrt(variance + EPS)
+    standard = (means_ref[...] - mean) * inverse
+    summary = (standard * vectors[1:2] + vectors[2:3]).astype(HALF)
+    standard_ref[...] = standard
+    summary_ref[...] = summary
+    vector_rows = [vectors[i : i + 1] for i in range(4)]
+    for ref, value in zip(stat_refs, [mean, variance, inverse] + vector_rows):
+        ref[...] = value
+    key_far_ref[...] = dot(summary, w_ref[:, width : 2 * width]).astype(HALF)
+    value_far_ref[...] = dot(summary, w_ref[:, 2 * width :]).astype(HALF)
 
 
 def vmem_specs(count):
     return [pl.BlockSpec(memory_space=pltpu.VMEM)] * count
 
 
-def projection_weights(index, tail, summary_low, pieces, block):
-    width = tail.shape[1]
-    arrays, masks = [p[0] for p in pieces], [p[1:] for p in pieces]
-    far = summary_low.shape[0]
+def projection_weights(index, pieces, block, images, local_rows, summary_count):
+    arrays, masks = [p[0] for p in pieces], [p[1] for p in pieces]
+    width = arrays[0].shape[1]
+    far = 4 * images * local_rows
     return pl.pallas_call(
-        functools.partial(projection_weights_kernel, masks, block),
-        in_specs=[pl.BlockSpec(memory_space=pltpu.SMEM)] + vmem_specs(2 + len(arrays)),
-        out_specs=vmem_specs(3),
+        functools.partial(
+            projection_weights_kernel, masks, block, images, local_rows, summary_count
+        ),
+        in_specs=[pl.BlockSpec(memory_space=pltpu.SMEM)] + vmem_specs(len(arrays)),
+        out_specs=vmem_specs(12),
         out_shape=[
             jax.ShapeDtypeStruct((width, 3 * width), HALF),
             jax.ShapeDtypeStruct((far, width), HALF),
             jax.ShapeDtypeStruct((far, width), HALF),
+            jax.ShapeDtypeStruct((far, width), SINGLE),
+            jax.ShapeDtypeStruct((far, width), HALF),
+        ]
+        + [jax.ShapeDtypeStruct((1, width), SINGLE)] * 7,
+        scratch_shapes=[
+            pltpu.VMEM((TAIL + 3 * width, width), HALF),
+            pltpu.VMEM((8, 4 * TAIL, width), HALF),
+            pltpu.VMEM((far, width), SINGLE),
         ],
-        scratch_shapes=[pltpu.VMEM((TAIL + 3 * width, width), HALF)],
         compiler_params=pltpu.CompilerParams(vmem_limit_bytes=VMEM_BYTES),
         name="projection_weights",
-    )(index, tail, summary_low, *arrays)
+    )(index, *arrays)
+
+
+def with_sums(value, small):
+    high = lax.reduce_precision(small[:8], 8, 7)
+    return jnp.concatenate(
+        [value, high.astype(HALF), (small[:8] - high).astype(HALF), small[8:].astype(HALF)]
+    )
+
+
+def sums_of(rows):
+    rows = rows.astype(SINGLE)
+    return jnp.concatenate([rows[:8] + rows[8:16], rows[16:]])
 
 
 def swap_core(value):
@@ -915,33 +945,10 @@
     return lax.ppermute(value, "img", [(i, i ^ 4) for i in range(lax.axis_size("img")) if i // 2 != 2])
 
 
-def send_down(value, distance):
-    size = lax.axis_size("img")
-    senders = [i for i in range(size) if i & distance and not i & (distance - 1) & ~1]
-    return lax.ppermute(value, "img", [(i, i ^ distance) for i in senders])
-
-
-def corners(over_x, over_y, split):
-    rows = over_x.ndim - 2
-    first = lax.slice_in_dim(over_x, 0, split, axis=rows)
-    second = lax.slice_in_dim(over_y, split, over_y.shape[rows], axis=rows)
-    return (swap_y(first), swap_x(second))
-
-
-def with_cores(value, over_x, over_y, corner_first, corner_second, split):
-    near = [(value, 0, 0), (over_x, 2, 0), (over_y, 4, 0), (corner_first, 6, 0), (corner_second, 6, split)]
-    return near + [(swap_core(array), mask | 1, first) for array, mask, first in near]
-
-
-def sum_planes(value):
-    far = lax.ppermute(value, "img", [(i, i ^ 6) for i in range(lax.axis_size("img"))])
-    return value + swap_near(value) + swap_far(value) + far
-
-
 def piece_plan(block, slots):
     plan, shapes = [], []
     rows = block + TAIL
-    for out, (side, masks) in enumerate(((0, (0,)), (0, (2, 4, 6)), (1, (0, 2, 4, 6)))):
+    for out, (side, masks) in enumerate(((0, (0,)), (0, (2,)), (0, (4,)), (0, (6,)), (1, (0, 2, 4, 6)))):
         shapes.append((len(masks), slots, rows))
         for place, mask in enumerate(masks):
             for slot in range(slots):
@@ -953,9 +960,18 @@
     return plan, shapes
 
 
-def sum_core(kept, sent, other):
-    other = swap_core(other).astype(SINGLE)
-    return (kept[0].astype(SINGLE) + other[0], (sent.astype(SINGLE) + other[1:]).astype(HALF))
+def sum_core(kept, over_x, over_y, over_both, other):
+    other = swap_core(other)
+    own = kept[0].astype(SINGLE) + other[0].astype(SINGLE)
+    sent = [
+        (piece[0].astype(SINGLE) + other[i + 1].astype(SINGLE)).astype(HALF)
+        for i, piece in enumerate((over_x, over_y, over_both))
+    ]
+    return (own, sent)
+
+
+def send_down(value):
+    return lax.ppermute(value, "img", [(i, i ^ 4) for i in range(lax.axis_size("img")) if i // 2 == 2])
 
 
 def across_plane(sent):
@@ -999,76 +1015,69 @@
     block_in = activations.reshape(tokens, width)
 
     row_means = jnp.mean(activations.astype(SINGLE), axis=2)
+    sums = jnp.stack([jnp.sum(row_means, axis=(0, 1)), jnp.sum(row_means * row_means, axis=(0, 1))])
     if planes:
         own, start = own_rows(weights, width)
-        shown = jnp.concatenate(
-            [
-                jnp.where(me == 0, own[TAIL - 4 : TAIL].astype(SINGLE), 0.0),
-                jnp.where(me == 8, own[:TAIL].astype(SINGLE), 0.0),
-            ]
+        piece_rows = block + TAIL
+        own = jnp.concatenate([own] + parts_of(sums) + [jnp.zeros((TAIL - 6, width), HALF)])
+        over_far = swap_far(own)
+        over_near = swap_near(jnp.stack([own, over_far]))
+        held = [own, over_near[0], over_far, over_near[1]]
+        sums = [whole_of(array[piece_rows : piece_rows + 6]) for array in held]
+        sums = (sums[0] + sums[1]) + (sums[2] + sums[3])
+        held = jnp.stack([array[:piece_rows] for array in held])
+        slots = [lax.dynamic_index_in_dim(held, z ^ i, 0, keepdims=False) for i in range(4)]
+        means = row_means.reshape(-1, width)
+        spare = jnp.zeros((TAIL - 2 - means.shape[0], width), SINGLE)
+        known = parts_of(jnp.concatenate([means, sums, spare]))
+        first_slot = jnp.concatenate([slots[0], slots[1][:TAIL]] + known)
+        other_slots = jnp.stack(slots[1:])
+        first_near = [swap_x(first_slot), swap_y(first_slot), swap_both(first_slot)]
+        first_near, other_slots = together(first_near, other_slots)
+        first_pieces = [(array, 2 * i) for i, array in enumerate([first_slot] + list(first_near))]
+        first_pieces += [(swap_core(array), mask | 1) for array, mask in first_pieces]
+        other_near = [swap_x(other_slots), swap_y(other_slots), swap_both(other_slots)]
+        w_qkv, key_far, value_far, standard, summary_low, *stats = projection_weights(
+            index, first_pieces, block, images, local_rows, summary_count
         )
+        summary_mean, summary_var, summary_inv = (row.reshape(width) for row in stats[:3])
+        gain_one, gain_sum, bias_sum, gain_two = stats[3:]
+        standard = standard.reshape(images, rows_all, width)
     else:
-        gathered, matrix_rows = gather_weights(weights, width)
-        shown = jnp.zeros((4 + TAIL, width), SINGLE)
-    all_means, shown = gather_rows(row_means, shown)
-    sums = jnp.stack([jnp.sum(all_means, axis=(0, 1)), jnp.sum(all_means * all_means, axis=(0, 1))])
-    sums = jnp.concatenate([sums, shown])
-    if planes:
-        over_far, sums = together(swap_far(own), sums)
-        over_near = swap_near(jnp.stack([own, over_far]))
-        over_near, sums = together(over_near, sum_planes(sums + swap_y(sums)))
-        held = jnp.stack([own, over_near[0], over_far, over_near[1]])
-        first_slot = lax.dynamic_index_in_dim(held, z, 0, keepdims=False)
-        first_near = [swap_x(first_slot), swap_y(first_slot), swap_both(first_slot)]
-        other_slots = jnp.stack(
-            [lax.dynamic_index_in_dim(held, z ^ i, 0, keepdims=False) for i in (1, 2, 3)]
+        vectors, matrix_rows = gather_weights(weights, width)
+        gain_one, gain_sum, bias_sum, gain_two = (
+            vectors[i : i + 1].astype(SINGLE) for i in range(4)
         )
-        first_near, other_slots, sums = together(first_near, other_slots, sums)
-        first_pieces = [(array, 2 * i, 0) for i, array in enumerate([first_slot] + list(first_near))]
-        first_pieces += [(swap_core(array), mask | 1, 0) for array, mask, _ in first_pieces]
-        other_x, other_y = swap_x(other_slots), swap_y(other_slots)
-    else:
-        for axis, distance, _ in image_hops():
+        all_means = gather_rows(row_means)
+        for axis, distance, _ in row_hops() + image_hops():
             sums = sums + swap(sums, axis, distance)
-    summary_mean = sums[0] / summary_count
-    summary_var = sums[1] / summary_count - summary_mean * summary_mean
-    summary_inv = lax.rsqrt(summary_var + EPS)
-    standard = (all_means - summary_mean) * summary_inv
-    vectors = sums[2:6] if planes else gathered.astype(SINGLE)
-    gain_one, gain_sum, bias_sum, gain_two = (vectors[i : i + 1] for i in range(4))
-    summary_low = (standard * gain_sum + bias_sum).astype(HALF).reshape(far, width)
-
-    if planes:
-        w_qkv, key_far, value_far = projection_weights(
-            index, sums[6:].astype(HALF), summary_low, first_pieces, block
-        )
-    else:
+        summary_mean = sums[0] / summary_count
+        summary_var = sums[1] / summary_count - summary_mean * summary_mean
+        summary_inv = lax.rsqrt(summary_var + EPS)
+        standard = (all_means - summary_mean) * summary_inv
+        summary_low = (standard * gain_sum + bias_sum).astype(HALF).reshape(far, width)
         w_qkv = jnp.concatenate([matrix_rows[i * width : (i + 1) * width] for i in range(3)], axis=1)
         key_far = dot(summary_low, w_qkv[:, width : 2 * width]).astype(HALF)
         value_far = dot(summary_low, w_qkv[:, 2 * width :]).astype(HALF)
     key_far = key_far.reshape(images, rows_all, width)
     value_far = value_far.reshape(images, rows_all, width)
 
-    forward = None
-    for group in image_groups(images):
-        forward = attention_forward(
-            group,
-            forward,
-            block_in,
-            gain_one,
-            w_qkv,
-            key_far,
-            value_far,
-            first_row[None],
-            local_rows,
-            columns,
-        )
-        if planes and group[0] == 0:
-            other_x, other_y, forward = together(other_x, other_y, forward)
-            other_corners = corners(other_x, other_y, split)
+    forward = attention_forward(
+        (0, images),
+        None,
+        block_in,
+        gain_one,
+        w_qkv,
+        key_far,
+        value_far,
+        first_row[None],
+        local_rows,
+        columns,
+    )
     if planes:
-        other_corners, forward = together(other_corners, forward)
-        given = with_cores(other_slots, other_x, other_y, *other_corners, split)
+        other_near, forward = together(other_near, forward)
+        given = [(array, 2 * i, 0) for i, array in enumerate([other_slots] + list(other_near))]
+        given += [(swap_core(array), mask | 1, 0) for array, mask, _ in given]
     query, key, value, mixed, probs = forward
 
     if planes:
@@ -1125,27 +1134,39 @@
         (late_kept, late_sent), shared, early = together(
             sum_core(*late), shared + swap_core(shared), sum_plane(early_kept, *early_in)
         )
+        small = shared[far:]
+        late_sent = [with_sums(sent[0], small) for sent in late_sent]
+        late_sent[0] = jnp.concatenate([late_sent[0], shared[:far].astype(HALF)])
         late_in = across_plane(late_sent)
         by_mask = [
             jnp.where(z == i, 0.0, lax.dynamic_index_in_dim(early, (z ^ i) - 1, 0, keepdims=False))
             for i in range(4)
         ]
         early_in = swap_near(jnp.stack([by_mask[1], by_mask[3]]).astype(HALF))
-        small = shared[far:]
-        over_x = swap_x(shared)
-        small = small + over_x[far:] + swap_y(small) + swap_both(small)
-        late_in, small, shared, early_in = together(
-            late_in, small, shared[:far] + over_x[:far], early_in
-        )
-        late = sum_plane(late_kept, *late_in)[0]
-        late = late + send_down(late.astype(HALF), 2).astype(SINGLE)
-        late, small = together(late, sum_planes(small))
+        late_in, early_in = together(late_in, early_in)
+        rows = late_kept.shape[1]
+        both = rows + small.shape[0] + 8
+        late = sum_plane(late_kept[0], *[array[:rows] for array in late_in])
+        over_x, over_y, over_both = (sums_of(array[rows:both]) for array in late_in)
+        shared = shared[:far] + late_in[0][both:].astype(SINGLE)
+        small = (small + over_x) + (over_y + over_both)
+        early_far = send_far((by_mask[2] + early_in[1].astype(SINGLE)).astype(HALF))
+        near_in = swap_near(with_sums(late.astype(HALF), small))
     else:
         for axis, distance, _ in row_hops():
             shared = shared + swap(shared, axis, distance)
         small = shared[far:]
         for axis, distance, _ in image_hops():
             small = small + swap(small, axis, distance)
+    input_grad = input_grads(
+        block_in, gain_one, query_grad, key_grad, value_grad, w_qkv, middle_grad, local_rows, columns
+    )
+    if planes:
+        near_in, early_far, input_grad = together(near_in, early_far, input_grad)
+        late = late + near_in[:rows].astype(SINGLE)
+        small = small + sums_of(near_in[rows:])
+        late_own = late + send_down(late.astype(HALF)).astype(SINGLE)
+        small = small + swap_far(small)
     own_grad = lax.dynamic_slice_in_dim(
         shared[:far].reshape(images, rows_all, width), first_row, local_rows, axis=1
     )
@@ -1153,25 +1174,8 @@
     mean_grad = summary_inv * (
         own_grad - small[0] / summary_count - own_standard * (small[1] / summary_count)
     )
-    input_grad = None
-    for group in [(0, images)]:
-        input_grad = input_grads(
-            group,
-            input_grad,
-            block_in,
-            gain_one,
-            query_grad,
-            key_grad,
-            value_grad,
-            w_qkv,
-            middle_grad,
-            mean_grad / columns,
-            local_rows,
-            columns,
-        )
+    input_grad = input_grad.reshape(activations.shape) + (mean_grad / columns)[:, :, None, :]
     if planes:
-        late_own = late + send_down(late.astype(HALF), 4).astype(SINGLE)
-        early_far = send_far((by_mask[2] + early_in[1].astype(SINGLE)).astype(HALF))
         early_own = by_mask[0] + early_in[0].astype(SINGLE) + early_far.astype(SINGLE)
         head = jnp.where(
             me == 0,
@@ -1186,7 +1190,7 @@
         weight_grad = scatter_grads(small[2:6], grad_rows, weights.shape[0])
     return (
         out.reshape(activations.shape),
-        input_grad.reshape(activations.shape),
+        input_grad,
         weight_grad,
         summary_mean,
         summary_var,

time: 229 us -> 218 us (0.952)
  starting transfers between devices: 44.2 us -> 34.3 us
  local copies, waits for them, and re-layouts: 12.7 us -> 7.31 us
  waiting for transfers between devices: 49.2 us -> 53.1 us
  other arithmetic: 10.7 us -> 14 us
  Pallas kernels: 110 us -> 107 us
    ppermute x34 -> x24, waiting for transfers between devices: 35.1 us -> 44.5 us  [swap(): return lax.ppermute(value, axis, [(i, i ^ distance) for i in range(size)])]
    ppermute x34 -> x24, starting transfers between devices: 30.7 us -> 22.7 us  [swap(): return lax.ppermute(value, axis, [(i, i ^ distance) for i in range(size)])]
    ppermute x4 -> x1, waiting for transfers between devices: 9.41 us -> 3.63 us  [send_down(): lax.ppermute(value, 'img', [(i, i ^ 4) for i in range(lax.axis_size('img'...]
    ppermute x4 -> x1, starting transfers between devices: 6.05 us -> 1.29 us  [send_down(): lax.ppermute(value, 'img', [(i, i ^ 4) for i in range(lax.axis_size('img'...]
    ppermute x1, starting transfers between devices: 1.85 us -> 5.73 us  [send_far(): lax.ppermute(value, 'img', [(i, i ^ 4) for i in range(lax.axis_size('img'...]
    ppermute x1, waiting for transfers between devices: 0.01 us -> 3.31 us  [send_far(): lax.ppermute(value, 'img', [(i, i ^ 4) for i in range(lax.axis_size('img'...]
    ppermute x4, waiting for transfers between devices: 4.69 us -> 1.63 us  [swap_both(): lax.ppermute(value, ('img', 'row'), [(i, i ^ 6) for i in range(size)])]
    pallas_call x2 -> x1, Pallas kernels: 22.8 us -> 20 us  [attention_forward(): pl.pallas_call(body, grid_spec=pltpu.PrefetchScalarGridSpec(num_scalar_pr...]
  transfers between devices with their start and end apart: 43 -> 30, of which waited for: 17 -> 15; matrix products, arithmetic and copies ran while one was open for 4% -> 4% of each run, Pallas kernels for 27% -> 27%
where the time goes in v1:
time: 218 us; the launch traced here: 217 us
  Pallas kernels  107 us (49%)
  waiting for transfers between devices  53.1 us (24%)
  starting transfers between devices  34.3 us (16%)
  other arithmetic  14 us (6%)
  local copies, waits for them, and re-layouts  7.31 us (3%)
    pallas_call x1, Pallas kernels, feed_forward(): pl.pallas_call(functools.partial(feed_forward_kernel, 512, plan, masks, b...  48.5 us
    ppermute x24, waiting for transfers between devices, swap(): return lax.ppermute(value, axis, [(i, i ^ distance) for i in range(size)])  44.5 us
    pallas_call x1, Pallas kernels, attention_backward(): pl.pallas_call(functools.partial(attention_backward_kernel, 1.0 / math.sq...  23.6 us
    ppermute x24, starting transfers between devices, swap(): return lax.ppermute(value, axis, [(i, i ^ distance) for i in range(size)])  22.7 us
    pallas_call x1, Pallas kernels, attention_forward(): pl.pallas_call(body, grid_spec=pltpu.PrefetchScalarGridSpec(num_scalar_pr...  20 us
    pallas_call x1, Pallas kernels, input_grads(): pl.pallas_call(input_grad_kernel, grid=(tokens // size,), in_specs=[block...  11.4 us
    ppermute x1, starting transfers between devices, send_far(): lax.ppermute(value, 'img', [(i, i ^ 4) for i in range(lax.axis_size('img'...  5.73 us
    ppermute x4, starting transfers between devices, swap_both(): lax.ppermute(value, ('img', 'row'), [(i, i ^ 6) for i in range(size)])  4.62 us
  transfers between devices with their start and end apart: 30, of which 15 were waited for; matrix products, arithmetic and copies ran while one was open for 4% of the time, Pallas kernels for 27%

profile of v1, /device:TPU:0, one launch (start us, length us, event | category | flops | bytes accessed | tf_op | source)
XLA Modules:
  0.0 216.8 jit_solution(4015097784007538614)
XLA Ops:
  0.7 3.8 %dynamic_update_slice.3 = bf16[106496]{0:T(1024)(128)(2,1)S(1)} dynamic-update-slice(bf16[106496]{0:T(1024)(128)(2,1)S(1)} %broadcast_in_dim.41, bf16[98368]{0:T(1024)(128)(2,1)} %param.5, s32[]{:T(128)S(6)} %select_n.97) | dynamic-update-slice | bytes 393476 | tf_op jit(solution)/shard_map/dynamic_update_slice | solution.py:997
  4.6 2.0 convert_reduce_fusion
  7.0 4.1 %collective-permute-start = (bf16[224,512]{1,0:T(8,128)(2,1)S(1)}, bf16[224,512]{1,0:T(8,128)(2,1)S(1)}, u32[]{:S(2)}, u32[]{:S(2)}) collective-permute-start(bf16[224,512]{1,0:T(8,128)(2,1)S(1)} %concatenate.42), channel_id=1, source_target_pairs={{0,16},{4,20},{8,24},{12,28},{16,0},{20,4},{24,8},{28,12},{1,17},{... | collective-permute-start | bytes 688136 | tf_op jit(solution)/shard_map/ppermute | solution.py:27
  11.3 10.3 %collective-permute-done = bf16[224,512]{1,0:T(8,128)(2,1)S(1)} collective-permute-done((bf16[224,512]{1,0:T(8,128)(2,1)S(1)}, bf16[224,512]{1,0:T(8,128)(2,1)S(1)}, u32[]{:S(2)}, u32[]{:S(2)}) %collective-permute-start) | collective-permute-done | bytes 229408 | tf_op jit(solution)/shard_map/ppermute | solution.py:27
  22.4 11.0 %collective-permute-done.1 = bf16[2,224,512]{2,1,0:T(8,128)(2,1)S(1)} collective-permute-done((bf16[2,224,512]{2,1,0:T(8,128)(2,1)S(1)}, bf16[2,224,512]{2,1,0:T(8,128)(2,1)S(1)}, u32[]{:S(2)}, u32[]{:S(2)}) %collective-permute-start.1) | collective-permute-done | bytes 458784 | tf_op jit(solution)/shard_map/ppermute | solution.py:27
  33.9 1.3 collective-permute-start.2
  35.2 1.5 collective-permute-start.3
  37.6 6.0 %collective-permute-done.2.refs_1_ = bf16[272,512]{1,0:T(8,128)(2,1)S(1)} collective-permute-done((bf16[272,512]{1,0:T(8,128)(2,1)S(1)}, bf16[272,512]{1,0:T(8,128)(2,1)S(1)}, u32[]{:S(2)}, u32[]{:S(2)}) %collective-permute-start.2) | collective-permute-done | bytes 278560 | tf_op jit(solution)/shard_map/ppermute | solution.py:27
  43.6 4.3 %collective-permute-done.3.refs_2_ = bf16[272,512]{1,0:T(8,128)(2,1)S(1)} collective-permute-done((bf16[272,512]{1,0:T(8,128)(2,1)S(1)}, bf16[272,512]{1,0:T(8,128)(2,1)S(1)}, u32[]{:S(2)}, u32[]{:S(2)}) %collective-permute-start.3) | collective-permute-done | bytes 278560 | tf_op jit(solution)/shard_map/ppermute | solution.py:27
  50.6 1.4 collective-permute-start.7
  53.5 3.3 %projection_weights.1 = (bf16[512,1536]{1,0:T(8,128)(2,1)}, bf16[48,512]{1,0:T(8,128)(2,1)}, bf16[48,512]{1,0:T(8,128)(2,1)}, f32[48,512]{1,0:T(8,128)}, bf16[48...) custom-call(s32[1]{0:T(128)} %bitcast.index_ref, ...), custom_call_target="tpu_custom_call" | custom-call | tf_op jit(solution)/shard_map/projection_weights/pallas_call | solution.py:883
  56.8 20.0 %attention_forward.1 = (bf16[2304,512]{1,0:T(8,128)(2,1)}, bf16[2304,512]{1,0:T(8,128)(2,1)}, bf16[2304,512]{1,0:T(8,128)(2,1)}, bf16[2304,512]{1,0:T(8,128)(2,1)}, bf16[12,8,208,192]{3,2,1,0:T(8,128)(2,1)}) custom-call(s32[1]{0:T(128)} %bitcast.11.refs_0_, bf16[2304,512]{1,0:T(8,128)(2,1)} %bitcast.74, f32[1,512]{1,0:T(1,128)} %get-tuple-element.73.refs_2_.rest_0_.gain_ref, ...), custom_call_target="tpu_custom_call" | custom-call | flops 5586812928 | bytes 21823488 | tf_op jit(solution)/shard_map/attention_forward/pallas_call | solution.py:321
  76.8 1.4 collective-permute-done.6.rest_2_
  78.3 1.6 collective-permute-done.7.rest_3_
  80.4 1.6 collective-permute-done.13.rest_5_
  84.6 48.5 %feed_forward.1 = (bf16[2304,512]{1,0:T(8,128)(2,1)}, f32[2304,512]{1,0:T(8,128)}, bf16[2304,512]{1,0:T(8,128)(2,1)}, f32[1,512]{1,0:T(1,128)}, bf16[1,3,208,512...) custom-call(s32[1]{0:T(128)} %bitcast.index_ref, ...), custom_call_target="tpu_custom_call" | custom-call | flops 32614907904 | bytes 24903680 | tf_op jit(solution)/shard_map/feed_forward/pallas_call | solution.py:490
  133.3 4.9 %collective-permute-done.16 = bf16[4,3,208,512]{3,2,1,0:T(8,128)(2,1)S(1)} collective-permute-done((bf16[4,3,208,512]{3,2,1,0:T(8,128)(2,1)}, bf16[4,3,208,512]{3,2,1,0:T(8,128)(2,1)S(1)}, u32[]{:S(2)}, u32[]{:S(2)}) %collective-permute-start.16) | collective-permute-done | bytes 2555936 | tf_op jit(solution)/shard_map/ppermute | solution.py:27
  138.2 3.2 %fusion.2 = (bf16[3,208,512]{2,1,0:T(8,128)(2,1)S(1)}, bf16[3,208,512]{2,1,0:T(8,128)(2,1)S(1)}, bf16[3,208,512]{2,1,0:T(8,128)(2,1)}, f32[3,208,512]{2,1,0:T(8,128)S(1)}) fusion(bf16[1,3,208,512]{3,2,1,0:T(8,128)(2,1)} %get-tuple-element.96, bf16[4,3,208,512]{3,2,1,0:T(8,128)(2,1)S(1)} %collective-permute-done.16, ...), kind=kLoop, calls=%fused_computation.10 | loop fusion | flops 4792320 | bytes 8306688 | tf_op jit(solution)/shard_map/convert_element_type | solution.py:967
  142.3 1.5 collective-permute-start.20
  144.9 23.6 %attention_backward.1 = (bf16[2304,512]{1,0:T(8,128)(2,1)}, bf16[2304,512]{1,0:T(8,128)(2,1)}, bf16[2304,512]{1,0:T(8,128)(2,1)}, f32[72,512]{1,0:T(8,128)}, bf1...) custom-call(s32[1]{0:T(128)} %bitcast.index_ref, ...), custom_call_target="tpu_custom_call" | custom-call | flops 7549747200 | bytes 26542080 | tf_op jit(solution)/shard_map/attention_backward/pallas_call | solution.py:723
  169.1 2.3 %collective-permute-done.18 = f32[72,512]{1,0:T(8,128)S(1)} collective-permute-done((f32[72,512]{1,0:T(8,128)}, f32[72,512]{1,0:T(8,128)S(1)}, u32[]{:S(2)}, u32[]{:S(2)}) %collective-permute-start.18) | collective-permute-done | bytes 147488 | tf_op jit(solution)/shard_map/ppermute | solution.py:27
  172.4 1.9 add_add_fusion
  174.7 2.5 %collective-permute-start.25 = (bf16[2,208,512]{2,1,0:T(8,128)(2,1)S(1)}, bf16[2,208,512]{2,1,0:T(8,128)(2,1)S(1)}, u32[]{:S(2)}, u32[]{:S(2)}) collective-permute-start(bf16[2,208,512]{2,1,0:T(8,128)(2,1)S(1)} %pad_maximum_fusion.3), channel_id=1, source_target_pairs={{0,8},{4,12},{8,0},{12,4},{16,24},{20,28},{24,16},{28,20},{1,9},{5... | collective-permute-start | bytes 1277960 | tf_op jit(solution)/shard_map/ppermute | solution.py:27
  177.4 1.4 collective-permute-start.23
  178.7 1.4 collective-permute-start.24
  181.0 11.4 %input_grads.1 = f32[2304,512]{1,0:T(8,128)} custom-call(bf16[2304,512]{1,0:T(8,128)(2,1)} %bitcast.77, f32[1,512]{1,0:T(1,128)} %get-tuple-element.73.refs_2_.rest_0_.gain_ref, bf16[2304,512]{1,0:T(8,128)(2,1)} %get-tuple-element.123.query_grad_ref, bf16[2304,512]{1,0:T(8,128)(2,1)} %get-tuple-element.124.key_grad_ref, ...), custom_call_target="tpu_custom_call" | custom-call | flops 3623878656 | bytes 18874368 | tf_op jit(solution)/shard_map/input_grads/pallas_call | solution.py:778
  193.5 5.7 %collective-permute-start.27 = (bf16[208,512]{1,0:T(8,128)(2,1)S(1)}, bf16[208,512]{1,0:T(8,128)(2,1)S(1)}, u32[]{:S(2)}, u32[]{:S(2)}) collective-permute-start(bf16[208,512]{1,0:T(8,128)(2,1)S(1)} %fusion.9), channel_id=1, source_target_pairs={{0,16},{4,20},{8,24},{12,28},{24,8},{28,12},{1,17},{5,21},{9,25},{... | collective-permute-start | bytes 638984 | tf_op jit(solution)/shard_map/ppermute | solution.py:945
  199.2 3.3 %collective-permute-done.27 = bf16[208,512]{1,0:T(8,128)(2,1)S(1)} collective-permute-done((bf16[208,512]{1,0:T(8,128)(2,1)S(1)}, bf16[208,512]{1,0:T(8,128)(2,1)S(1)}, u32[]{:S(2)}, u32[]{:S(2)}) %collective-permute-start.27) | collective-permute-done | bytes 213024 | tf_op jit(solution)/shard_map/ppermute | solution.py:945
  202.6 3.5 %collective-permute-start.28 = (f32[24,512]{1,0:T(8,128)S(1)}, f32[24,512]{1,0:T(8,128)S(1)}, u32[]{:S(2)}, u32[]{:S(2)}) collective-permute-start(f32[24,512]{1,0:T(8,128)S(1)} %maximum_add_fusion.2), channel_id=1, source_target_pairs={{0,16},{4,20},{8,24},{12,28},{16,0},{20,4},{24,8},{28,12},{1,17},{... | collective-permute-start | bytes 147464 | tf_op jit(solution)/shard_map/ppermute | solution.py:27
  206.1 1.3 collective-permute-start.29
  209.0 2.8 %broadcast_add_fusion = f32[3,4,192,512]{3,2,1,0:T(8,128)} fusion(f32[3,4,192,512]{3,2,1,0:T(8,128)S(1)} %bitcast.73, f32[3,4,512]{2,1,0:T(4,128)S(1)} %multiply_multiply_fusion), kind=kLoop, calls=%fused_computation.1 | loop fusion | flops 1179648 | bytes 9461760 | tf_op jit(solution)/shard_map/add | solution.py:1177
  211.8 3.6 %collective-permute-done.29 = bf16[208,512]{1,0:T(8,128)(2,1)S(1)} collective-permute-done((bf16[208,512]{1,0:T(8,128)(2,1)S(1)}, bf16[208,512]{1,0:T(8,128)(2,1)S(1)}, u32[]{:S(2)}, u32[]{:S(2)}) %collective-permute-start.29) | collective-permute-done | bytes 213024 | tf_op jit(solution)/shard_map/ppermute | solution.py:974
  (147 shorter events, 19.0 us)
Async XLA Ops:
  7.0 14.6 %collective-permute-start = (bf16[224,512]{1,0:T(8,128)(2,1)S(1)}, bf16[224,512]{1,0:T(8,128)(2,1)S(1)}, u32[]{:S(2)}, u32[]{:S(2)}) collective-permute-start(bf16[224,512]{1,0:T(8,128)(2,1)S(1)} %concatenate.42), channel_id=1, source_target_pairs={{0,16},{4,20},{8,24},{12,28},{16,0},{20,4},{24,8},{28,12},{1,17},{... | collective-permute-start | bytes 688136 | tf_op jit(solution)/shard_map/ppermute | solution.py:27
  21.6 11.8 %collective-permute-start.1 = (bf16[2,224,512]{2,1,0:T(8,128)(2,1)S(1)}, bf16[2,224,512]{2,1,0:T(8,128)(2,1)S(1)}, u32[]{:S(2)}, u32[]{:S(2)}) collective-permute-start(bf16[2,224,512]{2,1,0:T(8,128)(2,1)S(1)} %pad_maximum_fusion.2), channel_id=1, source_target_pairs={{0,8},{4,12},{8,0},{12,4},{16,24},{20,28},{24,16},{28,20},{1,9},{5... | collective-permute-start | bytes 1376264 | tf_op jit(solution)/shard_map/ppermute | solution.py:27
  33.9 18.8 %copy-start.1 = (bf16[272,512]{1,0:T(8,128)(2,1)}, bf16[272,512]{1,0:T(8,128)(2,1)S(1)}, u32[]{:S(2)}) copy-start(bf16[272,512]{1,0:T(8,128)(2,1)S(1)} %constant_dynamic-update-slice_fusion.refs_0_) | copy-start | bytes 835588
  33.9 9.7 %collective-permute-start.2 = (bf16[272,512]{1,0:T(8,128)(2,1)S(1)}, bf16[272,512]{1,0:T(8,128)(2,1)S(1)}, u32[]{:S(2)}, u32[]{:S(2)}) collective-permute-start(bf16[272,512]{1,0:T(8,128)(2,1)S(1)} %constant_dynamic-update-slice_fusion.refs_0_), channel_id=1, source_target_pairs={{0,2},{1,3},{2,0},{3,1},{4,6},{5,7},{6,4},{7,5},{8,10},{9,11},{10,... | collective-permute-start | bytes 835592 | tf_op jit(solution)/shard_map/ppermute | solution.py:27
  35.2 12.6 %collective-permute-start.3 = (bf16[272,512]{1,0:T(8,128)(2,1)S(1)}, bf16[272,512]{1,0:T(8,128)(2,1)S(1)}, u32[]{:S(2)}, u32[]{:S(2)}) collective-permute-start(bf16[272,512]{1,0:T(8,128)(2,1)S(1)} %constant_dynamic-update-slice_fusion.refs_0_), channel_id=1, source_target_pairs={{0,4},{4,0},{8,12},{12,8},{16,20},{20,16},{24,28},{28,24},{1,5},{5... | collective-permute-start | bytes 835592 | tf_op jit(solution)/shard_map/ppermute | solution.py:27
  36.8 11.1 %collective-permute-start.4 = (bf16[272,512]{1,0:T(8,128)(2,1)S(1)}, bf16[272,512]{1,0:T(8,128)(2,1)S(1)}, u32[]{:S(2)}, u32[]{:S(2)}) collective-permute-start(bf16[272,512]{1,0:T(8,128)(2,1)S(1)} %constant_dynamic-update-slice_fusion.refs_0_), channel_id=1, source_target_pairs={{0,6},{1,7},{2,4},{3,5},{4,2},{5,3},{6,0},{7,1},{8,14},{9,15},{10,... | collective-permute-start | bytes 835592 | tf_op jit(solution)/shard_map/ppermute | solution.py:933
  37.4 12.2 %collective-permute-start.8 = (bf16[272,512]{1,0:T(8,128)(2,1)S(1)}, bf16[272,512]{1,0:T(8,128)(2,1)S(1)}, u32[]{:S(2)}, u32[]{:S(2)}) collective-permute-start(bf16[272,512]{1,0:T(8,128)(2,1)S(1)} %constant_dynamic-update-slice_fusion.refs_0_), channel_id=1, source_target_pairs={{0,1},{1,0},{2,3},{3,2},{4,5},{5,4},{6,7},{7,6},{8,9},{9,8},{10,11... | collective-permute-start | bytes 835592 | tf_op jit(solution)/shard_map/ppermute | solution.py:27
  37.6 39.2 %copy-start.2 = (bf16[3,208,512]{2,1,0:T(8,128)(2,1)}, bf16[3,208,512]{2,1,0:T(8,128)(2,1)S(1)}, u32[]{:S(2)}) copy-start(bf16[3,208,512]{2,1,0:T(8,128)(2,1)S(1)} %pad_maximum_fusion.1.rest_0_) | copy-start | bytes 1916932
  47.9 2.7 %collective-permute-start.10 = (bf16[272,512]{1,0:T(8,128)(2,1)S(1)}, bf16[272,512]{1,0:T(8,128)(2,1)S(1)}, u32[]{:S(2)}, u32[]{:S(2)}) collective-permute-start(bf16[272,512]{1,0:T(8,128)(2,1)S(1)} %collective-permute-done.3.refs_2_), channel_id=1, source_target_pairs={{0,1},{1,0},{2,3},{3,2},{4,5},{5,4},{6,7},{7,6},{8,9},{9,8},{10,11... | collective-permute-start | bytes 835592 | tf_op jit(solution)/shard_map/ppermute | solution.py:27
  47.9 4.8 %collective-permute-start.11 = (bf16[272,512]{1,0:T(8,128)(2,1)S(1)}, bf16[272,512]{1,0:T(8,128)(2,1)S(1)}, u32[]{:S(2)}, u32[]{:S(2)}) collective-permute-start(bf16[272,512]{1,0:T(8,128)(2,1)S(1)} %collective-permute-done.4.refs_3_), channel_id=1, source_target_pairs={{0,1},{1,0},{2,3},{3,2},{4,5},{5,4},{6,7},{7,6},{8,9},{9,8},{10,11... | collective-permute-start | bytes 835592 | tf_op jit(solution)/shard_map/ppermute | solution.py:27
  48.4 4.3 %collective-permute-start.9 = (bf16[272,512]{1,0:T(8,128)(2,1)S(1)}, bf16[272,512]{1,0:T(8,128)(2,1)S(1)}, u32[]{:S(2)}, u32[]{:S(2)}) collective-permute-start(bf16[272,512]{1,0:T(8,128)(2,1)S(1)} %collective-permute-done.2.refs_1_), channel_id=1, source_target_pairs={{0,1},{1,0},{2,3},{3,2},{4,5},{5,4},{6,7},{7,6},{8,9},{9,8},{10,11... | collective-permute-start | bytes 835592 | tf_op jit(solution)/shard_map/ppermute | solution.py:27
  48.5 28.3 %collective-permute-start.5 = (bf16[3,208,512]{2,1,0:T(8,128)(2,1)S(1)}, bf16[3,208,512]{2,1,0:T(8,128)(2,1)S(1)}, u32[]{:S(2)}, u32[]{:S(2)}) collective-permute-start(bf16[3,208,512]{2,1,0:T(8,128)(2,1)S(1)} %pad_maximum_fusion.1.rest_0_), channel_id=1, source_target_pairs={{0,2},{1,3},{2,0},{3,1},{4,6},{5,7},{6,4},{7,5},{8,10},{9,11},{10,... | collective-permute-start | bytes 1916936 | tf_op jit(solution)/shard_map/ppermute | solution.py:27
  49.6 28.7 %collective-permute-start.6 = (bf16[3,208,512]{2,1,0:T(8,128)(2,1)S(1)}, bf16[3,208,512]{2,1,0:T(8,128)(2,1)S(1)}, u32[]{:S(2)}, u32[]{:S(2)}) collective-permute-start(bf16[3,208,512]{2,1,0:T(8,128)(2,1)S(1)} %pad_maximum_fusion.1.rest_0_), channel_id=1, source_target_pairs={{0,4},{4,0},{8,12},{12,8},{16,20},{20,16},{24,28},{28,24},{1,5},{5... | collective-permute-start | bytes 1916936 | tf_op jit(solution)/shard_map/ppermute | solution.py:27
  50.6 29.3 %collective-permute-start.7 = (bf16[3,208,512]{2,1,0:T(8,128)(2,1)S(1)}, bf16[3,208,512]{2,1,0:T(8,128)(2,1)S(1)}, u32[]{:S(2)}, u32[]{:S(2)}) collective-permute-start(bf16[3,208,512]{2,1,0:T(8,128)(2,1)S(1)} %pad_maximum_fusion.1.rest_0_), channel_id=1, source_target_pairs={{0,6},{1,7},{2,4},{3,5},{4,2},{5,3},{6,0},{7,1},{8,14},{9,15},{10,... | collective-permute-start | bytes 1916936 | tf_op jit(solution)/shard_map/ppermute | solution.py:933
  52.7 27.7 %collective-permute-start.12 = (bf16[3,208,512]{2,1,0:T(8,128)(2,1)S(1)}, bf16[3,208,512]{2,1,0:T(8,128)(2,1)S(1)}, u32[]{:S(2)}, u32[]{:S(2)}) collective-permute-start(bf16[3,208,512]{2,1,0:T(8,128)(2,1)S(1)} %pad_maximum_fusion.1.rest_0_), channel_id=1, source_target_pairs={{0,1},{1,0},{2,3},{3,2},{4,5},{5,4},{6,7},{7,6},{8,9},{9,8},{10,11... | collective-permute-start | bytes 1916936 | tf_op jit(solution)/shard_map/ppermute | solution.py:27
  79.9 2.1 collective-permute-start.13
  79.9 3.0 %collective-permute-start.14 = (bf16[3,208,512]{2,1,0:T(8,128)(2,1)S(1)}, bf16[3,208,512]{2,1,0:T(8,128)(2,1)S(1)}, u32[]{:S(2)}, u32[]{:S(2)}) collective-permute-start(bf16[3,208,512]{2,1,0:T(8,128)(2,1)S(1)} %collective-permute-done.6.rest_2_), channel_id=1, source_target_pairs={{0,1},{1,0},{2,3},{3,2},{4,5},{5,4},{6,7},{7,6},{8,9},{9,8},{10,11... | collective-permute-start | bytes 1916936 | tf_op jit(solution)/shard_map/ppermute | solution.py:27
  80.4 3.4 %collective-permute-start.15 = (bf16[3,208,512]{2,1,0:T(8,128)(2,1)S(1)}, bf16[3,208,512]{2,1,0:T(8,128)(2,1)S(1)}, u32[]{:S(2)}, u32[]{:S(2)}) collective-permute-start(bf16[3,208,512]{2,1,0:T(8,128)(2,1)S(1)} %collective-permute-done.7.rest_3_), channel_id=1, source_target_pairs={{0,1},{1,0},{2,3},{3,2},{4,5},{5,4},{6,7},{7,6},{8,9},{9,8},{10,11... | collective-permute-start | bytes 1916936 | tf_op jit(solution)/shard_map/ppermute | solution.py:27
  133.1 5.1 %collective-permute-start.16 = (bf16[4,3,208,512]{3,2,1,0:T(8,128)(2,1)}, bf16[4,3,208,512]{3,2,1,0:T(8,128)(2,1)S(1)}, u32[]{:S(2)}, u32[]{:S(2)}) collective-permute-start(bf16[4,3,208,512]{3,2,1,0:T(8,128)(2,1)} %get-tuple-element.93), channel_id=1, source_target_pairs={{0,1},{1,0},{2,3},{3,2},{4,5},{5,4},{6,7},{7,6},{8,9},{9,8},{10,11... | collective-permute-start | bytes 7667720 | tf_op jit(solution)/shard_map/ppermute | solution.py:27
  141.4 30.9 %collective-permute-start.19 = (bf16[3,208,512]{2,1,0:T(8,128)(2,1)}, bf16[3,208,512]{2,1,0:T(8,128)(2,1)}, u32[]{:S(2)}, u32[]{:S(2)}) collective-permute-start(bf16[3,208,512]{2,1,0:T(8,128)(2,1)} %get-tuple-element.110), channel_id=1, source_target_pairs={{0,2},{1,3},{2,0},{3,1},{4,6},{5,7},{6,4},{7,5},{8,10},{9,11},{10,... | collective-permute-start | bytes 1916936 | tf_op jit(solution)/shard_map/ppermute | solution.py:27
  142.3 30.0 %collective-permute-start.20 = (bf16[3,208,512]{2,1,0:T(8,128)(2,1)S(1)}, bf16[3,208,512]{2,1,0:T(8,128)(2,1)}, u32[]{:S(2)}, u32[]{:S(2)}) collective-permute-start(bf16[3,208,512]{2,1,0:T(8,128)(2,1)S(1)} %get-tuple-element.111), channel_id=1, source_target_pairs={{0,4},{4,0},{8,12},{12,8},{16,20},{20,16},{24,28},{28,24},{1,5},{5... | collective-permute-start | bytes 1916936 | tf_op jit(solution)/shard_map/ppermute | solution.py:27
  143.8 28.6 %collective-permute-start.21 = (bf16[3,208,512]{2,1,0:T(8,128)(2,1)S(1)}, bf16[3,208,512]{2,1,0:T(8,128)(2,1)}, u32[]{:S(2)}, u32[]{:S(2)}) collective-permute-start(bf16[3,208,512]{2,1,0:T(8,128)(2,1)S(1)} %get-tuple-element.112), channel_id=1, source_target_pairs={{0,6},{1,7},{2,4},{3,5},{4,2},{5,3},{6,0},{7,1},{8,14},{9,15},{10,... | collective-permute-start | bytes 1916936 | tf_op jit(solution)/shard_map/ppermute | solution.py:933
  168.5 5.8 %collective-permute-start.17 = (bf16[4,1,208,512]{3,2,1,0:T(8,128)(2,1)}, bf16[4,1,208,512]{3,2,1,0:T(8,128)(2,1)S(1)}, u32[]{:S(2)}, u32[]{:S(2)}) collective-permute-start(bf16[4,1,208,512]{3,2,1,0:T(8,128)(2,1)} %get-tuple-element.104), channel_id=1, source_target_pairs={{0,1},{1,0},{2,3},{3,2},{4,5},{5,4},{6,7},{7,6},{8,9},{9,8},{10,11... | collective-permute-start | bytes 2555912 | tf_op jit(solution)/shard_map/ppermute | solution.py:27
  168.6 2.8 %collective-permute-start.18 = (f32[72,512]{1,0:T(8,128)}, f32[72,512]{1,0:T(8,128)S(1)}, u32[]{:S(2)}, u32[]{:S(2)}) collective-permute-start(f32[72,512]{1,0:T(8,128)} %get-tuple-element.108), channel_id=1, source_target_pairs={{0,1},{1,0},{2,3},{3,2},{4,5},{5,4},{6,7},{7,6},{8,9},{9,8},{10,11... | collective-permute-start | bytes 442376 | tf_op jit(solution)/shard_map/ppermute | solution.py:27
  174.7 18.0 %collective-permute-start.25 = (bf16[2,208,512]{2,1,0:T(8,128)(2,1)S(1)}, bf16[2,208,512]{2,1,0:T(8,128)(2,1)S(1)}, u32[]{:S(2)}, u32[]{:S(2)}) collective-permute-start(bf16[2,208,512]{2,1,0:T(8,128)(2,1)S(1)} %pad_maximum_fusion.3), channel_id=1, source_target_pairs={{0,8},{4,12},{8,0},{12,4},{16,24},{20,28},{24,16},{28,20},{1,9},{5... | collective-permute-start | bytes 1277960 | tf_op jit(solution)/shard_map/ppermute | solution.py:27
  177.4 15.0 %collective-permute-start.23 = (bf16[240,512]{1,0:T(8,128)(2,1)S(1)}, bf16[240,512]{1,0:T(8,128)(2,1)S(1)}, u32[]{:S(2)}, u32[]{:S(2)}) collective-permute-start(bf16[240,512]{1,0:T(8,128)(2,1)S(1)} %get-tuple-element.165), channel_id=1, source_target_pairs={{0,4},{4,0},{8,12},{12,8},{16,20},{20,16},{24,28},{28,24},{1,5},{5... | collective-permute-start | bytes 737288 | tf_op jit(solution)/shard_map/ppermute | solution.py:27
  178.7 13.7 %collective-permute-start.24 = (bf16[240,512]{1,0:T(8,128)(2,1)S(1)}, bf16[240,512]{1,0:T(8,128)(2,1)S(1)}, u32[]{:S(2)}, u32[]{:S(2)}) collective-permute-start(bf16[240,512]{1,0:T(8,128)(2,1)S(1)} %get-tuple-element.164), channel_id=1, source_target_pairs={{0,6},{1,7},{2,4},{3,5},{4,2},{5,3},{6,0},{7,1},{8,14},{9,15},{10,... | collective-permute-start | bytes 737288 | tf_op jit(solution)/shard_map/ppermute | solution.py:933
  180.1 12.6 %collective-permute-start.22 = (bf16[288,512]{1,0:T(8,128)(2,1)S(1)}, bf16[288,512]{1,0:T(8,128)(2,1)S(1)}, u32[]{:S(2)}, u32[]{:S(2)}) collective-permute-start(bf16[288,512]{1,0:T(8,128)(2,1)S(1)} %fusion.11), channel_id=1, source_target_pairs={{0,2},{1,3},{2,0},{3,1},{4,6},{5,7},{6,4},{7,5},{8,10},{9,11},{10,... | collective-permute-start | bytes 884744 | tf_op jit(solution)/shard_map/ppermute | solution.py:27
  193.0 9.5 %collective-permute-start.26 = (bf16[240,512]{1,0:T(8,128)(2,1)S(1)}, bf16[240,512]{1,0:T(8,128)(2,1)S(1)}, u32[]{:S(2)}, u32[]{:S(2)}) collective-permute-start(bf16[240,512]{1,0:T(8,128)(2,1)S(1)} %pad_maximum_fusion.10), channel_id=1, source_target_pairs={{0,8},{4,12},{8,0},{12,4},{16,24},{20,28},{24,16},{28,20},{1,9},{5... | collective-permute-start | bytes 737288 | tf_op jit(solution)/shard_map/ppermute | solution.py:27
  193.5 9.1 %collective-permute-start.27 = (bf16[208,512]{1,0:T(8,128)(2,1)S(1)}, bf16[208,512]{1,0:T(8,128)(2,1)S(1)}, u32[]{:S(2)}, u32[]{:S(2)}) collective-permute-start(bf16[208,512]{1,0:T(8,128)(2,1)S(1)} %fusion.9), channel_id=1, source_target_pairs={{0,16},{4,20},{8,24},{12,28},{24,8},{28,12},{1,17},{5,21},{9,25},{... | collective-permute-start | bytes 638984 | tf_op jit(solution)/shard_map/ppermute | solution.py:945
  202.6 5.5 %collective-permute-start.28 = (f32[24,512]{1,0:T(8,128)S(1)}, f32[24,512]{1,0:T(8,128)S(1)}, u32[]{:S(2)}, u32[]{:S(2)}) collective-permute-start(f32[24,512]{1,0:T(8,128)S(1)} %maximum_add_fusion.2), channel_id=1, source_target_pairs={{0,16},{4,20},{8,24},{12,28},{16,0},{20,4},{24,8},{28,12},{1,17},{... | collective-permute-start | bytes 147464 | tf_op jit(solution)/shard_map/ppermute | solution.py:27
  206.1 9.3 %collective-permute-start.29 = (bf16[208,512]{1,0:T(8,128)(2,1)S(1)}, bf16[208,512]{1,0:T(8,128)(2,1)S(1)}, u32[]{:S(2)}, u32[]{:S(2)}) collective-permute-start(bf16[208,512]{1,0:T(8,128)(2,1)S(1)} %fusion.5), channel_id=1, source_target_pairs={{16,0},{20,4},{17,1},{21,5},{18,2},{22,6},{19,3},{23,7}} | collective-permute-start | bytes 638984 | tf_op jit(solution)/shard_map/ppermute | solution.py:974
  (20 other events, 88.7 us)

commit v2 on v1

--- a/solution.py
+++ b/solution.py
@@ -235,8 +235,8 @@
     first_half = lax.broadcasted_iota(jnp.int32, (columns + far, LANES), 1) < head_width
     far_index = lax.broadcasted_iota(jnp.int32, (far, columns), 0)
     keys = head_keys(rows_per_step, width)
-    for start in range(0, len(keys), HEADS):
-        group = keys[start : start + HEADS]
+    for start in range(0, len(keys), 4 * HEADS):
+        group = keys[start : start + 4 * HEADS]
         scores, low, mixed = {}, {}, {}
         for row, pair, half in group:
             global_row = first_row_ref[0] + lax.rem(step * rows_per_step + row, local_rows)
@@ -254,7 +254,7 @@
         for row, pair, half in group:
             found = scores.pop((row, pair, half))
             top = jnp.max(found, axis=0, keepdims=True)
-            powers = jnp.exp((found - top) * scaling)
+            powers = jnp.exp2((found - top) * (scaling * math.log2(math.e)))
             inverse = 1.0 / jnp.sum(powers, axis=0, keepdims=True)
             low[row, pair, half] = (powers * inverse).astype(HALF)
             probs_ref[row, 2 * pair + half] = low[row, pair, half]
@@ -296,7 +296,7 @@
     tokens, width = block_in.shape
     images, far, _ = key_far.shape
     first_image, count = group
-    rows_per_step = math.gcd(local_rows, 2)
+    rows_per_step = math.gcd(local_rows, 4)
     steps = local_rows // rows_per_step
     first_step = first_image * steps
     size = rows_per_step * columns
@@ -382,7 +382,7 @@
     gain_ref,
     *rest,
 ):
-    given, rest = rest[: len(masks)], rest[len(masks) :]
+    given, rest = rest[: max(1, 3 * len(masks))], rest[max(1, 3 * len(masks)) :]
     out_ref, middle_grad_ref, mixed_grad_ref, grad_gain_ref, *rest = rest
     *pieces, grad_out_ref, grad_inner_ref, grad_outer_ref, w_inner_ref, flat_ref, sems = rest
     width, hidden = w_inner_ref.shape
@@ -400,8 +400,24 @@
         if block is None:
             flat_ref[...] = given[0][...]
         else:
-            placed = [(ref, mask, first) for ref, (mask, first) in zip(given, masks)]
-            assemble(flat_ref, placed, lax.rem(index_ref[0], 8), block, 3)
+            plane = 8 * block
+            here, z = lax.rem(index_ref[0], 8), lax.div(index_ref[0], 8)
+            own, first, last = (
+                list(zip(given[i * len(masks) : (i + 1) * len(masks)], masks)) for i in range(3)
+            )
+            clear_seams(flat_ref, block, 3)
+
+            @pl.when(z == 0)
+            def _():
+                assemble(flat_ref, first, here, block, 0)
+
+            @pl.when(z > 0)
+            def _():
+                assemble(flat_ref, own, here, block, (z - 1) * plane)
+
+            for i, slot in enumerate(second_slots(z)):
+                pieces_here = [(ref.at[i], mask) for ref, mask in last]
+                assemble(flat_ref, pieces_here, here, block, (slot - 1) * plane)
         mix = weave(groups, per)
         for c in range(width // per):
             start = inner_start + c * groups * per
@@ -486,13 +502,14 @@
     tokens, width = block_in.shape
     tile = pl.BlockSpec((size, width), lambda i, _: (i, 0))
     piece_specs, piece_shapes = piece_outputs(shapes)
-    masks = [entry[1:] for entry in given]
+    masks = [] if block is None else [mask for _, mask in given[: len(given) // 3]]
+    arrays = [given] if block is None else [array for array, _ in given]
     return pl.pallas_call(
-        functools.partial(feed_forward_kernel, 512, plan, masks, block),
+        functools.partial(feed_forward_kernel, 256, plan, masks, block),
         grid_spec=pltpu.PrefetchScalarGridSpec(
             num_scalar_prefetch=1,
             grid=(tokens // size,),
-            in_specs=[tile, tile, tile, whole_block((1, width))] + vmem_specs(len(given)),
+            in_specs=[tile, tile, tile, whole_block((1, width))] + vmem_specs(len(arrays)),
             out_specs=[tile, tile, tile, whole_block((1, width))] + piece_specs,
             scratch_shapes=[
                 pltpu.VMEM((width, width), SINGLE),
@@ -517,7 +534,7 @@
             transcendentals=tokens * hidden,
         ),
         name="feed_forward",
-    )(index, block_in, mixed, cotangent, gain, *[entry[0] for entry in given])
+    )(index, block_in, mixed, cotangent, gain, *arrays)
 
 
 def attention_backward_kernel(
@@ -564,8 +581,8 @@
 
     first_half = lax.broadcasted_iota(jnp.int32, (columns + far, LANES), 1) < head_width
     keys = head_keys(rows_per_step, width)
-    for start in range(0, len(keys), HEADS):
-        group = keys[start : start + HEADS]
+    for start in range(0, len(keys), 2 * HEADS):
+        group = keys[start : start + 2 * HEADS]
         prob_grad, score_grad, value_grad, key_grad, query_grad = {}, {}, {}, {}, {}
         for row, pair, half in group:
             tokens = slice(row * columns, (row + 1) * columns)
@@ -791,25 +808,24 @@
     )(block_in, gain, query_grad, key_grad, value_grad, w_qkv, middle_grad)
 
 
-def assemble(flat_ref, pieces, index, block, count):
-    plane = 8 * block
-    width = flat_ref.shape[1]
-    for at in range(0, count * plane + 1, block):
-        flat_ref[at : at + TAIL] = jnp.zeros((TAIL, width), HALF)
-    for ref, mask, first in pieces:
-        spot = pl.multiple_of((index ^ mask) * block, TAIL)
-        for slot in range(count):
-            part = ref.at[slot] if len(ref.shape) == 3 else ref
-            last = first + part.shape[0]
-            for low, high in ((0, TAIL), (TAIL, block), (block, block + TAIL)):
-                low, high = max(low, first), min(high, last)
-                if low >= high:
-                    continue
-                rows = pl.ds(spot + (slot * plane + low), high - low)
-                value = part[low - first : high - first]
-                if low < TAIL or low >= block:
-                    value = flat_ref[rows] + value
-                flat_ref[rows] = value
+def clear_seams(flat_ref, block, count):
+    for at in range(0, count * 8 * block + 1, block):
+        flat_ref[at : at + TAIL] = jnp.zeros((TAIL, flat_ref.shape[1]), HALF)
+
+
+def assemble(flat_ref, pieces, index, block, base):
+    for ref, mask in pieces:
+        spot = pl.multiple_of(base + (index ^ mask) * block, TAIL)
+        for low, high in ((0, TAIL), (TAIL, block), (block, block + TAIL)):
+            rows = pl.ds(spot + low, high - low)
+            value = ref[low:high]
+            if low != TAIL:
+                value = flat_ref[rows] + value
+            flat_ref[rows] = value
+
+
+def second_slots(z):
+    return [jnp.where(z < 2, 2, 1), jnp.where(z < 3, 3, 2)]
 
 
 def parts_of(value):
@@ -834,15 +850,23 @@
     index_ref,
     *refs,
 ):
-    piece_refs, refs = refs[: len(masks)], refs[len(masks) :]
+    count = len(masks)
+    own_refs, piece_refs, refs = refs[:count], refs[count : 2 * count], refs[2 * count :]
     w_ref, key_far_ref, value_far_ref, standard_ref, summary_ref, *refs = refs
     *stat_refs, flat_ref, shown_ref, means_ref = refs
     width = flat_ref.shape[1]
     rows = block + TAIL
     here = lax.rem(index_ref[0], 8)
-    assemble(
-        flat_ref, [(ref.at[:rows], mask, 0) for ref, mask in zip(piece_refs, masks)], here, block, 1
-    )
+    clear_seams(flat_ref, block, 1)
+
+    @pl.when(index_ref[0] < 8)
+    def _():
+        assemble(flat_ref, list(zip(own_refs, masks)), here, block, 0)
+
+    @pl.when(index_ref[0] >= 8)
+    def _():
+        assemble(flat_ref, list(zip(piece_refs, masks)), here, block, 0)
+
     for ref, mask in zip(piece_refs, masks):
         shown_ref[here ^ mask] = ref[rows:]
     flat_ref[3 * width :] += shown_ref[0, :TAIL]
@@ -876,8 +900,8 @@
     return [pl.BlockSpec(memory_space=pltpu.VMEM)] * count
 
 
-def projection_weights(index, pieces, block, images, local_rows, summary_count):
-    arrays, masks = [p[0] for p in pieces], [p[1] for p in pieces]
+def projection_weights(index, own_pieces, pieces, block, images, local_rows, summary_count):
+    arrays, masks = [p[0] for p in own_pieces + pieces], [p[1] for p in pieces]
     width = arrays[0].shape[1]
     far = 4 * images * local_rows
     return pl.pallas_call(
@@ -974,6 +998,11 @@
     return lax.ppermute(value, "img", [(i, i ^ 4) for i in range(lax.axis_size("img")) if i // 2 == 2])
 
 
+def plane_pieces(own, near):
+    pieces = [(array, 2 * i) for i, array in enumerate([own] + list(near))]
+    return pieces + [(swap_core(array), mask | 1) for array, mask in pieces]
+
+
 def across_plane(sent):
     return (swap_x(sent[0]), swap_y(sent[1]), swap_both(sent[2]))
 
@@ -1017,28 +1046,34 @@
     row_means = jnp.mean(activations.astype(SINGLE), axis=2)
     sums = jnp.stack([jnp.sum(row_means, axis=(0, 1)), jnp.sum(row_means * row_means, axis=(0, 1))])
     if planes:
+        weights, sums, row_means = together(weights, sums, row_means)
         own, start = own_rows(weights, width)
         piece_rows = block + TAIL
         own = jnp.concatenate([own] + parts_of(sums) + [jnp.zeros((TAIL - 6, width), HALF)])
         over_far = swap_far(own)
+        own_rows_only = own[:piece_rows]
+        own_near = across_plane([own_rows_only] * 3)
         over_near = swap_near(jnp.stack([own, over_far]))
+        over_near, own_near = together(over_near, own_near)
+        own_pieces = plane_pieces(own_rows_only, own_near)
         held = [own, over_near[0], over_far, over_near[1]]
         sums = [whole_of(array[piece_rows : piece_rows + 6]) for array in held]
         sums = (sums[0] + sums[1]) + (sums[2] + sums[3])
         held = jnp.stack([array[:piece_rows] for array in held])
-        slots = [lax.dynamic_index_in_dim(held, z ^ i, 0, keepdims=False) for i in range(4)]
+
+        def slot(i):
+            return lax.dynamic_index_in_dim(held, z ^ i, 0, keepdims=False)
+
         means = row_means.reshape(-1, width)
         spare = jnp.zeros((TAIL - 2 - means.shape[0], width), SINGLE)
         known = parts_of(jnp.concatenate([means, sums, spare]))
-        first_slot = jnp.concatenate([slots[0], slots[1][:TAIL]] + known)
-        other_slots = jnp.stack(slots[1:])
-        first_near = [swap_x(first_slot), swap_y(first_slot), swap_both(first_slot)]
-        first_near, other_slots = together(first_near, other_slots)
-        first_pieces = [(array, 2 * i) for i, array in enumerate([first_slot] + list(first_near))]
-        first_pieces += [(swap_core(array), mask | 1) for array, mask in first_pieces]
-        other_near = [swap_x(other_slots), swap_y(other_slots), swap_both(other_slots)]
+        first_slot = jnp.concatenate([slot(jnp.where(z == 0, 1, 0)), slot(1)[:TAIL]] + known)
+        last_slots = jnp.stack([slot(i) for i in second_slots(z)])
+        first_near, last_slots = together(across_plane([first_slot] * 3), last_slots)
+        first_pieces = plane_pieces(first_slot, first_near)
+        last_near = across_plane([last_slots] * 3)
         w_qkv, key_far, value_far, standard, summary_low, *stats = projection_weights(
-            index, first_pieces, block, images, local_rows, summary_count
+            index, own_pieces, first_pieces, block, images, local_rows, summary_count
         )
         summary_mean, summary_var, summary_inv = (row.reshape(width) for row in stats[:3])
         gain_one, gain_sum, bias_sum, gain_two = stats[3:]
@@ -1075,9 +1110,8 @@
         columns,
     )
     if planes:
-        other_near, forward = together(other_near, forward)
-        given = [(array, 2 * i, 0) for i, array in enumerate([other_slots] + list(other_near))]
-        given += [(swap_core(array), mask | 1, 0) for array, mask, _ in given]
+        last_near, forward = together(last_near, forward)
+        given = own_pieces + first_pieces + plane_pieces(last_slots, last_near)
     query, key, value, mixed, probs = forward
 
     if planes:
@@ -1090,7 +1124,7 @@
         late_shapes = [(TAIL + 3 * width, width)]
         early_plan = [(0, (), lambda i: i * 0, early_shapes[0][0])]
         late_plan = [(0, (), lambda i: i * 0, late_shapes[0][0])]
-        given = [(jnp.pad(matrix_rows[3 * width :], ((TAIL, 0), (0, 0))), 0, 0)]
+        given = jnp.pad(matrix_rows[3 * width :], ((TAIL, 0), (0, 0)))
 
     out, middle_grad, mixed_grad, gain_two_grad, *early = feed_forward(
         index,

time: 218 us -> 213 us (0.977)
  waiting for transfers between devices: 53.1 us -> 45.5 us
  starting transfers between devices: 34.3 us -> 39.1 us
    ppermute x24 -> x30, waiting for transfers between devices: 44.5 us -> 37.9 us  [swap(): return lax.ppermute(value, axis, [(i, i ^ distance) for i in range(size)])]
    ppermute x24 -> x30, starting transfers between devices: 22.7 us -> 26.6 us  [swap(): return lax.ppermute(value, axis, [(i, i ^ distance) for i in range(size)])]
    pallas_call x1, Pallas kernels: 20 us -> 17.7 us  [attention_forward(): pl.pallas_call(body, grid_spec=pltpu.PrefetchScalarGridSpec(num_scalar_pr...]
    ppermute x4 -> x5, starting transfers between devices: 4.62 us -> 5.3 us  [swap_both(): lax.ppermute(value, ('img', 'row'), [(i, i ^ 6) for i in range(size)])]
  transfers between devices with their start and end apart: 30 -> 37, of which waited for: 15 -> 15; matrix products, arithmetic and copies ran while one was open for 4% -> 4% of each run, Pallas kernels for 27% -> 27%
where the time goes in v2:
time: 213 us; the launch traced here: 212 us
  Pallas kernels  105 us (49%)
  waiting for transfers between devices  45.5 us (21%)
  starting transfers between devices  39.1 us (18%)
  other arithmetic  13.9 us (7%)
  local copies, waits for them, and re-layouts  7.27 us (3%)
    pallas_call x1, Pallas kernels, feed_forward(): pl.pallas_call(functools.partial(feed_forward_kernel, 256, plan, masks, b...  48.3 us
    ppermute x30, waiting for transfers between devices, swap(): return lax.ppermute(value, axis, [(i, i ^ distance) for i in range(size)])  37.9 us
    ppermute x30, starting transfers between devices, swap(): return lax.ppermute(value, axis, [(i, i ^ distance) for i in range(size)])  26.6 us
    pallas_call x1, Pallas kernels, attention_backward(): pl.pallas_call(functools.partial(attention_backward_kernel, 1.0 / math.sq...  23.4 us
    pallas_call x1, Pallas kernels, attention_forward(): pl.pallas_call(body, grid_spec=pltpu.PrefetchScalarGridSpec(num_scalar_pr...  17.7 us
    pallas_call x1, Pallas kernels, input_grads(): pl.pallas_call(input_grad_kernel, grid=(tokens // size,), in_specs=[block...  11.4 us
    ppermute x1, starting transfers between devices, send_far(): lax.ppermute(value, 'img', [(i, i ^ 4) for i in range(lax.axis_size('img'...  5.97 us
    ppermute x5, starting transfers between devices, swap_both(): lax.ppermute(value, ('img', 'row'), [(i, i ^ 6) for i in range(size)])  5.3 us
  transfers between devices with their start and end apart: 37, of which 15 were waited for; matrix products, arithmetic and copies ran while one was open for 4% of the time, Pallas kernels for 27%

profile of v2, /device:TPU:0, one launch (start us, length us, event | category | flops | bytes accessed | tf_op | source)
XLA Modules:
  0.0 212.1 jit_solution(3080034838998578728)
XLA Ops:
  0.7 2.1 convert_reduce_fusion
  2.8 2.0 dynamic_update_slice.3
  5.2 4.1 %collective-permute-start = (bf16[224,512]{1,0:T(8,128)(2,1)S(1)}, bf16[224,512]{1,0:T(8,128)(2,1)S(1)}, u32[]{:S(2)}, u32[]{:S(2)}) collective-permute-start(bf16[224,512]{1,0:T(8,128)(2,1)S(1)} %concatenate.42), channel_id=1, source_target_pairs={{0,16},{4,20},{8,24},{12,28},{16,0},{20,4},{24,8},{28,12},{1,17},{... | collective-permute-start | bytes 688136 | tf_op jit(solution)/shard_map/ppermute | solution.py:27
  9.3 1.5 collective-permute-start.2
  10.8 1.5 collective-permute-start.3
  13.1 6.7 %collective-permute-done = bf16[224,512]{1,0:T(8,128)(2,1)S(1)} collective-permute-done((bf16[224,512]{1,0:T(8,128)(2,1)S(1)}, bf16[224,512]{1,0:T(8,128)(2,1)S(1)}, u32[]{:S(2)}, u32[]{:S(2)}) %collective-permute-start) | collective-permute-done | bytes 229408 | tf_op jit(solution)/shard_map/ppermute | solution.py:27
  21.8 9.8 %collective-permute-done.1 = bf16[2,224,512]{2,1,0:T(8,128)(2,1)S(1)} collective-permute-done((bf16[2,224,512]{2,1,0:T(8,128)(2,1)S(1)}, bf16[2,224,512]{2,1,0:T(8,128)(2,1)S(1)}, u32[]{:S(2)}, u32[]{:S(2)}) %collective-permute-start.1) | collective-permute-done | bytes 458784 | tf_op jit(solution)/shard_map/ppermute | solution.py:27
  32.1 1.3 collective-permute-start.5
  33.5 1.5 collective-permute-start.6
  36.2 5.6 %collective-permute-done.5.refs_9_.rest_9_ = bf16[272,512]{1,0:T(8,128)(2,1)S(1)} collective-permute-done((bf16[272,512]{1,0:T(8,128)(2,1)S(1)}, bf16[272,512]{1,0:T(8,128)(2,1)S(1)}, u32[]{:S(2)}, u32[]{:S(2)}) %collective-permute-start.5) | collective-permute-done | bytes 278560 | tf_op jit(solution)/shard_map/ppermute | solution.py:27
  41.9 4.2 %collective-permute-done.6.refs_10_.rest_10_ = bf16[272,512]{1,0:T(8,128)(2,1)S(1)} collective-permute-done((bf16[272,512]{1,0:T(8,128)(2,1)S(1)}, bf16[272,512]{1,0:T(8,128)(2,1)S(1)}, u32[]{:S(2)}, u32[]{:S(2)}) %collective-permute-start.6) | collective-permute-done | bytes 278560 | tf_op jit(solution)/shard_map/ppermute | solution.py:27
  50.1 1.5 collective-permute-start.10
  51.6 1.5 collective-permute-start.8
  54.4 3.9 %projection_weights.1 = (bf16[512,1536]{1,0:T(8,128)(2,1)}, bf16[48,512]{1,0:T(8,128)(2,1)}, bf16[48,512]{1,0:T(8,128)(2,1)}, f32[48,512]{1,0:T(8,128)}, bf16[48...) custom-call(s32[1]{0:T(128)} %bitcast.index_ref, ...), custom_call_target="tpu_custom_call" | custom-call | tf_op jit(solution)/shard_map/projection_weights/pallas_call | solution.py:907
  58.4 17.7 %attention_forward.1 = (bf16[2304,512]{1,0:T(8,128)(2,1)}, bf16[2304,512]{1,0:T(8,128)(2,1)}, bf16[2304,512]{1,0:T(8,128)(2,1)}, bf16[2304,512]{1,0:T(8,128)(2,1)}, bf16[12,8,208,192]{3,2,1,0:T(8,128)(2,1)}) custom-call(s32[1]{0:T(128)} %bitcast.11.refs_0_, bf16[2304,512]{1,0:T(8,128)(2,1)} %bitcast.74, f32[1,512]{1,0:T(1,128)} %get-tuple-element.87.refs_2_.rest_0_.gain_ref, ...), custom_call_target="tpu_custom_call" | custom-call | flops 5586812928 | bytes 21823488 | tf_op jit(solution)/shard_map/attention_forward/pallas_call | solution.py:321
  80.0 48.3 %feed_forward.1 = (bf16[2304,512]{1,0:T(8,128)(2,1)}, f32[2304,512]{1,0:T(8,128)}, bf16[2304,512]{1,0:T(8,128)(2,1)}, f32[1,512]{1,0:T(1,128)}, bf16[1,3,208,512...) custom-call(s32[1]{0:T(128)} %bitcast.index_ref, ...), custom_call_target="tpu_custom_call" | custom-call | flops 32614907904 | bytes 24903680 | tf_op jit(solution)/shard_map/feed_forward/pallas_call | solution.py:507
  128.7 4.7 %collective-permute-done.23 = bf16[4,3,208,512]{3,2,1,0:T(8,128)(2,1)S(1)} collective-permute-done((bf16[4,3,208,512]{3,2,1,0:T(8,128)(2,1)}, bf16[4,3,208,512]{3,2,1,0:T(8,128)(2,1)S(1)}, u32[]{:S(2)}, u32[]{:S(2)}) %collective-permute-start.23) | collective-permute-done | bytes 2555936 | tf_op jit(solution)/shard_map/ppermute | solution.py:27
  133.4 3.2 %fusion.2 = (bf16[3,208,512]{2,1,0:T(8,128)(2,1)S(1)}, bf16[3,208,512]{2,1,0:T(8,128)(2,1)S(1)}, bf16[3,208,512]{2,1,0:T(8,128)(2,1)}, f32[3,208,512]{2,1,0:T(8,128)S(1)}) fusion(bf16[1,3,208,512]{3,2,1,0:T(8,128)(2,1)} %get-tuple-element.110, bf16[4,3,208,512]{3,2,1,0:T(8,128)(2,1)S(1)} %collective-permute-done.23, ...), kind=kLoop, calls=%fused_computation.10 | loop fusion | flops 4792320 | bytes 8306688 | tf_op jit(solution)/shard_map/convert_element_type | solution.py:991
  138.7 1.4 collective-permute-start.28
  140.1 23.4 %attention_backward.1 = (bf16[2304,512]{1,0:T(8,128)(2,1)}, bf16[2304,512]{1,0:T(8,128)(2,1)}, bf16[2304,512]{1,0:T(8,128)(2,1)}, f32[72,512]{1,0:T(8,128)}, bf1...) custom-call(s32[1]{0:T(128)} %bitcast.index_ref, ...), custom_call_target="tpu_custom_call" | custom-call | flops 7549747200 | bytes 26542080 | tf_op jit(solution)/shard_map/attention_backward/pallas_call | solution.py:740
  164.1 2.3 %collective-permute-done.25 = f32[72,512]{1,0:T(8,128)S(1)} collective-permute-done((f32[72,512]{1,0:T(8,128)}, f32[72,512]{1,0:T(8,128)S(1)}, u32[]{:S(2)}, u32[]{:S(2)}) %collective-permute-start.25) | collective-permute-done | bytes 147488 | tf_op jit(solution)/shard_map/ppermute | solution.py:27
  168.2 1.8 add_add_fusion
  170.5 2.5 %collective-permute-start.32 = (bf16[2,208,512]{2,1,0:T(8,128)(2,1)S(1)}, bf16[2,208,512]{2,1,0:T(8,128)(2,1)S(1)}, u32[]{:S(2)}, u32[]{:S(2)}) collective-permute-start(bf16[2,208,512]{2,1,0:T(8,128)(2,1)S(1)} %pad_maximum_fusion.3), channel_id=1, source_target_pairs={{0,8},{4,12},{8,0},{12,4},{16,24},{20,28},{24,16},{28,20},{1,9},{5... | collective-permute-start | bytes 1277960 | tf_op jit(solution)/shard_map/ppermute | solution.py:27
  174.0 1.2 collective-permute-start.31
  175.2 1.5 collective-permute-start.29
  176.7 11.4 %input_grads.1 = f32[2304,512]{1,0:T(8,128)} custom-call(bf16[2304,512]{1,0:T(8,128)(2,1)} %bitcast.77, f32[1,512]{1,0:T(1,128)} %get-tuple-element.87.refs_2_.rest_0_.gain_ref, bf16[2304,512]{1,0:T(8,128)(2,1)} %get-tuple-element.137.query_grad_ref, bf16[2304,512]{1,0:T(8,128)(2,1)} %get-tuple-element.138.key_grad_ref, ...), custom_call_target="tpu_custom_call" | custom-call | flops 3623878656 | bytes 18874368 | tf_op jit(solution)/shard_map/input_grads/pallas_call | solution.py:795
  188.7 6.0 %collective-permute-start.34 = (bf16[208,512]{1,0:T(8,128)(2,1)S(1)}, bf16[208,512]{1,0:T(8,128)(2,1)S(1)}, u32[]{:S(2)}, u32[]{:S(2)}) collective-permute-start(bf16[208,512]{1,0:T(8,128)(2,1)S(1)} %fusion.9), channel_id=1, source_target_pairs={{0,16},{4,20},{8,24},{12,28},{24,8},{28,12},{1,17},{5,21},{9,25},{... | collective-permute-start | bytes 638984 | tf_op jit(solution)/shard_map/ppermute | solution.py:969
  194.7 3.3 %collective-permute-done.34 = bf16[208,512]{1,0:T(8,128)(2,1)S(1)} collective-permute-done((bf16[208,512]{1,0:T(8,128)(2,1)S(1)}, bf16[208,512]{1,0:T(8,128)(2,1)S(1)}, u32[]{:S(2)}, u32[]{:S(2)}) %collective-permute-start.34) | collective-permute-done | bytes 213024 | tf_op jit(solution)/shard_map/ppermute | solution.py:969
  198.1 3.4 %collective-permute-start.35 = (f32[24,512]{1,0:T(8,128)S(1)}, f32[24,512]{1,0:T(8,128)S(1)}, u32[]{:S(2)}, u32[]{:S(2)}) collective-permute-start(f32[24,512]{1,0:T(8,128)S(1)} %maximum_add_fusion.2), channel_id=1, source_target_pairs={{0,16},{4,20},{8,24},{12,28},{16,0},{20,4},{24,8},{28,12},{1,17},{... | collective-permute-start | bytes 147464 | tf_op jit(solution)/shard_map/ppermute | solution.py:27
  201.6 1.3 collective-permute-start.36
  204.5 2.8 %broadcast_add_fusion = f32[3,4,192,512]{3,2,1,0:T(8,128)} fusion(f32[3,4,192,512]{3,2,1,0:T(8,128)S(1)} %bitcast.73, f32[3,4,512]{2,1,0:T(4,128)S(1)} %multiply_multiply_fusion), kind=kLoop, calls=%fused_computation.1 | loop fusion | flops 1179648 | bytes 9461760 | tf_op jit(solution)/shard_map/add | solution.py:1211
  207.3 3.4 %collective-permute-done.36 = bf16[208,512]{1,0:T(8,128)(2,1)S(1)} collective-permute-done((bf16[208,512]{1,0:T(8,128)(2,1)S(1)}, bf16[208,512]{1,0:T(8,128)(2,1)S(1)}, u32[]{:S(2)}, u32[]{:S(2)}) %collective-permute-start.36) | collective-permute-done | bytes 213024 | tf_op jit(solution)/shard_map/ppermute | solution.py:998
  (180 shorter events, 23.5 us)
Async XLA Ops:
  5.2 14.6 %collective-permute-start = (bf16[224,512]{1,0:T(8,128)(2,1)S(1)}, bf16[224,512]{1,0:T(8,128)(2,1)S(1)}, u32[]{:S(2)}, u32[]{:S(2)}) collective-permute-start(bf16[224,512]{1,0:T(8,128)(2,1)S(1)} %concatenate.42), channel_id=1, source_target_pairs={{0,16},{4,20},{8,24},{12,28},{16,0},{20,4},{24,8},{28,12},{1,17},{... | collective-permute-start | bytes 688136 | tf_op jit(solution)/shard_map/ppermute | solution.py:27
  9.3 11.4 %collective-permute-start.2 = (bf16[208,512]{1,0:T(8,128)(2,1)S(1)}, bf16[208,512]{1,0:T(8,128)(2,1)S(1)}, u32[]{:S(2)}, u32[]{:S(2)}) collective-permute-start(bf16[208,512]{1,0:T(8,128)(2,1)S(1)} %reshape.250.refs_0_.rest_0_), channel_id=1, source_target_pairs={{0,2},{1,3},{2,0},{3,1},{4,6},{5,7},{6,4},{7,5},{8,10},{9,11},{10,... | collective-permute-start | bytes 638984 | tf_op jit(solution)/shard_map/ppermute | solution.py:27
  10.8 11.0 %collective-permute-start.3 = (bf16[208,512]{1,0:T(8,128)(2,1)S(1)}, bf16[208,512]{1,0:T(8,128)(2,1)S(1)}, u32[]{:S(2)}, u32[]{:S(2)}) collective-permute-start(bf16[208,512]{1,0:T(8,128)(2,1)S(1)} %reshape.250.refs_0_.rest_0_), channel_id=1, source_target_pairs={{0,4},{4,0},{8,12},{12,8},{16,20},{20,16},{24,28},{28,24},{1,5},{5... | collective-permute-start | bytes 638984 | tf_op jit(solution)/shard_map/ppermute | solution.py:27
  12.3 9.5 %collective-permute-start.4 = (bf16[208,512]{1,0:T(8,128)(2,1)S(1)}, bf16[208,512]{1,0:T(8,128)(2,1)S(1)}, u32[]{:S(2)}, u32[]{:S(2)}) collective-permute-start(bf16[208,512]{1,0:T(8,128)(2,1)S(1)} %reshape.250.refs_0_.rest_0_), channel_id=1, source_target_pairs={{0,6},{1,7},{2,4},{3,5},{4,2},{5,3},{6,0},{7,1},{8,14},{9,15},{10,... | collective-permute-start | bytes 638984 | tf_op jit(solution)/shard_map/ppermute | solution.py:957
  19.9 11.8 %collective-permute-start.1 = (bf16[2,224,512]{2,1,0:T(8,128)(2,1)S(1)}, bf16[2,224,512]{2,1,0:T(8,128)(2,1)S(1)}, u32[]{:S(2)}, u32[]{:S(2)}) collective-permute-start(bf16[2,224,512]{2,1,0:T(8,128)(2,1)S(1)} %pad_maximum_fusion.1), channel_id=1, source_target_pairs={{0,8},{4,12},{8,0},{12,4},{16,24},{20,28},{24,16},{28,20},{1,9},{5... | collective-permute-start | bytes 1376264 | tf_op jit(solution)/shard_map/ppermute | solution.py:27
  32.1 9.7 %collective-permute-start.5 = (bf16[272,512]{1,0:T(8,128)(2,1)S(1)}, bf16[272,512]{1,0:T(8,128)(2,1)S(1)}, u32[]{:S(2)}, u32[]{:S(2)}) collective-permute-start(bf16[272,512]{1,0:T(8,128)(2,1)S(1)} %constant_dynamic-update-slice_fusion.refs_8_.rest_8_), channel_id=1, source_target_pairs={{0,2},{1,3},{2,0},{3,1},{4,6},{5,7},{6,4},{7,5},{8,10},{9,11},{10,... | collective-permute-start | bytes 835592 | tf_op jit(solution)/shard_map/ppermute | solution.py:27
  33.5 12.6 %collective-permute-start.6 = (bf16[272,512]{1,0:T(8,128)(2,1)S(1)}, bf16[272,512]{1,0:T(8,128)(2,1)S(1)}, u32[]{:S(2)}, u32[]{:S(2)}) collective-permute-start(bf16[272,512]{1,0:T(8,128)(2,1)S(1)} %constant_dynamic-update-slice_fusion.refs_8_.rest_8_), channel_id=1, source_target_pairs={{0,4},{4,0},{8,12},{12,8},{16,20},{20,16},{24,28},{28,24},{1,5},{5... | collective-permute-start | bytes 835592 | tf_op jit(solution)/shard_map/ppermute | solution.py:27
  35.0 11.1 %collective-permute-start.7 = (bf16[272,512]{1,0:T(8,128)(2,1)S(1)}, bf16[272,512]{1,0:T(8,128)(2,1)S(1)}, u32[]{:S(2)}, u32[]{:S(2)}) collective-permute-start(bf16[272,512]{1,0:T(8,128)(2,1)S(1)} %constant_dynamic-update-slice_fusion.refs_8_.rest_8_), channel_id=1, source_target_pairs={{0,6},{1,7},{2,4},{3,5},{4,2},{5,3},{6,0},{7,1},{8,14},{9,15},{10,... | collective-permute-start | bytes 835592 | tf_op jit(solution)/shard_map/ppermute | solution.py:957
  35.7 10.9 %collective-permute-start.11 = (bf16[208,512]{1,0:T(8,128)(2,1)S(1)}, bf16[208,512]{1,0:T(8,128)(2,1)S(1)}, u32[]{:S(2)}, u32[]{:S(2)}) collective-permute-start(bf16[208,512]{1,0:T(8,128)(2,1)S(1)} %reshape.250.refs_0_.rest_0_), channel_id=1, source_target_pairs={{0,1},{1,0},{2,3},{3,2},{4,5},{5,4},{6,7},{7,6},{8,9},{9,8},{10,11... | collective-permute-start | bytes 638984 | tf_op jit(solution)/shard_map/ppermute | solution.py:27
  35.7 11.6 %collective-permute-start.12 = (bf16[208,512]{1,0:T(8,128)(2,1)S(1)}, bf16[208,512]{1,0:T(8,128)(2,1)S(1)}, u32[]{:S(2)}, u32[]{:S(2)}) collective-permute-start(bf16[208,512]{1,0:T(8,128)(2,1)S(1)} %collective-permute-done.2.refs_1_.rest_1_), channel_id=1, source_target_pairs={{0,1},{1,0},{2,3},{3,2},{4,5},{5,4},{6,7},{7,6},{8,9},{9,8},{10,11... | collective-permute-start | bytes 638984 | tf_op jit(solution)/shard_map/ppermute | solution.py:27
  41.8 5.6 %collective-permute-start.13 = (bf16[208,512]{1,0:T(8,128)(2,1)S(1)}, bf16[208,512]{1,0:T(8,128)(2,1)S(1)}, u32[]{:S(2)}, u32[]{:S(2)}) collective-permute-start(bf16[208,512]{1,0:T(8,128)(2,1)S(1)} %collective-permute-done.3.refs_2_.rest_2_), channel_id=1, source_target_pairs={{0,1},{1,0},{2,3},{3,2},{4,5},{5,4},{6,7},{7,6},{8,9},{9,8},{10,11... | collective-permute-start | bytes 638984 | tf_op jit(solution)/shard_map/ppermute | solution.py:27
  46.1 5.5 %collective-permute-start.15 = (bf16[272,512]{1,0:T(8,128)(2,1)S(1)}, bf16[272,512]{1,0:T(8,128)(2,1)S(1)}, u32[]{:S(2)}, u32[]{:S(2)}) collective-permute-start(bf16[272,512]{1,0:T(8,128)(2,1)S(1)} %constant_dynamic-update-slice_fusion.refs_8_.rest_8_), channel_id=1, source_target_pairs={{0,1},{1,0},{2,3},{3,2},{4,5},{5,4},{6,7},{7,6},{8,9},{9,8},{10,11... | collective-permute-start | bytes 835592 | tf_op jit(solution)/shard_map/ppermute | solution.py:27
  46.1 7.0 %collective-permute-start.16 = (bf16[272,512]{1,0:T(8,128)(2,1)S(1)}, bf16[272,512]{1,0:T(8,128)(2,1)S(1)}, u32[]{:S(2)}, u32[]{:S(2)}) collective-permute-start(bf16[272,512]{1,0:T(8,128)(2,1)S(1)} %collective-permute-done.5.refs_9_.rest_9_), channel_id=1, source_target_pairs={{0,1},{1,0},{2,3},{3,2},{4,5},{5,4},{6,7},{7,6},{8,9},{9,8},{10,11... | collective-permute-start | bytes 835592 | tf_op jit(solution)/shard_map/ppermute | solution.py:27
  46.6 7.0 %collective-permute-start.17 = (bf16[272,512]{1,0:T(8,128)(2,1)S(1)}, bf16[272,512]{1,0:T(8,128)(2,1)S(1)}, u32[]{:S(2)}, u32[]{:S(2)}) collective-permute-start(bf16[272,512]{1,0:T(8,128)(2,1)S(1)} %collective-permute-done.6.refs_10_.rest_10_), channel_id=1, source_target_pairs={{0,1},{1,0},{2,3},{3,2},{4,5},{5,4},{6,7},{7,6},{8,9},{9,8},{10,11... | collective-permute-start | bytes 835592 | tf_op jit(solution)/shard_map/ppermute | solution.py:27
  47.3 6.3 %collective-permute-start.18 = (bf16[272,512]{1,0:T(8,128)(2,1)S(1)}, bf16[272,512]{1,0:T(8,128)(2,1)S(1)}, u32[]{:S(2)}, u32[]{:S(2)}) collective-permute-start(bf16[272,512]{1,0:T(8,128)(2,1)S(1)} %collective-permute-done.7.refs_11_.rest_11_), channel_id=1, source_target_pairs={{0,1},{1,0},{2,3},{3,2},{4,5},{5,4},{6,7},{7,6},{8,9},{9,8},{10,11... | collective-permute-start | bytes 835592 | tf_op jit(solution)/shard_map/ppermute | solution.py:27
  50.1 26.0 %collective-permute-start.10 = (bf16[2,208,512]{2,1,0:T(8,128)(2,1)S(1)}, bf16[2,208,512]{2,1,0:T(8,128)(2,1)S(1)}, u32[]{:S(2)}, u32[]{:S(2)}) collective-permute-start(bf16[2,208,512]{2,1,0:T(8,128)(2,1)S(1)} %pad_maximum_fusion.2.rest_16_), channel_id=1, source_target_pairs={{0,6},{1,7},{2,4},{3,5},{4,2},{5,3},{6,0},{7,1},{8,14},{9,15},{10,... | collective-permute-start | bytes 1277960 | tf_op jit(solution)/shard_map/ppermute | solution.py:957
  51.6 24.5 %collective-permute-start.8 = (bf16[2,208,512]{2,1,0:T(8,128)(2,1)S(1)}, bf16[2,208,512]{2,1,0:T(8,128)(2,1)S(1)}, u32[]{:S(2)}, u32[]{:S(2)}) collective-permute-start(bf16[2,208,512]{2,1,0:T(8,128)(2,1)S(1)} %pad_maximum_fusion.2.rest_16_), channel_id=1, source_target_pairs={{0,2},{1,3},{2,0},{3,1},{4,6},{5,7},{6,4},{7,5},{8,10},{9,11},{10,... | collective-permute-start | bytes 1277960 | tf_op jit(solution)/shard_map/ppermute | solution.py:27
  53.1 23.0 %collective-permute-start.9 = (bf16[2,208,512]{2,1,0:T(8,128)(2,1)S(1)}, bf16[2,208,512]{2,1,0:T(8,128)(2,1)S(1)}, u32[]{:S(2)}, u32[]{:S(2)}) collective-permute-start(bf16[2,208,512]{2,1,0:T(8,128)(2,1)S(1)} %pad_maximum_fusion.2.rest_16_), channel_id=1, source_target_pairs={{0,4},{4,0},{8,12},{12,8},{16,20},{20,16},{24,28},{28,24},{1,5},{5... | collective-permute-start | bytes 1277960 | tf_op jit(solution)/shard_map/ppermute | solution.py:27
  53.6 23.5 %collective-permute-start.19 = (bf16[2,208,512]{2,1,0:T(8,128)(2,1)S(1)}, bf16[2,208,512]{2,1,0:T(8,128)(2,1)S(1)}, u32[]{:S(2)}, u32[]{:S(2)}) collective-permute-start(bf16[2,208,512]{2,1,0:T(8,128)(2,1)S(1)} %pad_maximum_fusion.2.rest_16_), channel_id=1, source_target_pairs={{0,1},{1,0},{2,3},{3,2},{4,5},{5,4},{6,7},{7,6},{8,9},{9,8},{10,11... | collective-permute-start | bytes 1277960 | tf_op jit(solution)/shard_map/ppermute | solution.py:27
  128.3 5.1 %collective-permute-start.23 = (bf16[4,3,208,512]{3,2,1,0:T(8,128)(2,1)}, bf16[4,3,208,512]{3,2,1,0:T(8,128)(2,1)S(1)}, u32[]{:S(2)}, u32[]{:S(2)}) collective-permute-start(bf16[4,3,208,512]{3,2,1,0:T(8,128)(2,1)} %get-tuple-element.107), channel_id=1, source_target_pairs={{0,1},{1,0},{2,3},{3,2},{4,5},{5,4},{6,7},{7,6},{8,9},{9,8},{10,11... | collective-permute-start | bytes 7667720 | tf_op jit(solution)/shard_map/ppermute | solution.py:27
  136.6 30.8 %collective-permute-start.26 = (bf16[3,208,512]{2,1,0:T(8,128)(2,1)}, bf16[3,208,512]{2,1,0:T(8,128)(2,1)}, u32[]{:S(2)}, u32[]{:S(2)}) collective-permute-start(bf16[3,208,512]{2,1,0:T(8,128)(2,1)} %get-tuple-element.124), channel_id=1, source_target_pairs={{0,2},{1,3},{2,0},{3,1},{4,6},{5,7},{6,4},{7,5},{8,10},{9,11},{10,... | collective-permute-start | bytes 1916936 | tf_op jit(solution)/shard_map/ppermute | solution.py:27
  137.5 29.9 %collective-permute-start.27 = (bf16[3,208,512]{2,1,0:T(8,128)(2,1)S(1)}, bf16[3,208,512]{2,1,0:T(8,128)(2,1)}, u32[]{:S(2)}, u32[]{:S(2)}) collective-permute-start(bf16[3,208,512]{2,1,0:T(8,128)(2,1)S(1)} %get-tuple-element.125), channel_id=1, source_target_pairs={{0,4},{4,0},{8,12},{12,8},{16,20},{20,16},{24,28},{28,24},{1,5},{5... | collective-permute-start | bytes 1916936 | tf_op jit(solution)/shard_map/ppermute | solution.py:27
  138.7 29.6 %collective-permute-start.28 = (bf16[3,208,512]{2,1,0:T(8,128)(2,1)S(1)}, bf16[3,208,512]{2,1,0:T(8,128)(2,1)}, u32[]{:S(2)}, u32[]{:S(2)}) collective-permute-start(bf16[3,208,512]{2,1,0:T(8,128)(2,1)S(1)} %get-tuple-element.126), channel_id=1, source_target_pairs={{0,6},{1,7},{2,4},{3,5},{4,2},{5,3},{6,0},{7,1},{8,14},{9,15},{10,... | collective-permute-start | bytes 1916936 | tf_op jit(solution)/shard_map/ppermute | solution.py:957
  163.6 6.5 %collective-permute-start.24 = (bf16[4,1,208,512]{3,2,1,0:T(8,128)(2,1)}, bf16[4,1,208,512]{3,2,1,0:T(8,128)(2,1)S(1)}, u32[]{:S(2)}, u32[]{:S(2)}) collective-permute-start(bf16[4,1,208,512]{3,2,1,0:T(8,128)(2,1)} %get-tuple-element.118), channel_id=1, source_target_pairs={{0,1},{1,0},{2,3},{3,2},{4,5},{5,4},{6,7},{7,6},{8,9},{9,8},{10,11... | collective-permute-start | bytes 2555912 | tf_op jit(solution)/shard_map/ppermute | solution.py:27
  170.5 17.7 %collective-permute-start.32 = (bf16[2,208,512]{2,1,0:T(8,128)(2,1)S(1)}, bf16[2,208,512]{2,1,0:T(8,128)(2,1)S(1)}, u32[]{:S(2)}, u32[]{:S(2)}) collective-permute-start(bf16[2,208,512]{2,1,0:T(8,128)(2,1)S(1)} %pad_maximum_fusion.3), channel_id=1, source_target_pairs={{0,8},{4,12},{8,0},{12,4},{16,24},{20,28},{24,16},{28,20},{1,9},{5... | collective-permute-start | bytes 1277960 | tf_op jit(solution)/shard_map/ppermute | solution.py:27
  173.1 15.0 %collective-permute-start.30 = (bf16[240,512]{1,0:T(8,128)(2,1)S(1)}, bf16[240,512]{1,0:T(8,128)(2,1)S(1)}, u32[]{:S(2)}, u32[]{:S(2)}) collective-permute-start(bf16[240,512]{1,0:T(8,128)(2,1)S(1)} %get-tuple-element.178), channel_id=1, source_target_pairs={{0,4},{4,0},{8,12},{12,8},{16,20},{20,16},{24,28},{28,24},{1,5},{5... | collective-permute-start | bytes 737288 | tf_op jit(solution)/shard_map/ppermute | solution.py:27
  174.0 14.1 %collective-permute-start.31 = (bf16[240,512]{1,0:T(8,128)(2,1)S(1)}, bf16[240,512]{1,0:T(8,128)(2,1)S(1)}, u32[]{:S(2)}, u32[]{:S(2)}) collective-permute-start(bf16[240,512]{1,0:T(8,128)(2,1)S(1)} %get-tuple-element.177), channel_id=1, source_target_pairs={{0,6},{1,7},{2,4},{3,5},{4,2},{5,3},{6,0},{7,1},{8,14},{9,15},{10,... | collective-permute-start | bytes 737288 | tf_op jit(solution)/shard_map/ppermute | solution.py:957
  175.2 12.9 %collective-permute-start.29 = (bf16[288,512]{1,0:T(8,128)(2,1)S(1)}, bf16[288,512]{1,0:T(8,128)(2,1)S(1)}, u32[]{:S(2)}, u32[]{:S(2)}) collective-permute-start(bf16[288,512]{1,0:T(8,128)(2,1)S(1)} %fusion.11), channel_id=1, source_target_pairs={{0,2},{1,3},{2,0},{3,1},{4,6},{5,7},{6,4},{7,5},{8,10},{9,11},{10,... | collective-permute-start | bytes 884744 | tf_op jit(solution)/shard_map/ppermute | solution.py:27
  188.5 9.5 %collective-permute-start.33 = (bf16[240,512]{1,0:T(8,128)(2,1)S(1)}, bf16[240,512]{1,0:T(8,128)(2,1)S(1)}, u32[]{:S(2)}, u32[]{:S(2)}) collective-permute-start(bf16[240,512]{1,0:T(8,128)(2,1)S(1)} %pad_maximum_fusion.10), channel_id=1, source_target_pairs={{0,8},{4,12},{8,0},{12,4},{16,24},{20,28},{24,16},{28,20},{1,9},{5... | collective-permute-start | bytes 737288 | tf_op jit(solution)/shard_map/ppermute | solution.py:27
  188.7 9.3 %collective-permute-start.34 = (bf16[208,512]{1,0:T(8,128)(2,1)S(1)}, bf16[208,512]{1,0:T(8,128)(2,1)S(1)}, u32[]{:S(2)}, u32[]{:S(2)}) collective-permute-start(bf16[208,512]{1,0:T(8,128)(2,1)S(1)} %fusion.9), channel_id=1, source_target_pairs={{0,16},{4,20},{8,24},{12,28},{24,8},{28,12},{1,17},{5,21},{9,25},{... | collective-permute-start | bytes 638984 | tf_op jit(solution)/shard_map/ppermute | solution.py:969
  198.1 5.5 %collective-permute-start.35 = (f32[24,512]{1,0:T(8,128)S(1)}, f32[24,512]{1,0:T(8,128)S(1)}, u32[]{:S(2)}, u32[]{:S(2)}) collective-permute-start(f32[24,512]{1,0:T(8,128)S(1)} %maximum_add_fusion.2), channel_id=1, source_target_pairs={{0,16},{4,20},{8,24},{12,28},{16,0},{20,4},{24,8},{28,12},{1,17},{... | collective-permute-start | bytes 147464 | tf_op jit(solution)/shard_map/ppermute | solution.py:27
  201.6 9.2 %collective-permute-start.36 = (bf16[208,512]{1,0:T(8,128)(2,1)S(1)}, bf16[208,512]{1,0:T(8,128)(2,1)S(1)}, u32[]{:S(2)}, u32[]{:S(2)}) collective-permute-start(bf16[208,512]{1,0:T(8,128)(2,1)S(1)} %fusion.5), channel_id=1, source_target_pairs={{16,0},{20,4},{17,1},{21,5},{18,2},{22,6},{19,3},{23,7}} | collective-permute-start | bytes 638984 | tf_op jit(solution)/shard_map/ppermute | solution.py:998
  (36 other events, 235.5 us)

commit v3 on v2

--- a/solution.py
+++ b/solution.py
@@ -216,14 +216,13 @@
     w_ref,
     key_far_ref,
     value_far_ref,
-    causal_ref,
     query_ref,
     key_ref,
     value_ref,
     mixed_ref,
     probs_ref,
 ):
-    columns = causal_ref.shape[0]
+    columns = block_ref.shape[0] // rows_per_step
     far = key_far_ref.shape[0]
     width = block_ref.shape[1]
     head_width = width // HEADS
@@ -234,6 +233,9 @@
         ref[...] = dot(attn_in, w_ref[:, i * width : (i + 1) * width]).astype(HALF)
     first_half = lax.broadcasted_iota(jnp.int32, (columns + far, LANES), 1) < head_width
     far_index = lax.broadcasted_iota(jnp.int32, (far, columns), 0)
+    key_index = lax.broadcasted_iota(jnp.int32, (columns, columns), 0)
+    query_index = lax.broadcasted_iota(jnp.int32, (columns, columns), 1)
+    causal = jnp.where(key_index <= query_index, 0.0, NEGATIVE)
     keys = head_keys(rows_per_step, width)
     for start in range(0, len(keys), 4 * HEADS):
         group = keys[start : start + 4 * HEADS]
@@ -249,7 +251,7 @@
             )
             found = dot_rows(one_head, query_ref[tokens, lanes])
             scores[row, pair, half] = jnp.concatenate(
-                [found[:columns] + causal_ref[...], found[columns:] + far_bias], axis=0
+                [found[:columns] + causal, found[columns:] + far_bias], axis=0
             )
         for row, pair, half in group:
             found = scores.pop((row, pair, half))
@@ -300,14 +302,12 @@
     steps = local_rows // rows_per_step
     first_step = first_image * steps
     size = rows_per_step * columns
-    position = jnp.arange(columns)
-    causal = jnp.where(position[:, None] <= position[None, :], 0.0, NEGATIVE).astype(SINGLE)
     block = pl.BlockSpec((size, width), lambda i, _: (first_step + i, 0))
     far_block = pl.BlockSpec((None, far, width), lambda i, _: (first_image + i // steps, 0, 0))
     probs_block = pl.BlockSpec(
         (rows_per_step, HEADS, columns + far, columns), lambda i, _: (first_step + i, 0, 0, 0)
     )
-    inputs = [block_in, gain, w_qkv, key_far, value_far, causal]
+    inputs = [block_in, gain, w_qkv, key_far, value_far]
     kept, kept_specs, aliases = kept_arrays(previous, 1 + len(inputs))
     low = jax.ShapeDtypeStruct((tokens, width), HALF)
     part = count * tokens // images
@@ -329,7 +329,6 @@
                 whole_block((width, 3 * width)),
                 far_block,
                 far_block,
-                whole_block((columns, columns)),
             ]
             + kept_specs,
             out_specs=[block] * 4 + [probs_block],
@@ -867,17 +866,17 @@
     def _():
         assemble(flat_ref, list(zip(piece_refs, masks)), here, block, 0)
 
-    for ref, mask in zip(piece_refs, masks):
-        shown_ref[here ^ mask] = ref[rows:]
+    for own_ref, ref, mask in zip(own_refs, piece_refs, masks):
+        shown_ref[here ^ mask, : 2 * TAIL] = ref[rows:]
+        shown_ref[here ^ mask, 2 * TAIL :] = own_ref[rows:]
     flat_ref[3 * width :] += shown_ref[0, :TAIL]
     for i in range(3):
         w_ref[:, i * width : (i + 1) * width] = flat_ref[TAIL + i * width : TAIL + (i + 1) * width]
-    own_rows = images * local_rows
     total = jnp.zeros((2, width), SINGLE)
     for j in range(8):
-        total = total + whole_of(shown_ref[j, TAIL:])[own_rows : own_rows + 2]
+        total = total + whole_of(shown_ref[j, TAIL : 2 * TAIL].astype(SINGLE)[:6])
     for j in range(4):
-        means = whole_of(shown_ref[lax.div(here, 4) * 4 + j, TAIL:])
+        means = whole_of(shown_ref[lax.div(here, 4) * 4 + j, 2 * TAIL :])
         for image in range(images):
             start = (image * 4 + j) * local_rows
             means_ref[start : start + local_rows] = means[image * local_rows : (image + 1) * local_rows]
@@ -920,7 +919,7 @@
         + [jax.ShapeDtypeStruct((1, width), SINGLE)] * 7,
         scratch_shapes=[
             pltpu.VMEM((TAIL + 3 * width, width), HALF),
-            pltpu.VMEM((8, 4 * TAIL, width), HALF),
+            pltpu.VMEM((8, 5 * TAIL, width), HALF),
             pltpu.VMEM((far, width), SINGLE),
         ],
         compiler_params=pltpu.CompilerParams(vmem_limit_bytes=VMEM_BYTES),
@@ -1051,11 +1050,13 @@
         piece_rows = block + TAIL
         own = jnp.concatenate([own] + parts_of(sums) + [jnp.zeros((TAIL - 6, width), HALF)])
         over_far = swap_far(own)
-        own_rows_only = own[:piece_rows]
-        own_near = across_plane([own_rows_only] * 3)
+        means = row_means.reshape(-1, width)
+        spare = jnp.zeros((TAIL - means.shape[0], width), SINGLE)
+        own_shown = jnp.concatenate([own[:piece_rows]] + parts_of(jnp.concatenate([means, spare])))
+        own_near = across_plane([own_shown] * 3)
         over_near = swap_near(jnp.stack([own, over_far]))
         over_near, own_near = together(over_near, own_near)
-        own_pieces = plane_pieces(own_rows_only, own_near)
+        own_pieces = plane_pieces(own_shown, own_near)
         held = [own, over_near[0], over_far, over_near[1]]
         sums = [whole_of(array[piece_rows : piece_rows + 6]) for array in held]
         sums = (sums[0] + sums[1]) + (sums[2] + sums[3])
@@ -1064,9 +1065,7 @@
         def slot(i):
             return lax.dynamic_index_in_dim(held, z ^ i, 0, keepdims=False)
 
-        means = row_means.reshape(-1, width)
-        spare = jnp.zeros((TAIL - 2 - means.shape[0], width), SINGLE)
-        known = parts_of(jnp.concatenate([means, sums, spare]))
+        known = parts_of(sums) + [jnp.zeros((TAIL - 6, width), HALF)]
         first_slot = jnp.concatenate([slot(jnp.where(z == 0, 1, 0)), slot(1)[:TAIL]] + known)
         last_slots = jnp.stack([slot(i) for i in second_slots(z)])
         first_near, last_slots = together(across_plane([first_slot] * 3), last_slots)

time: 213 us -> 209 us (0.981)
  transfers between devices with their start and end apart: 37 -> 37, of which waited for: 15 -> 14; matrix products, arithmetic and copies ran while one was open for 4% -> 3% of each run, Pallas kernels for 27% -> 27%
where the time goes in v3:
time: 209 us
  Pallas kernels  105 us (50%)
  waiting for transfers between devices  43.6 us (21%)
  starting transfers between devices  39.9 us (19%)
  other arithmetic  13 us (6%)
  local copies, waits for them, and re-layouts  5.89 us (3%)
    pallas_call x1, Pallas kernels, feed_forward(): pl.pallas_call(functools.partial(feed_forward_kernel, 256, plan, masks, b...  48.3 us
    ppermute x30, waiting for transfers between devices, swap(): return lax.ppermute(value, axis, [(i, i ^ distance) for i in range(size)])  36 us
    ppermute x30, starting transfers between devices, swap(): return lax.ppermute(value, axis, [(i, i ^ distance) for i in range(size)])  27.4 us
    pallas_call x1, Pallas kernels, attention_backward(): pl.pallas_call(functools.partial(attention_backward_kernel, 1.0 / math.sq...  23.5 us
    pallas_call x1, Pallas kernels, attention_forward(): pl.pallas_call(body, grid_spec=pltpu.PrefetchScalarGridSpec(num_scalar_pr...  17.7 us
    pallas_call x1, Pallas kernels, input_grads(): pl.pallas_call(input_grad_kernel, grid=(tokens // size,), in_specs=[block...  11.4 us
    ppermute x1, starting transfers between devices, send_far(): lax.ppermute(value, 'img', [(i, i ^ 4) for i in range(lax.axis_size('img'...  5.95 us
    ppermute x5, starting transfers between devices, swap_both(): lax.ppermute(value, ('img', 'row'), [(i, i ^ 6) for i in range(size)])  5.26 us
  transfers between devices with their start and end apart: 37, of which 14 were waited for; matrix products, arithmetic and copies ran while one was open for 3% of the time, Pallas kernels for 27%

profile of v3, /device:TPU:0, one launch (start us, length us, event | category | flops | bytes accessed | tf_op | source)
XLA Modules:
  0.0 208.6 jit_solution(3551436311608181594)
XLA Ops:
  0.7 2.1 convert_reduce_fusion
  2.8 2.0 dynamic_update_slice.3
  5.2 4.1 %collective-permute-start = (bf16[224,512]{1,0:T(8,128)(2,1)S(1)}, bf16[224,512]{1,0:T(8,128)(2,1)S(1)}, u32[]{:S(2)}, u32[]{:S(2)}) collective-permute-start(bf16[224,512]{1,0:T(8,128)(2,1)S(1)} %concatenate.45), channel_id=1, source_target_pairs={{0,16},{4,20},{8,24},{12,28},{16,0},{20,4},{24,8},{28,12},{1,17},{... | collective-permute-start | bytes 688136 | tf_op jit(solution)/shard_map/ppermute | solution.py:27
  9.4 1.6 collective-permute-start.2
  10.9 1.5 collective-permute-start.3
  13.1 6.7 %collective-permute-done = bf16[224,512]{1,0:T(8,128)(2,1)S(1)} collective-permute-done((bf16[224,512]{1,0:T(8,128)(2,1)S(1)}, bf16[224,512]{1,0:T(8,128)(2,1)S(1)}, u32[]{:S(2)}, u32[]{:S(2)}) %collective-permute-start) | collective-permute-done | bytes 229408 | tf_op jit(solution)/shard_map/ppermute | solution.py:27
  20.7 3.3 %collective-permute-done.3.refs_2_.rest_2_ = bf16[256,512]{1,0:T(8,128)(2,1)S(1)} collective-permute-done((bf16[256,512]{1,0:T(8,128)(2,1)S(1)}, bf16[256,512]{1,0:T(8,128)(2,1)S(1)}, u32[]{:S(2)}, u32[]{:S(2)}) %collective-permute-start.3) | collective-permute-done | bytes 262176 | tf_op jit(solution)/shard_map/ppermute | solution.py:27
  24.0 7.6 %collective-permute-done.1 = bf16[2,224,512]{2,1,0:T(8,128)(2,1)S(1)} collective-permute-done((bf16[2,224,512]{2,1,0:T(8,128)(2,1)S(1)}, bf16[2,224,512]{2,1,0:T(8,128)(2,1)S(1)}, u32[]{:S(2)}, u32[]{:S(2)}) %collective-permute-start.1) | collective-permute-done | bytes 458784 | tf_op jit(solution)/shard_map/ppermute | solution.py:27
  32.2 1.3 collective-permute-start.5
  33.5 1.5 collective-permute-start.6
  36.3 5.0 %collective-permute-done.5.refs_9_.rest_9_ = bf16[240,512]{1,0:T(8,128)(2,1)} collective-permute-done((bf16[240,512]{1,0:T(8,128)(2,1)S(1)}, bf16[240,512]{1,0:T(8,128)(2,1)}, u32[]{:S(2)}, u32[]{:S(2)}) %collective-permute-start.5) | collective-permute-done | bytes 245792 | tf_op jit(solution)/shard_map/ppermute | solution.py:27
  41.2 3.6 %collective-permute-done.6.refs_10_.rest_10_ = bf16[240,512]{1,0:T(8,128)(2,1)} collective-permute-done((bf16[240,512]{1,0:T(8,128)(2,1)S(1)}, bf16[240,512]{1,0:T(8,128)(2,1)}, u32[]{:S(2)}, u32[]{:S(2)}) %collective-permute-start.6) | collective-permute-done | bytes 245792 | tf_op jit(solution)/shard_map/ppermute | solution.py:27
  46.7 1.5 collective-permute-start.10
  48.2 1.5 collective-permute-start.8
  51.0 3.8 %projection_weights.1 = (bf16[512,1536]{1,0:T(8,128)(2,1)}, bf16[48,512]{1,0:T(8,128)(2,1)}, bf16[48,512]{1,0:T(8,128)(2,1)}, f32[48,512]{1,0:T(8,128)}, bf16[48...) custom-call(s32[1]{0:T(128)} %bitcast.index_ref, ...), custom_call_target="tpu_custom_call" | custom-call | tf_op jit(solution)/shard_map/projection_weights/pallas_call | solution.py:906
  54.8 17.7 %attention_forward.1 = (bf16[2304,512]{1,0:T(8,128)(2,1)}, bf16[2304,512]{1,0:T(8,128)(2,1)}, bf16[2304,512]{1,0:T(8,128)(2,1)}, bf16[2304,512]{1,0:T(8,128)(2,1)}, bf16[12,8,208,192]{3,2,1,0:T(8,128)(2,1)}) custom-call(s32[1]{0:T(128)} %bitcast.11.refs_0_, bf16[2304,512]{1,0:T(8,128)(2,1)} %bitcast.74, f32[1,512]{1,0:T(1,128)} %get-tuple-element.87.refs_2_.rest_0_.gain_ref, ...), custom_call_target="tpu_custom_call" | custom-call | flops 5586812928 | bytes 21823488 | tf_op jit(solution)/shard_map/attention_forward/pallas_call | solution.py:321
  76.5 48.3 %feed_forward.1 = (bf16[2304,512]{1,0:T(8,128)(2,1)}, f32[2304,512]{1,0:T(8,128)}, bf16[2304,512]{1,0:T(8,128)(2,1)}, f32[1,512]{1,0:T(1,128)}, bf16[1,3,208,512...) custom-call(s32[1]{0:T(128)} %bitcast.index_ref, ...), custom_call_target="tpu_custom_call" | custom-call | flops 32614907904 | bytes 24903680 | tf_op jit(solution)/shard_map/feed_forward/pallas_call | solution.py:506
  125.3 4.7 %collective-permute-done.23 = bf16[4,3,208,512]{3,2,1,0:T(8,128)(2,1)S(1)} collective-permute-done((bf16[4,3,208,512]{3,2,1,0:T(8,128)(2,1)}, bf16[4,3,208,512]{3,2,1,0:T(8,128)(2,1)S(1)}, u32[]{:S(2)}, u32[]{:S(2)}) %collective-permute-start.23) | collective-permute-done | bytes 2555936 | tf_op jit(solution)/shard_map/ppermute | solution.py:27
  129.9 3.2 %fusion.2 = (bf16[3,208,512]{2,1,0:T(8,128)(2,1)S(1)}, bf16[3,208,512]{2,1,0:T(8,128)(2,1)S(1)}, bf16[3,208,512]{2,1,0:T(8,128)(2,1)}, f32[3,208,512]{2,1,0:T(8,128)S(1)}) fusion(bf16[1,3,208,512]{3,2,1,0:T(8,128)(2,1)} %get-tuple-element.110, bf16[4,3,208,512]{3,2,1,0:T(8,128)(2,1)S(1)} %collective-permute-done.23, ...), kind=kLoop, calls=%fused_computation.10 | loop fusion | flops 4792320 | bytes 8306688 | tf_op jit(solution)/shard_map/convert_element_type | solution.py:990
  135.2 1.4 collective-permute-start.28
  136.7 23.5 %attention_backward.1 = (bf16[2304,512]{1,0:T(8,128)(2,1)}, bf16[2304,512]{1,0:T(8,128)(2,1)}, bf16[2304,512]{1,0:T(8,128)(2,1)}, f32[72,512]{1,0:T(8,128)}, bf1...) custom-call(s32[1]{0:T(128)} %bitcast.index_ref, ...), custom_call_target="tpu_custom_call" | custom-call | flops 7549747200 | bytes 26542080 | tf_op jit(solution)/shard_map/attention_backward/pallas_call | solution.py:739
  160.7 2.3 %collective-permute-done.25 = f32[72,512]{1,0:T(8,128)S(1)} collective-permute-done((f32[72,512]{1,0:T(8,128)}, f32[72,512]{1,0:T(8,128)S(1)}, u32[]{:S(2)}, u32[]{:S(2)}) %collective-permute-start.25) | collective-permute-done | bytes 147488 | tf_op jit(solution)/shard_map/ppermute | solution.py:27
  164.8 1.8 add_add_fusion
  167.0 2.5 %collective-permute-start.32 = (bf16[2,208,512]{2,1,0:T(8,128)(2,1)S(1)}, bf16[2,208,512]{2,1,0:T(8,128)(2,1)S(1)}, u32[]{:S(2)}, u32[]{:S(2)}) collective-permute-start(bf16[2,208,512]{2,1,0:T(8,128)(2,1)S(1)} %pad_maximum_fusion.3), channel_id=1, source_target_pairs={{0,8},{4,12},{8,0},{12,4},{16,24},{20,28},{24,16},{28,20},{1,9},{5... | collective-permute-start | bytes 1277960 | tf_op jit(solution)/shard_map/ppermute | solution.py:27
  171.8 1.5 collective-permute-start.29
  173.3 11.4 %input_grads.1 = f32[2304,512]{1,0:T(8,128)} custom-call(bf16[2304,512]{1,0:T(8,128)(2,1)} %bitcast.77, f32[1,512]{1,0:T(1,128)} %get-tuple-element.87.refs_2_.rest_0_.gain_ref, bf16[2304,512]{1,0:T(8,128)(2,1)} %get-tuple-element.137.query_grad_ref, bf16[2304,512]{1,0:T(8,128)(2,1)} %get-tuple-element.138.key_grad_ref, ...), custom_call_target="tpu_custom_call" | custom-call | flops 3623878656 | bytes 18874368 | tf_op jit(solution)/shard_map/input_grads/pallas_call | solution.py:794
  185.3 6.0 %collective-permute-start.34 = (bf16[208,512]{1,0:T(8,128)(2,1)S(1)}, bf16[208,512]{1,0:T(8,128)(2,1)S(1)}, u32[]{:S(2)}, u32[]{:S(2)}) collective-permute-start(bf16[208,512]{1,0:T(8,128)(2,1)S(1)} %fusion.9), channel_id=1, source_target_pairs={{0,16},{4,20},{8,24},{12,28},{24,8},{28,12},{1,17},{5,21},{9,25},{... | collective-permute-start | bytes 638984 | tf_op jit(solution)/shard_map/ppermute | solution.py:968
  191.2 3.3 %collective-permute-done.34 = bf16[208,512]{1,0:T(8,128)(2,1)S(1)} collective-permute-done((bf16[208,512]{1,0:T(8,128)(2,1)S(1)}, bf16[208,512]{1,0:T(8,128)(2,1)S(1)}, u32[]{:S(2)}, u32[]{:S(2)}) %collective-permute-start.34) | collective-permute-done | bytes 213024 | tf_op jit(solution)/shard_map/ppermute | solution.py:968
  194.6 3.4 %collective-permute-start.35 = (f32[24,512]{1,0:T(8,128)S(1)}, f32[24,512]{1,0:T(8,128)S(1)}, u32[]{:S(2)}, u32[]{:S(2)}) collective-permute-start(f32[24,512]{1,0:T(8,128)S(1)} %maximum_add_fusion.2), channel_id=1, source_target_pairs={{0,16},{4,20},{8,24},{12,28},{16,0},{20,4},{24,8},{28,12},{1,17},{... | collective-permute-start | bytes 147464 | tf_op jit(solution)/shard_map/ppermute | solution.py:27
  198.1 1.3 collective-permute-start.36
  201.0 2.8 %broadcast_add_fusion = f32[3,4,192,512]{3,2,1,0:T(8,128)} fusion(f32[3,4,192,512]{3,2,1,0:T(8,128)S(1)} %bitcast.73, f32[3,4,512]{2,1,0:T(4,128)S(1)} %multiply_multiply_fusion), kind=kLoop, calls=%fused_computation.1 | loop fusion | flops 1179648 | bytes 9461760 | tf_op jit(solution)/shard_map/add | solution.py:1210
  203.8 3.4 %collective-permute-done.36 = bf16[208,512]{1,0:T(8,128)(2,1)S(1)} collective-permute-done((bf16[208,512]{1,0:T(8,128)(2,1)S(1)}, bf16[208,512]{1,0:T(8,128)(2,1)S(1)}, u32[]{:S(2)}, u32[]{:S(2)}) %collective-permute-start.36) | collective-permute-done | bytes 213024 | tf_op jit(solution)/shard_map/ppermute | solution.py:997
  (169 shorter events, 21.4 us)
Async XLA Ops:
  5.2 14.6 %collective-permute-start = (bf16[224,512]{1,0:T(8,128)(2,1)S(1)}, bf16[224,512]{1,0:T(8,128)(2,1)S(1)}, u32[]{:S(2)}, u32[]{:S(2)}) collective-permute-start(bf16[224,512]{1,0:T(8,128)(2,1)S(1)} %concatenate.45), channel_id=1, source_target_pairs={{0,16},{4,20},{8,24},{12,28},{16,0},{20,4},{24,8},{28,12},{1,17},{... | collective-permute-start | bytes 688136 | tf_op jit(solution)/shard_map/ppermute | solution.py:27
  9.4 11.3 %collective-permute-start.2 = (bf16[256,512]{1,0:T(8,128)(2,1)S(1)}, bf16[256,512]{1,0:T(8,128)(2,1)S(1)}, u32[]{:S(2)}, u32[]{:S(2)}) collective-permute-start(bf16[256,512]{1,0:T(8,128)(2,1)S(1)} %pad_maximum_fusion.10.refs_0_.rest_0_), channel_id=1, source_target_pairs={{0,2},{1,3},{2,0},{3,1},{4,6},{5,7},{6,4},{7,5},{8,10},{9,11},{10,... | collective-permute-start | bytes 786440 | tf_op jit(solution)/shard_map/ppermute | solution.py:27
  10.9 13.1 %collective-permute-start.3 = (bf16[256,512]{1,0:T(8,128)(2,1)S(1)}, bf16[256,512]{1,0:T(8,128)(2,1)S(1)}, u32[]{:S(2)}, u32[]{:S(2)}) collective-permute-start(bf16[256,512]{1,0:T(8,128)(2,1)S(1)} %pad_maximum_fusion.10.refs_0_.rest_0_), channel_id=1, source_target_pairs={{0,4},{4,0},{8,12},{12,8},{16,20},{20,16},{24,28},{28,24},{1,5},{5... | collective-permute-start | bytes 786440 | tf_op jit(solution)/shard_map/ppermute | solution.py:27
  12.4 11.6 %collective-permute-start.4 = (bf16[256,512]{1,0:T(8,128)(2,1)S(1)}, bf16[256,512]{1,0:T(8,128)(2,1)S(1)}, u32[]{:S(2)}, u32[]{:S(2)}) collective-permute-start(bf16[256,512]{1,0:T(8,128)(2,1)S(1)} %pad_maximum_fusion.10.refs_0_.rest_0_), channel_id=1, source_target_pairs={{0,6},{1,7},{2,4},{3,5},{4,2},{5,3},{6,0},{7,1},{8,14},{9,15},{10,... | collective-permute-start | bytes 786440 | tf_op jit(solution)/shard_map/ppermute | solution.py:956
  19.9 11.8 %collective-permute-start.1 = (bf16[2,224,512]{2,1,0:T(8,128)(2,1)S(1)}, bf16[2,224,512]{2,1,0:T(8,128)(2,1)S(1)}, u32[]{:S(2)}, u32[]{:S(2)}) collective-permute-start(bf16[2,224,512]{2,1,0:T(8,128)(2,1)S(1)} %pad_maximum_fusion.1), channel_id=1, source_target_pairs={{0,8},{4,12},{8,0},{12,4},{16,24},{20,28},{24,16},{28,20},{1,9},{5... | collective-permute-start | bytes 1376264 | tf_op jit(solution)/shard_map/ppermute | solution.py:27
  32.2 9.0 %collective-permute-start.5 = (bf16[240,512]{1,0:T(8,128)(2,1)S(1)}, bf16[240,512]{1,0:T(8,128)(2,1)}, u32[]{:S(2)}, u32[]{:S(2)}) collective-permute-start(bf16[240,512]{1,0:T(8,128)(2,1)S(1)} %concatenate.49.refs_8_.rest_8_), channel_id=1, source_target_pairs={{0,2},{1,3},{2,0},{3,1},{4,6},{5,7},{6,4},{7,5},{8,10},{9,11},{10,... | collective-permute-start | bytes 737288 | tf_op jit(solution)/shard_map/ppermute | solution.py:27
  33.5 11.3 %collective-permute-start.6 = (bf16[240,512]{1,0:T(8,128)(2,1)S(1)}, bf16[240,512]{1,0:T(8,128)(2,1)}, u32[]{:S(2)}, u32[]{:S(2)}) collective-permute-start(bf16[240,512]{1,0:T(8,128)(2,1)S(1)} %concatenate.49.refs_8_.rest_8_), channel_id=1, source_target_pairs={{0,4},{4,0},{8,12},{12,8},{16,20},{20,16},{24,28},{28,24},{1,5},{5... | collective-permute-start | bytes 737288 | tf_op jit(solution)/shard_map/ppermute | solution.py:27
  35.1 9.8 %collective-permute-start.7 = (bf16[240,512]{1,0:T(8,128)(2,1)S(1)}, bf16[240,512]{1,0:T(8,128)(2,1)}, u32[]{:S(2)}, u32[]{:S(2)}) collective-permute-start(bf16[240,512]{1,0:T(8,128)(2,1)S(1)} %concatenate.49.refs_8_.rest_8_), channel_id=1, source_target_pairs={{0,6},{1,7},{2,4},{3,5},{4,2},{5,3},{6,0},{7,1},{8,14},{9,15},{10,... | collective-permute-start | bytes 737288 | tf_op jit(solution)/shard_map/ppermute | solution.py:956
  35.8 9.7 %collective-permute-start.11 = (bf16[256,512]{1,0:T(8,128)(2,1)S(1)}, bf16[256,512]{1,0:T(8,128)(2,1)S(1)}, u32[]{:S(2)}, u32[]{:S(2)}) collective-permute-start(bf16[256,512]{1,0:T(8,128)(2,1)S(1)} %pad_maximum_fusion.10.refs_0_.rest_0_), channel_id=1, source_target_pairs={{0,1},{1,0},{2,3},{3,2},{4,5},{5,4},{6,7},{7,6},{8,9},{9,8},{10,11... | collective-permute-start | bytes 786440 | tf_op jit(solution)/shard_map/ppermute | solution.py:27
  35.8 10.3 %collective-permute-start.12 = (bf16[256,512]{1,0:T(8,128)(2,1)S(1)}, bf16[256,512]{1,0:T(8,128)(2,1)S(1)}, u32[]{:S(2)}, u32[]{:S(2)}) collective-permute-start(bf16[256,512]{1,0:T(8,128)(2,1)S(1)} %collective-permute-done.2.refs_1_.rest_1_), channel_id=1, source_target_pairs={{0,1},{1,0},{2,3},{3,2},{4,5},{5,4},{6,7},{7,6},{8,9},{9,8},{10,11... | collective-permute-start | bytes 786440 | tf_op jit(solution)/shard_map/ppermute | solution.py:27
  41.2 4.4 %collective-permute-start.15 = (bf16[240,512]{1,0:T(8,128)(2,1)S(1)}, bf16[240,512]{1,0:T(8,128)(2,1)S(1)}, u32[]{:S(2)}, u32[]{:S(2)}) collective-permute-start(bf16[240,512]{1,0:T(8,128)(2,1)S(1)} %concatenate.49.refs_8_.rest_8_), channel_id=1, source_target_pairs={{0,1},{1,0},{2,3},{3,2},{4,5},{5,4},{6,7},{7,6},{8,9},{9,8},{10,11... | collective-permute-start | bytes 737288 | tf_op jit(solution)/shard_map/ppermute | solution.py:27
  44.9 3.3 %collective-permute-start.14 = (bf16[256,512]{1,0:T(8,128)(2,1)S(1)}, bf16[256,512]{1,0:T(8,128)(2,1)}, u32[]{:S(2)}, u32[]{:S(2)}) collective-permute-start(bf16[256,512]{1,0:T(8,128)(2,1)S(1)} %collective-permute-done.4.refs_3_.rest_3_), channel_id=1, source_target_pairs={{0,1},{1,0},{2,3},{3,2},{4,5},{5,4},{6,7},{7,6},{8,9},{9,8},{10,11... | collective-permute-start | bytes 786440 | tf_op jit(solution)/shard_map/ppermute | solution.py:27
  45.5 4.3 %collective-permute-start.16 = (bf16[240,512]{1,0:T(8,128)(2,1)}, bf16[240,512]{1,0:T(8,128)(2,1)S(1)}, u32[]{:S(2)}, u32[]{:S(2)}) collective-permute-start(bf16[240,512]{1,0:T(8,128)(2,1)} %collective-permute-done.5.refs_9_.rest_9_), channel_id=1, source_target_pairs={{0,1},{1,0},{2,3},{3,2},{4,5},{5,4},{6,7},{7,6},{8,9},{9,8},{10,11... | collective-permute-start | bytes 737288 | tf_op jit(solution)/shard_map/ppermute | solution.py:27
  45.6 4.6 %collective-permute-start.17 = (bf16[240,512]{1,0:T(8,128)(2,1)}, bf16[240,512]{1,0:T(8,128)(2,1)S(1)}, u32[]{:S(2)}, u32[]{:S(2)}) collective-permute-start(bf16[240,512]{1,0:T(8,128)(2,1)} %collective-permute-done.6.refs_10_.rest_10_), channel_id=1, source_target_pairs={{0,1},{1,0},{2,3},{3,2},{4,5},{5,4},{6,7},{7,6},{8,9},{9,8},{10,11... | collective-permute-start | bytes 737288 | tf_op jit(solution)/shard_map/ppermute | solution.py:27
  46.4 3.9 %collective-permute-start.18 = (bf16[240,512]{1,0:T(8,128)(2,1)}, bf16[240,512]{1,0:T(8,128)(2,1)S(1)}, u32[]{:S(2)}, u32[]{:S(2)}) collective-permute-start(bf16[240,512]{1,0:T(8,128)(2,1)} %collective-permute-done.7.refs_11_.rest_11_), channel_id=1, source_target_pairs={{0,1},{1,0},{2,3},{3,2},{4,5},{5,4},{6,7},{7,6},{8,9},{9,8},{10,11... | collective-permute-start | bytes 737288 | tf_op jit(solution)/shard_map/ppermute | solution.py:27
  46.7 25.8 %collective-permute-start.10 = (bf16[2,208,512]{2,1,0:T(8,128)(2,1)S(1)}, bf16[2,208,512]{2,1,0:T(8,128)(2,1)S(1)}, u32[]{:S(2)}, u32[]{:S(2)}) collective-permute-start(bf16[2,208,512]{2,1,0:T(8,128)(2,1)S(1)} %pad_maximum_fusion.2.rest_16_), channel_id=1, source_target_pairs={{0,6},{1,7},{2,4},{3,5},{4,2},{5,3},{6,0},{7,1},{8,14},{9,15},{10,... | collective-permute-start | bytes 1277960 | tf_op jit(solution)/shard_map/ppermute | solution.py:956
  48.2 24.4 %collective-permute-start.8 = (bf16[2,208,512]{2,1,0:T(8,128)(2,1)S(1)}, bf16[2,208,512]{2,1,0:T(8,128)(2,1)S(1)}, u32[]{:S(2)}, u32[]{:S(2)}) collective-permute-start(bf16[2,208,512]{2,1,0:T(8,128)(2,1)S(1)} %pad_maximum_fusion.2.rest_16_), channel_id=1, source_target_pairs={{0,2},{1,3},{2,0},{3,1},{4,6},{5,7},{6,4},{7,5},{8,10},{9,11},{10,... | collective-permute-start | bytes 1277960 | tf_op jit(solution)/shard_map/ppermute | solution.py:27
  49.7 22.9 %collective-permute-start.9 = (bf16[2,208,512]{2,1,0:T(8,128)(2,1)S(1)}, bf16[2,208,512]{2,1,0:T(8,128)(2,1)S(1)}, u32[]{:S(2)}, u32[]{:S(2)}) collective-permute-start(bf16[2,208,512]{2,1,0:T(8,128)(2,1)S(1)} %pad_maximum_fusion.2.rest_16_), channel_id=1, source_target_pairs={{0,4},{4,0},{8,12},{12,8},{16,20},{20,16},{24,28},{28,24},{1,5},{5... | collective-permute-start | bytes 1277960 | tf_op jit(solution)/shard_map/ppermute | solution.py:27
  50.2 23.4 %collective-permute-start.19 = (bf16[2,208,512]{2,1,0:T(8,128)(2,1)S(1)}, bf16[2,208,512]{2,1,0:T(8,128)(2,1)S(1)}, u32[]{:S(2)}, u32[]{:S(2)}) collective-permute-start(bf16[2,208,512]{2,1,0:T(8,128)(2,1)S(1)} %pad_maximum_fusion.2.rest_16_), channel_id=1, source_target_pairs={{0,1},{1,0},{2,3},{3,2},{4,5},{5,4},{6,7},{7,6},{8,9},{9,8},{10,11... | collective-permute-start | bytes 1277960 | tf_op jit(solution)/shard_map/ppermute | solution.py:27
  124.8 5.1 %collective-permute-start.23 = (bf16[4,3,208,512]{3,2,1,0:T(8,128)(2,1)}, bf16[4,3,208,512]{3,2,1,0:T(8,128)(2,1)S(1)}, u32[]{:S(2)}, u32[]{:S(2)}) collective-permute-start(bf16[4,3,208,512]{3,2,1,0:T(8,128)(2,1)} %get-tuple-element.107), channel_id=1, source_target_pairs={{0,1},{1,0},{2,3},{3,2},{4,5},{5,4},{6,7},{7,6},{8,9},{9,8},{10,11... | collective-permute-start | bytes 7667720 | tf_op jit(solution)/shard_map/ppermute | solution.py:27
  133.2 30.8 %collective-permute-start.26 = (bf16[3,208,512]{2,1,0:T(8,128)(2,1)}, bf16[3,208,512]{2,1,0:T(8,128)(2,1)}, u32[]{:S(2)}, u32[]{:S(2)}) collective-permute-start(bf16[3,208,512]{2,1,0:T(8,128)(2,1)} %get-tuple-element.124), channel_id=1, source_target_pairs={{0,2},{1,3},{2,0},{3,1},{4,6},{5,7},{6,4},{7,5},{8,10},{9,11},{10,... | collective-permute-start | bytes 1916936 | tf_op jit(solution)/shard_map/ppermute | solution.py:27
  134.0 30.0 %collective-permute-start.27 = (bf16[3,208,512]{2,1,0:T(8,128)(2,1)S(1)}, bf16[3,208,512]{2,1,0:T(8,128)(2,1)}, u32[]{:S(2)}, u32[]{:S(2)}) collective-permute-start(bf16[3,208,512]{2,1,0:T(8,128)(2,1)S(1)} %get-tuple-element.125), channel_id=1, source_target_pairs={{0,4},{4,0},{8,12},{12,8},{16,20},{20,16},{24,28},{28,24},{1,5},{5... | collective-permute-start | bytes 1916936 | tf_op jit(solution)/shard_map/ppermute | solution.py:27
  135.2 29.6 %collective-permute-start.28 = (bf16[3,208,512]{2,1,0:T(8,128)(2,1)S(1)}, bf16[3,208,512]{2,1,0:T(8,128)(2,1)}, u32[]{:S(2)}, u32[]{:S(2)}) collective-permute-start(bf16[3,208,512]{2,1,0:T(8,128)(2,1)S(1)} %get-tuple-element.126), channel_id=1, source_target_pairs={{0,6},{1,7},{2,4},{3,5},{4,2},{5,3},{6,0},{7,1},{8,14},{9,15},{10,... | collective-permute-start | bytes 1916936 | tf_op jit(solution)/shard_map/ppermute | solution.py:956
  160.2 6.4 %collective-permute-start.24 = (bf16[4,1,208,512]{3,2,1,0:T(8,128)(2,1)}, bf16[4,1,208,512]{3,2,1,0:T(8,128)(2,1)S(1)}, u32[]{:S(2)}, u32[]{:S(2)}) collective-permute-start(bf16[4,1,208,512]{3,2,1,0:T(8,128)(2,1)} %get-tuple-element.118), channel_id=1, source_target_pairs={{0,1},{1,0},{2,3},{3,2},{4,5},{5,4},{6,7},{7,6},{8,9},{9,8},{10,11... | collective-permute-start | bytes 2555912 | tf_op jit(solution)/shard_map/ppermute | solution.py:27
  167.0 17.7 %collective-permute-start.32 = (bf16[2,208,512]{2,1,0:T(8,128)(2,1)S(1)}, bf16[2,208,512]{2,1,0:T(8,128)(2,1)S(1)}, u32[]{:S(2)}, u32[]{:S(2)}) collective-permute-start(bf16[2,208,512]{2,1,0:T(8,128)(2,1)S(1)} %pad_maximum_fusion.3), channel_id=1, source_target_pairs={{0,8},{4,12},{8,0},{12,4},{16,24},{20,28},{24,16},{28,20},{1,9},{5... | collective-permute-start | bytes 1277960 | tf_op jit(solution)/shard_map/ppermute | solution.py:27
  169.7 15.0 %collective-permute-start.30 = (bf16[240,512]{1,0:T(8,128)(2,1)S(1)}, bf16[240,512]{1,0:T(8,128)(2,1)S(1)}, u32[]{:S(2)}, u32[]{:S(2)}) collective-permute-start(bf16[240,512]{1,0:T(8,128)(2,1)S(1)} %get-tuple-element.181), channel_id=1, source_target_pairs={{0,4},{4,0},{8,12},{12,8},{16,20},{20,16},{24,28},{28,24},{1,5},{5... | collective-permute-start | bytes 737288 | tf_op jit(solution)/shard_map/ppermute | solution.py:27
  170.6 14.1 %collective-permute-start.31 = (bf16[240,512]{1,0:T(8,128)(2,1)S(1)}, bf16[240,512]{1,0:T(8,128)(2,1)S(1)}, u32[]{:S(2)}, u32[]{:S(2)}) collective-permute-start(bf16[240,512]{1,0:T(8,128)(2,1)S(1)} %get-tuple-element.180), channel_id=1, source_target_pairs={{0,6},{1,7},{2,4},{3,5},{4,2},{5,3},{6,0},{7,1},{8,14},{9,15},{10,... | collective-permute-start | bytes 737288 | tf_op jit(solution)/shard_map/ppermute | solution.py:956
  171.8 13.0 %collective-permute-start.29 = (bf16[288,512]{1,0:T(8,128)(2,1)S(1)}, bf16[288,512]{1,0:T(8,128)(2,1)S(1)}, u32[]{:S(2)}, u32[]{:S(2)}) collective-permute-start(bf16[288,512]{1,0:T(8,128)(2,1)S(1)} %fusion.10), channel_id=1, source_target_pairs={{0,2},{1,3},{2,0},{3,1},{4,6},{5,7},{6,4},{7,5},{8,10},{9,11},{10,... | collective-permute-start | bytes 884744 | tf_op jit(solution)/shard_map/ppermute | solution.py:27
  185.1 9.5 %collective-permute-start.33 = (bf16[240,512]{1,0:T(8,128)(2,1)S(1)}, bf16[240,512]{1,0:T(8,128)(2,1)S(1)}, u32[]{:S(2)}, u32[]{:S(2)}) collective-permute-start(bf16[240,512]{1,0:T(8,128)(2,1)S(1)} %pad_maximum_fusion.11), channel_id=1, source_target_pairs={{0,8},{4,12},{8,0},{12,4},{16,24},{20,28},{24,16},{28,20},{1,9},{5... | collective-permute-start | bytes 737288 | tf_op jit(solution)/shard_map/ppermute | solution.py:27
  185.3 9.3 %collective-permute-start.34 = (bf16[208,512]{1,0:T(8,128)(2,1)S(1)}, bf16[208,512]{1,0:T(8,128)(2,1)S(1)}, u32[]{:S(2)}, u32[]{:S(2)}) collective-permute-start(bf16[208,512]{1,0:T(8,128)(2,1)S(1)} %fusion.9), channel_id=1, source_target_pairs={{0,16},{4,20},{8,24},{12,28},{24,8},{28,12},{1,17},{5,21},{9,25},{... | collective-permute-start | bytes 638984 | tf_op jit(solution)/shard_map/ppermute | solution.py:968
  194.6 5.5 %collective-permute-start.35 = (f32[24,512]{1,0:T(8,128)S(1)}, f32[24,512]{1,0:T(8,128)S(1)}, u32[]{:S(2)}, u32[]{:S(2)}) collective-permute-start(f32[24,512]{1,0:T(8,128)S(1)} %maximum_add_fusion.2), channel_id=1, source_target_pairs={{0,16},{4,20},{8,24},{12,28},{16,0},{20,4},{24,8},{28,12},{1,17},{... | collective-permute-start | bytes 147464 | tf_op jit(solution)/shard_map/ppermute | solution.py:27
  198.1 9.2 %collective-permute-start.36 = (bf16[208,512]{1,0:T(8,128)(2,1)S(1)}, bf16[208,512]{1,0:T(8,128)(2,1)S(1)}, u32[]{:S(2)}, u32[]{:S(2)}) collective-permute-start(bf16[208,512]{1,0:T(8,128)(2,1)S(1)} %fusion.5), channel_id=1, source_target_pairs={{16,0},{20,4},{17,1},{21,5},{18,2},{22,6},{19,3},{23,7}} | collective-permute-start | bytes 638984 | tf_op jit(solution)/shard_map/ppermute | solution.py:997
  (32 other events, 195.4 us)

commit v4 on v3

--- a/solution.py
+++ b/solution.py
@@ -358,9 +358,11 @@
     return (activated, slope)
 
 
-def start_pieces(plan, flat_ref, outs, sems, index):
+def start_pieces(plan, flat_ref, outs, sems, index, wanted=lambda place: True):
     copies = []
     for i, (out, place, offset, rows) in enumerate(plan):
+        if not wanted(place):
+            continue
         source = flat_ref.at[pl.ds(pl.multiple_of(offset(index), TAIL), rows)]
         target = outs[out].at[place] if place else outs[out]
         copies.append(pltpu.make_async_copy(source, target, sems.at[i]))
@@ -463,6 +465,15 @@
 
     @pl.when(pl.program_id(0) == pl.num_programs(0) - 1)
     def _():
+        start = TAIL + width + hidden
+        for j in range(hidden // width):
+            turned = grad_outer_ref[:, j * width : (j + 1) * width].astype(HALF).T
+            flat_ref[start + j * width : start + (j + 1) * width] = turned
+
+        def behind(place):
+            return place != () and place[1] == 2
+
+        copies = start_pieces(plan, flat_ref, pieces, sems, index_ref[0], behind)
         flat_ref[:TAIL] = jnp.zeros((TAIL, width), HALF)
         flat_ref[TAIL : TAIL + width] = grad_out_ref[...].astype(HALF)
         mix = weave(groups, per)
@@ -474,11 +485,10 @@
             start = TAIL + width + c * groups * per
             woven = dot(mix, jnp.concatenate(parts, axis=0))
             flat_ref[start : start + groups * per] = woven.astype(HALF)
-        start = TAIL + width + hidden
-        for j in range(hidden // width):
-            turned = grad_outer_ref[:, j * width : (j + 1) * width].astype(HALF).T
-            flat_ref[start + j * width : start + (j + 1) * width] = turned
-        for copy in start_pieces(plan, flat_ref, pieces, sems, index_ref[0]):
+        copies += start_pieces(
+            plan, flat_ref, pieces, sems, index_ref[0], lambda place: not behind(place)
+        )
+        for copy in copies:
             copy.wait()
 
 

time: 209 us -> 209 us (level)
  no operation moved by 1% of the time
where the time goes in v4:
time: 209 us; the launch traced here: 208 us
  Pallas kernels  105 us (50%)
  waiting for transfers between devices  43.6 us (21%)
  starting transfers between devices  39.9 us (19%)
  other arithmetic  13 us (6%)
  local copies, waits for them, and re-layouts  5.89 us (3%)
    pallas_call x1, Pallas kernels, feed_forward(): pl.pallas_call(functools.partial(feed_forward_kernel, 256, plan, masks, b...  48.2 us
    ppermute x30, waiting for transfers between devices, swap(): return lax.ppermute(value, axis, [(i, i ^ distance) for i in range(size)])  36 us
    ppermute x30, starting transfers between devices, swap(): return lax.ppermute(value, axis, [(i, i ^ distance) for i in range(size)])  27.4 us
    pallas_call x1, Pallas kernels, attention_backward(): pl.pallas_call(functools.partial(attention_backward_kernel, 1.0 / math.sq...  23.5 us
    pallas_call x1, Pallas kernels, attention_forward(): pl.pallas_call(body, grid_spec=pltpu.PrefetchScalarGridSpec(num_scalar_pr...  17.7 us
    pallas_call x1, Pallas kernels, input_grads(): pl.pallas_call(input_grad_kernel, grid=(tokens // size,), in_specs=[block...  11.4 us
    ppermute x1, starting transfers between devices, send_far(): lax.ppermute(value, 'img', [(i, i ^ 4) for i in range(lax.axis_size('img'...  5.97 us
    ppermute x5, starting transfers between devices, swap_both(): lax.ppermute(value, ('img', 'row'), [(i, i ^ 6) for i in range(size)])  5.27 us
  transfers between devices with their start and end apart: 37, of which 14 were waited for; matrix products, arithmetic and copies ran while one was open for 3% of the time, Pallas kernels for 27%

profile of v4, /device:TPU:0, one launch (start us, length us, event | category | flops | bytes accessed | tf_op | source)
XLA Modules:
  0.0 208.5 jit_solution(14939518872163600060)
XLA Ops:
  0.7 2.1 convert_reduce_fusion
  2.8 2.0 dynamic_update_slice.3
  5.2 4.1 %collective-permute-start = (bf16[224,512]{1,0:T(8,128)(2,1)S(1)}, bf16[224,512]{1,0:T(8,128)(2,1)S(1)}, u32[]{:S(2)}, u32[]{:S(2)}) collective-permute-start(bf16[224,512]{1,0:T(8,128)(2,1)S(1)} %concatenate.45), channel_id=1, source_target_pairs={{0,16},{4,20},{8,24},{12,28},{16,0},{20,4},{24,8},{28,12},{1,17},{... | collective-permute-start | bytes 688136 | tf_op jit(solution)/shard_map/ppermute | solution.py:27
  9.4 1.6 collective-permute-start.2
  10.9 1.5 collective-permute-start.3
  13.1 6.7 %collective-permute-done = bf16[224,512]{1,0:T(8,128)(2,1)S(1)} collective-permute-done((bf16[224,512]{1,0:T(8,128)(2,1)S(1)}, bf16[224,512]{1,0:T(8,128)(2,1)S(1)}, u32[]{:S(2)}, u32[]{:S(2)}) %collective-permute-start) | collective-permute-done | bytes 229408 | tf_op jit(solution)/shard_map/ppermute | solution.py:27
  20.7 3.3 %collective-permute-done.3.refs_2_.rest_2_ = bf16[256,512]{1,0:T(8,128)(2,1)S(1)} collective-permute-done((bf16[256,512]{1,0:T(8,128)(2,1)S(1)}, bf16[256,512]{1,0:T(8,128)(2,1)S(1)}, u32[]{:S(2)}, u32[]{:S(2)}) %collective-permute-start.3) | collective-permute-done | bytes 262176 | tf_op jit(solution)/shard_map/ppermute | solution.py:27
  24.0 7.6 %collective-permute-done.1 = bf16[2,224,512]{2,1,0:T(8,128)(2,1)S(1)} collective-permute-done((bf16[2,224,512]{2,1,0:T(8,128)(2,1)S(1)}, bf16[2,224,512]{2,1,0:T(8,128)(2,1)S(1)}, u32[]{:S(2)}, u32[]{:S(2)}) %collective-permute-start.1) | collective-permute-done | bytes 458784 | tf_op jit(solution)/shard_map/ppermute | solution.py:27
  32.2 1.3 collective-permute-start.5
  33.5 1.5 collective-permute-start.6
  36.3 5.0 %collective-permute-done.5.refs_9_.rest_9_ = bf16[240,512]{1,0:T(8,128)(2,1)} collective-permute-done((bf16[240,512]{1,0:T(8,128)(2,1)S(1)}, bf16[240,512]{1,0:T(8,128)(2,1)}, u32[]{:S(2)}, u32[]{:S(2)}) %collective-permute-start.5) | collective-permute-done | bytes 245792 | tf_op jit(solution)/shard_map/ppermute | solution.py:27
  41.2 3.6 %collective-permute-done.6.refs_10_.rest_10_ = bf16[240,512]{1,0:T(8,128)(2,1)} collective-permute-done((bf16[240,512]{1,0:T(8,128)(2,1)S(1)}, bf16[240,512]{1,0:T(8,128)(2,1)}, u32[]{:S(2)}, u32[]{:S(2)}) %collective-permute-start.6) | collective-permute-done | bytes 245792 | tf_op jit(solution)/shard_map/ppermute | solution.py:27
  46.7 1.5 collective-permute-start.10
  48.2 1.5 collective-permute-start.8
  51.0 3.8 %projection_weights.1 = (bf16[512,1536]{1,0:T(8,128)(2,1)}, bf16[48,512]{1,0:T(8,128)(2,1)}, bf16[48,512]{1,0:T(8,128)(2,1)}, f32[48,512]{1,0:T(8,128)}, bf16[48...) custom-call(s32[1]{0:T(128)} %bitcast.index_ref, ...), custom_call_target="tpu_custom_call" | custom-call | tf_op jit(solution)/shard_map/projection_weights/pallas_call | solution.py:916
  54.8 17.7 %attention_forward.1 = (bf16[2304,512]{1,0:T(8,128)(2,1)}, bf16[2304,512]{1,0:T(8,128)(2,1)}, bf16[2304,512]{1,0:T(8,128)(2,1)}, bf16[2304,512]{1,0:T(8,128)(2,1)}, bf16[12,8,208,192]{3,2,1,0:T(8,128)(2,1)}) custom-call(s32[1]{0:T(128)} %bitcast.11.refs_0_, bf16[2304,512]{1,0:T(8,128)(2,1)} %bitcast.74, f32[1,512]{1,0:T(1,128)} %get-tuple-element.87.refs_2_.rest_0_.gain_ref, ...), custom_call_target="tpu_custom_call" | custom-call | flops 5586812928 | bytes 21823488 | tf_op jit(solution)/shard_map/attention_forward/pallas_call | solution.py:321
  76.5 48.2 %feed_forward.1 = (bf16[2304,512]{1,0:T(8,128)(2,1)}, f32[2304,512]{1,0:T(8,128)}, bf16[2304,512]{1,0:T(8,128)(2,1)}, f32[1,512]{1,0:T(1,128)}, bf16[1,3,208,512...) custom-call(s32[1]{0:T(128)} %bitcast.index_ref, ...), custom_call_target="tpu_custom_call" | custom-call | flops 32614907904 | bytes 24903680 | tf_op jit(solution)/shard_map/feed_forward/pallas_call | solution.py:516
  125.1 4.7 %collective-permute-done.23 = bf16[4,3,208,512]{3,2,1,0:T(8,128)(2,1)S(1)} collective-permute-done((bf16[4,3,208,512]{3,2,1,0:T(8,128)(2,1)}, bf16[4,3,208,512]{3,2,1,0:T(8,128)(2,1)S(1)}, u32[]{:S(2)}, u32[]{:S(2)}) %collective-permute-start.23) | collective-permute-done | bytes 2555936 | tf_op jit(solution)/shard_map/ppermute | solution.py:27
  129.8 3.2 %fusion.2 = (bf16[3,208,512]{2,1,0:T(8,128)(2,1)S(1)}, bf16[3,208,512]{2,1,0:T(8,128)(2,1)S(1)}, bf16[3,208,512]{2,1,0:T(8,128)(2,1)}, f32[3,208,512]{2,1,0:T(8,128)S(1)}) fusion(bf16[1,3,208,512]{3,2,1,0:T(8,128)(2,1)} %get-tuple-element.110, bf16[4,3,208,512]{3,2,1,0:T(8,128)(2,1)S(1)} %collective-permute-done.23, ...), kind=kLoop, calls=%fused_computation.10 | loop fusion | flops 4792320 | bytes 8306688 | tf_op jit(solution)/shard_map/convert_element_type | solution.py:1000
  135.1 1.4 collective-permute-start.28
  136.5 23.5 %attention_backward.1 = (bf16[2304,512]{1,0:T(8,128)(2,1)}, bf16[2304,512]{1,0:T(8,128)(2,1)}, bf16[2304,512]{1,0:T(8,128)(2,1)}, f32[72,512]{1,0:T(8,128)}, bf1...) custom-call(s32[1]{0:T(128)} %bitcast.index_ref, ...), custom_call_target="tpu_custom_call" | custom-call | flops 7549747200 | bytes 26542080 | tf_op jit(solution)/shard_map/attention_backward/pallas_call | solution.py:749
  160.6 2.3 %collective-permute-done.25 = f32[72,512]{1,0:T(8,128)S(1)} collective-permute-done((f32[72,512]{1,0:T(8,128)}, f32[72,512]{1,0:T(8,128)S(1)}, u32[]{:S(2)}, u32[]{:S(2)}) %collective-permute-start.25) | collective-permute-done | bytes 147488 | tf_op jit(solution)/shard_map/ppermute | solution.py:27
  164.6 1.8 add_add_fusion
  166.9 2.5 %collective-permute-start.32 = (bf16[2,208,512]{2,1,0:T(8,128)(2,1)S(1)}, bf16[2,208,512]{2,1,0:T(8,128)(2,1)S(1)}, u32[]{:S(2)}, u32[]{:S(2)}) collective-permute-start(bf16[2,208,512]{2,1,0:T(8,128)(2,1)S(1)} %pad_maximum_fusion.3), channel_id=1, source_target_pairs={{0,8},{4,12},{8,0},{12,4},{16,24},{20,28},{24,16},{28,20},{1,9},{5... | collective-permute-start | bytes 1277960 | tf_op jit(solution)/shard_map/ppermute | solution.py:27
  171.6 1.5 collective-permute-start.29
  173.1 11.4 %input_grads.1 = f32[2304,512]{1,0:T(8,128)} custom-call(bf16[2304,512]{1,0:T(8,128)(2,1)} %bitcast.77, f32[1,512]{1,0:T(1,128)} %get-tuple-element.87.refs_2_.rest_0_.gain_ref, bf16[2304,512]{1,0:T(8,128)(2,1)} %get-tuple-element.137.query_grad_ref, bf16[2304,512]{1,0:T(8,128)(2,1)} %get-tuple-element.138.key_grad_ref, ...), custom_call_target="tpu_custom_call" | custom-call | flops 3623878656 | bytes 18874368 | tf_op jit(solution)/shard_map/input_grads/pallas_call | solution.py:804
  185.1 6.0 %collective-permute-start.34 = (bf16[208,512]{1,0:T(8,128)(2,1)S(1)}, bf16[208,512]{1,0:T(8,128)(2,1)S(1)}, u32[]{:S(2)}, u32[]{:S(2)}) collective-permute-start(bf16[208,512]{1,0:T(8,128)(2,1)S(1)} %fusion.9), channel_id=1, source_target_pairs={{0,16},{4,20},{8,24},{12,28},{24,8},{28,12},{1,17},{5,21},{9,25},{... | collective-permute-start | bytes 638984 | tf_op jit(solution)/shard_map/ppermute | solution.py:978
  191.1 3.3 %collective-permute-done.34 = bf16[208,512]{1,0:T(8,128)(2,1)S(1)} collective-permute-done((bf16[208,512]{1,0:T(8,128)(2,1)S(1)}, bf16[208,512]{1,0:T(8,128)(2,1)S(1)}, u32[]{:S(2)}, u32[]{:S(2)}) %collective-permute-start.34) | collective-permute-done | bytes 213024 | tf_op jit(solution)/shard_map/ppermute | solution.py:978
  194.5 3.4 %collective-permute-start.35 = (f32[24,512]{1,0:T(8,128)S(1)}, f32[24,512]{1,0:T(8,128)S(1)}, u32[]{:S(2)}, u32[]{:S(2)}) collective-permute-start(f32[24,512]{1,0:T(8,128)S(1)} %maximum_add_fusion.2), channel_id=1, source_target_pairs={{0,16},{4,20},{8,24},{12,28},{16,0},{20,4},{24,8},{28,12},{1,17},{... | collective-permute-start | bytes 147464 | tf_op jit(solution)/shard_map/ppermute | solution.py:27
  198.0 1.3 collective-permute-start.36
  200.9 2.8 %broadcast_add_fusion = f32[3,4,192,512]{3,2,1,0:T(8,128)} fusion(f32[3,4,192,512]{3,2,1,0:T(8,128)S(1)} %bitcast.73, f32[3,4,512]{2,1,0:T(4,128)S(1)} %multiply_multiply_fusion), kind=kLoop, calls=%fused_computation.1 | loop fusion | flops 1179648 | bytes 9461760 | tf_op jit(solution)/shard_map/add | solution.py:1220
  203.7 3.4 %collective-permute-done.36 = bf16[208,512]{1,0:T(8,128)(2,1)S(1)} collective-permute-done((bf16[208,512]{1,0:T(8,128)(2,1)S(1)}, bf16[208,512]{1,0:T(8,128)(2,1)S(1)}, u32[]{:S(2)}, u32[]{:S(2)}) %collective-permute-start.36) | collective-permute-done | bytes 213024 | tf_op jit(solution)/shard_map/ppermute | solution.py:1007
  (169 shorter events, 21.4 us)
Async XLA Ops:
  5.2 14.6 %collective-permute-start = (bf16[224,512]{1,0:T(8,128)(2,1)S(1)}, bf16[224,512]{1,0:T(8,128)(2,1)S(1)}, u32[]{:S(2)}, u32[]{:S(2)}) collective-permute-start(bf16[224,512]{1,0:T(8,128)(2,1)S(1)} %concatenate.45), channel_id=1, source_target_pairs={{0,16},{4,20},{8,24},{12,28},{16,0},{20,4},{24,8},{28,12},{1,17},{... | collective-permute-start | bytes 688136 | tf_op jit(solution)/shard_map/ppermute | solution.py:27
  9.4 11.3 %collective-permute-start.2 = (bf16[256,512]{1,0:T(8,128)(2,1)S(1)}, bf16[256,512]{1,0:T(8,128)(2,1)S(1)}, u32[]{:S(2)}, u32[]{:S(2)}) collective-permute-start(bf16[256,512]{1,0:T(8,128)(2,1)S(1)} %pad_maximum_fusion.10.refs_0_.rest_0_), channel_id=1, source_target_pairs={{0,2},{1,3},{2,0},{3,1},{4,6},{5,7},{6,4},{7,5},{8,10},{9,11},{10,... | collective-permute-start | bytes 786440 | tf_op jit(solution)/shard_map/ppermute | solution.py:27
  10.9 13.1 %collective-permute-start.3 = (bf16[256,512]{1,0:T(8,128)(2,1)S(1)}, bf16[256,512]{1,0:T(8,128)(2,1)S(1)}, u32[]{:S(2)}, u32[]{:S(2)}) collective-permute-start(bf16[256,512]{1,0:T(8,128)(2,1)S(1)} %pad_maximum_fusion.10.refs_0_.rest_0_), channel_id=1, source_target_pairs={{0,4},{4,0},{8,12},{12,8},{16,20},{20,16},{24,28},{28,24},{1,5},{5... | collective-permute-start | bytes 786440 | tf_op jit(solution)/shard_map/ppermute | solution.py:27
  12.4 11.6 %collective-permute-start.4 = (bf16[256,512]{1,0:T(8,128)(2,1)S(1)}, bf16[256,512]{1,0:T(8,128)(2,1)S(1)}, u32[]{:S(2)}, u32[]{:S(2)}) collective-permute-start(bf16[256,512]{1,0:T(8,128)(2,1)S(1)} %pad_maximum_fusion.10.refs_0_.rest_0_), channel_id=1, source_target_pairs={{0,6},{1,7},{2,4},{3,5},{4,2},{5,3},{6,0},{7,1},{8,14},{9,15},{10,... | collective-permute-start | bytes 786440 | tf_op jit(solution)/shard_map/ppermute | solution.py:966
  19.9 11.8 %collective-permute-start.1 = (bf16[2,224,512]{2,1,0:T(8,128)(2,1)S(1)}, bf16[2,224,512]{2,1,0:T(8,128)(2,1)S(1)}, u32[]{:S(2)}, u32[]{:S(2)}) collective-permute-start(bf16[2,224,512]{2,1,0:T(8,128)(2,1)S(1)} %pad_maximum_fusion.1), channel_id=1, source_target_pairs={{0,8},{4,12},{8,0},{12,4},{16,24},{20,28},{24,16},{28,20},{1,9},{5... | collective-permute-start | bytes 1376264 | tf_op jit(solution)/shard_map/ppermute | solution.py:27
  32.2 9.0 %collective-permute-start.5 = (bf16[240,512]{1,0:T(8,128)(2,1)S(1)}, bf16[240,512]{1,0:T(8,128)(2,1)}, u32[]{:S(2)}, u32[]{:S(2)}) collective-permute-start(bf16[240,512]{1,0:T(8,128)(2,1)S(1)} %concatenate.49.refs_8_.rest_8_), channel_id=1, source_target_pairs={{0,2},{1,3},{2,0},{3,1},{4,6},{5,7},{6,4},{7,5},{8,10},{9,11},{10,... | collective-permute-start | bytes 737288 | tf_op jit(solution)/shard_map/ppermute | solution.py:27
  33.5 11.3 %collective-permute-start.6 = (bf16[240,512]{1,0:T(8,128)(2,1)S(1)}, bf16[240,512]{1,0:T(8,128)(2,1)}, u32[]{:S(2)}, u32[]{:S(2)}) collective-permute-start(bf16[240,512]{1,0:T(8,128)(2,1)S(1)} %concatenate.49.refs_8_.rest_8_), channel_id=1, source_target_pairs={{0,4},{4,0},{8,12},{12,8},{16,20},{20,16},{24,28},{28,24},{1,5},{5... | collective-permute-start | bytes 737288 | tf_op jit(solution)/shard_map/ppermute | solution.py:27
  35.1 9.8 %collective-permute-start.7 = (bf16[240,512]{1,0:T(8,128)(2,1)S(1)}, bf16[240,512]{1,0:T(8,128)(2,1)}, u32[]{:S(2)}, u32[]{:S(2)}) collective-permute-start(bf16[240,512]{1,0:T(8,128)(2,1)S(1)} %concatenate.49.refs_8_.rest_8_), channel_id=1, source_target_pairs={{0,6},{1,7},{2,4},{3,5},{4,2},{5,3},{6,0},{7,1},{8,14},{9,15},{10,... | collective-permute-start | bytes 737288 | tf_op jit(solution)/shard_map/ppermute | solution.py:966
  35.8 9.7 %collective-permute-start.11 = (bf16[256,512]{1,0:T(8,128)(2,1)S(1)}, bf16[256,512]{1,0:T(8,128)(2,1)S(1)}, u32[]{:S(2)}, u32[]{:S(2)}) collective-permute-start(bf16[256,512]{1,0:T(8,128)(2,1)S(1)} %pad_maximum_fusion.10.refs_0_.rest_0_), channel_id=1, source_target_pairs={{0,1},{1,0},{2,3},{3,2},{4,5},{5,4},{6,7},{7,6},{8,9},{9,8},{10,11... | collective-permute-start | bytes 786440 | tf_op jit(solution)/shard_map/ppermute | solution.py:27
  35.8 10.3 %collective-permute-start.12 = (bf16[256,512]{1,0:T(8,128)(2,1)S(1)}, bf16[256,512]{1,0:T(8,128)(2,1)S(1)}, u32[]{:S(2)}, u32[]{:S(2)}) collective-permute-start(bf16[256,512]{1,0:T(8,128)(2,1)S(1)} %collective-permute-done.2.refs_1_.rest_1_), channel_id=1, source_target_pairs={{0,1},{1,0},{2,3},{3,2},{4,5},{5,4},{6,7},{7,6},{8,9},{9,8},{10,11... | collective-permute-start | bytes 786440 | tf_op jit(solution)/shard_map/ppermute | solution.py:27
  41.2 4.4 %collective-permute-start.15 = (bf16[240,512]{1,0:T(8,128)(2,1)S(1)}, bf16[240,512]{1,0:T(8,128)(2,1)S(1)}, u32[]{:S(2)}, u32[]{:S(2)}) collective-permute-start(bf16[240,512]{1,0:T(8,128)(2,1)S(1)} %concatenate.49.refs_8_.rest_8_), channel_id=1, source_target_pairs={{0,1},{1,0},{2,3},{3,2},{4,5},{5,4},{6,7},{7,6},{8,9},{9,8},{10,11... | collective-permute-start | bytes 737288 | tf_op jit(solution)/shard_map/ppermute | solution.py:27
  44.9 3.3 %collective-permute-start.14 = (bf16[256,512]{1,0:T(8,128)(2,1)S(1)}, bf16[256,512]{1,0:T(8,128)(2,1)}, u32[]{:S(2)}, u32[]{:S(2)}) collective-permute-start(bf16[256,512]{1,0:T(8,128)(2,1)S(1)} %collective-permute-done.4.refs_3_.rest_3_), channel_id=1, source_target_pairs={{0,1},{1,0},{2,3},{3,2},{4,5},{5,4},{6,7},{7,6},{8,9},{9,8},{10,11... | collective-permute-start | bytes 786440 | tf_op jit(solution)/shard_map/ppermute | solution.py:27
  45.5 4.3 %collective-permute-start.16 = (bf16[240,512]{1,0:T(8,128)(2,1)}, bf16[240,512]{1,0:T(8,128)(2,1)S(1)}, u32[]{:S(2)}, u32[]{:S(2)}) collective-permute-start(bf16[240,512]{1,0:T(8,128)(2,1)} %collective-permute-done.5.refs_9_.rest_9_), channel_id=1, source_target_pairs={{0,1},{1,0},{2,3},{3,2},{4,5},{5,4},{6,7},{7,6},{8,9},{9,8},{10,11... | collective-permute-start | bytes 737288 | tf_op jit(solution)/shard_map/ppermute | solution.py:27
  45.6 4.6 %collective-permute-start.17 = (bf16[240,512]{1,0:T(8,128)(2,1)}, bf16[240,512]{1,0:T(8,128)(2,1)S(1)}, u32[]{:S(2)}, u32[]{:S(2)}) collective-permute-start(bf16[240,512]{1,0:T(8,128)(2,1)} %collective-permute-done.6.refs_10_.rest_10_), channel_id=1, source_target_pairs={{0,1},{1,0},{2,3},{3,2},{4,5},{5,4},{6,7},{7,6},{8,9},{9,8},{10,11... | collective-permute-start | bytes 737288 | tf_op jit(solution)/shard_map/ppermute | solution.py:27
  46.4 3.9 %collective-permute-start.18 = (bf16[240,512]{1,0:T(8,128)(2,1)}, bf16[240,512]{1,0:T(8,128)(2,1)S(1)}, u32[]{:S(2)}, u32[]{:S(2)}) collective-permute-start(bf16[240,512]{1,0:T(8,128)(2,1)} %collective-permute-done.7.refs_11_.rest_11_), channel_id=1, source_target_pairs={{0,1},{1,0},{2,3},{3,2},{4,5},{5,4},{6,7},{7,6},{8,9},{9,8},{10,11... | collective-permute-start | bytes 737288 | tf_op jit(solution)/shard_map/ppermute | solution.py:27
  46.7 25.8 %collective-permute-start.10 = (bf16[2,208,512]{2,1,0:T(8,128)(2,1)S(1)}, bf16[2,208,512]{2,1,0:T(8,128)(2,1)S(1)}, u32[]{:S(2)}, u32[]{:S(2)}) collective-permute-start(bf16[2,208,512]{2,1,0:T(8,128)(2,1)S(1)} %pad_maximum_fusion.2.rest_16_), channel_id=1, source_target_pairs={{0,6},{1,7},{2,4},{3,5},{4,2},{5,3},{6,0},{7,1},{8,14},{9,15},{10,... | collective-permute-start | bytes 1277960 | tf_op jit(solution)/shard_map/ppermute | solution.py:966
  48.2 24.4 %collective-permute-start.8 = (bf16[2,208,512]{2,1,0:T(8,128)(2,1)S(1)}, bf16[2,208,512]{2,1,0:T(8,128)(2,1)S(1)}, u32[]{:S(2)}, u32[]{:S(2)}) collective-permute-start(bf16[2,208,512]{2,1,0:T(8,128)(2,1)S(1)} %pad_maximum_fusion.2.rest_16_), channel_id=1, source_target_pairs={{0,2},{1,3},{2,0},{3,1},{4,6},{5,7},{6,4},{7,5},{8,10},{9,11},{10,... | collective-permute-start | bytes 1277960 | tf_op jit(solution)/shard_map/ppermute | solution.py:27
  49.7 22.9 %collective-permute-start.9 = (bf16[2,208,512]{2,1,0:T(8,128)(2,1)S(1)}, bf16[2,208,512]{2,1,0:T(8,128)(2,1)S(1)}, u32[]{:S(2)}, u32[]{:S(2)}) collective-permute-start(bf16[2,208,512]{2,1,0:T(8,128)(2,1)S(1)} %pad_maximum_fusion.2.rest_16_), channel_id=1, source_target_pairs={{0,4},{4,0},{8,12},{12,8},{16,20},{20,16},{24,28},{28,24},{1,5},{5... | collective-permute-start | bytes 1277960 | tf_op jit(solution)/shard_map/ppermute | solution.py:27
  50.2 23.4 %collective-permute-start.19 = (bf16[2,208,512]{2,1,0:T(8,128)(2,1)S(1)}, bf16[2,208,512]{2,1,0:T(8,128)(2,1)S(1)}, u32[]{:S(2)}, u32[]{:S(2)}) collective-permute-start(bf16[2,208,512]{2,1,0:T(8,128)(2,1)S(1)} %pad_maximum_fusion.2.rest_16_), channel_id=1, source_target_pairs={{0,1},{1,0},{2,3},{3,2},{4,5},{5,4},{6,7},{7,6},{8,9},{9,8},{10,11... | collective-permute-start | bytes 1277960 | tf_op jit(solution)/shard_map/ppermute | solution.py:27
  124.7 5.1 %collective-permute-start.23 = (bf16[4,3,208,512]{3,2,1,0:T(8,128)(2,1)}, bf16[4,3,208,512]{3,2,1,0:T(8,128)(2,1)S(1)}, u32[]{:S(2)}, u32[]{:S(2)}) collective-permute-start(bf16[4,3,208,512]{3,2,1,0:T(8,128)(2,1)} %get-tuple-element.107), channel_id=1, source_target_pairs={{0,1},{1,0},{2,3},{3,2},{4,5},{5,4},{6,7},{7,6},{8,9},{9,8},{10,11... | collective-permute-start | bytes 7667720 | tf_op jit(solution)/shard_map/ppermute | solution.py:27
  133.0 30.8 %collective-permute-start.26 = (bf16[3,208,512]{2,1,0:T(8,128)(2,1)}, bf16[3,208,512]{2,1,0:T(8,128)(2,1)}, u32[]{:S(2)}, u32[]{:S(2)}) collective-permute-start(bf16[3,208,512]{2,1,0:T(8,128)(2,1)} %get-tuple-element.124), channel_id=1, source_target_pairs={{0,2},{1,3},{2,0},{3,1},{4,6},{5,7},{6,4},{7,5},{8,10},{9,11},{10,... | collective-permute-start | bytes 1916936 | tf_op jit(solution)/shard_map/ppermute | solution.py:27
  133.9 29.9 %collective-permute-start.27 = (bf16[3,208,512]{2,1,0:T(8,128)(2,1)S(1)}, bf16[3,208,512]{2,1,0:T(8,128)(2,1)}, u32[]{:S(2)}, u32[]{:S(2)}) collective-permute-start(bf16[3,208,512]{2,1,0:T(8,128)(2,1)S(1)} %get-tuple-element.125), channel_id=1, source_target_pairs={{0,4},{4,0},{8,12},{12,8},{16,20},{20,16},{24,28},{28,24},{1,5},{5... | collective-permute-start | bytes 1916936 | tf_op jit(solution)/shard_map/ppermute | solution.py:27
  135.1 29.6 %collective-permute-start.28 = (bf16[3,208,512]{2,1,0:T(8,128)(2,1)S(1)}, bf16[3,208,512]{2,1,0:T(8,128)(2,1)}, u32[]{:S(2)}, u32[]{:S(2)}) collective-permute-start(bf16[3,208,512]{2,1,0:T(8,128)(2,1)S(1)} %get-tuple-element.126), channel_id=1, source_target_pairs={{0,6},{1,7},{2,4},{3,5},{4,2},{5,3},{6,0},{7,1},{8,14},{9,15},{10,... | collective-permute-start | bytes 1916936 | tf_op jit(solution)/shard_map/ppermute | solution.py:966
  160.0 6.4 %collective-permute-start.24 = (bf16[4,1,208,512]{3,2,1,0:T(8,128)(2,1)}, bf16[4,1,208,512]{3,2,1,0:T(8,128)(2,1)S(1)}, u32[]{:S(2)}, u32[]{:S(2)}) collective-permute-start(bf16[4,1,208,512]{3,2,1,0:T(8,128)(2,1)} %get-tuple-element.118), channel_id=1, source_target_pairs={{0,1},{1,0},{2,3},{3,2},{4,5},{5,4},{6,7},{7,6},{8,9},{9,8},{10,11... | collective-permute-start | bytes 2555912 | tf_op jit(solution)/shard_map/ppermute | solution.py:27
  166.9 17.7 %collective-permute-start.32 = (bf16[2,208,512]{2,1,0:T(8,128)(2,1)S(1)}, bf16[2,208,512]{2,1,0:T(8,128)(2,1)S(1)}, u32[]{:S(2)}, u32[]{:S(2)}) collective-permute-start(bf16[2,208,512]{2,1,0:T(8,128)(2,1)S(1)} %pad_maximum_fusion.3), channel_id=1, source_target_pairs={{0,8},{4,12},{8,0},{12,4},{16,24},{20,28},{24,16},{28,20},{1,9},{5... | collective-permute-start | bytes 1277960 | tf_op jit(solution)/shard_map/ppermute | solution.py:27
  169.5 15.0 %collective-permute-start.30 = (bf16[240,512]{1,0:T(8,128)(2,1)S(1)}, bf16[240,512]{1,0:T(8,128)(2,1)S(1)}, u32[]{:S(2)}, u32[]{:S(2)}) collective-permute-start(bf16[240,512]{1,0:T(8,128)(2,1)S(1)} %get-tuple-element.181), channel_id=1, source_target_pairs={{0,4},{4,0},{8,12},{12,8},{16,20},{20,16},{24,28},{28,24},{1,5},{5... | collective-permute-start | bytes 737288 | tf_op jit(solution)/shard_map/ppermute | solution.py:27
  170.4 14.1 %collective-permute-start.31 = (bf16[240,512]{1,0:T(8,128)(2,1)S(1)}, bf16[240,512]{1,0:T(8,128)(2,1)S(1)}, u32[]{:S(2)}, u32[]{:S(2)}) collective-permute-start(bf16[240,512]{1,0:T(8,128)(2,1)S(1)} %get-tuple-element.180), channel_id=1, source_target_pairs={{0,6},{1,7},{2,4},{3,5},{4,2},{5,3},{6,0},{7,1},{8,14},{9,15},{10,... | collective-permute-start | bytes 737288 | tf_op jit(solution)/shard_map/ppermute | solution.py:966
  171.6 12.9 %collective-permute-start.29 = (bf16[288,512]{1,0:T(8,128)(2,1)S(1)}, bf16[288,512]{1,0:T(8,128)(2,1)S(1)}, u32[]{:S(2)}, u32[]{:S(2)}) collective-permute-start(bf16[288,512]{1,0:T(8,128)(2,1)S(1)} %fusion.10), channel_id=1, source_target_pairs={{0,2},{1,3},{2,0},{3,1},{4,6},{5,7},{6,4},{7,5},{8,10},{9,11},{10,... | collective-permute-start | bytes 884744 | tf_op jit(solution)/shard_map/ppermute | solution.py:27
  184.9 9.5 %collective-permute-start.33 = (bf16[240,512]{1,0:T(8,128)(2,1)S(1)}, bf16[240,512]{1,0:T(8,128)(2,1)S(1)}, u32[]{:S(2)}, u32[]{:S(2)}) collective-permute-start(bf16[240,512]{1,0:T(8,128)(2,1)S(1)} %pad_maximum_fusion.11), channel_id=1, source_target_pairs={{0,8},{4,12},{8,0},{12,4},{16,24},{20,28},{24,16},{28,20},{1,9},{5... | collective-permute-start | bytes 737288 | tf_op jit(solution)/shard_map/ppermute | solution.py:27
  185.1 9.3 %collective-permute-start.34 = (bf16[208,512]{1,0:T(8,128)(2,1)S(1)}, bf16[208,512]{1,0:T(8,128)(2,1)S(1)}, u32[]{:S(2)}, u32[]{:S(2)}) collective-permute-start(bf16[208,512]{1,0:T(8,128)(2,1)S(1)} %fusion.9), channel_id=1, source_target_pairs={{0,16},{4,20},{8,24},{12,28},{24,8},{28,12},{1,17},{5,21},{9,25},{... | collective-permute-start | bytes 638984 | tf_op jit(solution)/shard_map/ppermute | solution.py:978
  194.5 5.5 %collective-permute-start.35 = (f32[24,512]{1,0:T(8,128)S(1)}, f32[24,512]{1,0:T(8,128)S(1)}, u32[]{:S(2)}, u32[]{:S(2)}) collective-permute-start(f32[24,512]{1,0:T(8,128)S(1)} %maximum_add_fusion.2), channel_id=1, source_target_pairs={{0,16},{4,20},{8,24},{12,28},{16,0},{20,4},{24,8},{28,12},{1,17},{... | collective-permute-start | bytes 147464 | tf_op jit(solution)/shard_map/ppermute | solution.py:27
  198.0 9.2 %collective-permute-start.36 = (bf16[208,512]{1,0:T(8,128)(2,1)S(1)}, bf16[208,512]{1,0:T(8,128)(2,1)S(1)}, u32[]{:S(2)}, u32[]{:S(2)}) collective-permute-start(bf16[208,512]{1,0:T(8,128)(2,1)S(1)} %fusion.5), channel_id=1, source_target_pairs={{16,0},{20,4},{17,1},{21,5},{18,2},{22,6},{19,3},{23,7}} | collective-permute-start | bytes 638984 | tf_op jit(solution)/shard_map/ppermute | solution.py:1007
  (32 other events, 195.5 us)
